TPU v7x, 512 devices: a whole 4x4x16 slice. The times are simulated.
512 devices in a mesh: dp: 2 (over y_hi), chan: 16 (over z), ctx: 16 (over x, y_lo, core).
Axes of the slice: x: 4, y: 4 (y_hi: 2, y_lo: 2; y = y_hi * 2 + y_lo), z: 16, core: 2. Of those that a mesh axis runs over, the one named last changes fastest.
Arguments:
- values: bfloat16 [2, 8192, 4096], P('dp', 'ctx', 'chan'), may hold values from -6 to 6
- gate_first: bfloat16 [2, 8192, 4096], P('dp', 'ctx', 'chan'), may hold values from -6 to 6
- gate_second: bfloat16 [2, 8192, 4096], P('dp', 'ctx', 'chan'), may hold values from -6 to 6
- filter_features: bfloat16 [64, 8192], P(None, 'ctx'), may hold values from -4 to 4
- filter_weight: bfloat16 [64, 4096], P(None, 'chan'), may hold values from -0.75 to 0.75
- decay_rate: float32 [4096], P('chan'), may hold values from 0.5 to 8
- skip_bias: float32 [4096], P('chan'), may hold values from -4 to 4
- output_grad: bfloat16 [2, 8192, 4096], P('dp', 'ctx', 'chan'), may hold values from -6 to 6
Outputs:
- output: bfloat16 [2, 8192, 4096], P('dp', 'ctx', 'chan')
- values_grad: bfloat16 [2, 8192, 4096], P('dp', 'ctx', 'chan')
- first_grad: bfloat16 [2, 8192, 4096], P('dp', 'ctx', 'chan')
- second_grad: bfloat16 [2, 8192, 4096], P('dp', 'ctx', 'chan')
- weight_grad: float32 [64, 4096], P(None, 'chan')
- feature_grad: float32 [64, 8192], P(None, 'ctx')
All inputs are finite; a program needn't handle non-finite values.
Results may differ from a plain program's by a relative error of at most 0.03.
Values may be sent and summed in bfloat16 or wider, within the bound.
No kernel may reach another device: no remote copies, remote signals or barrier semaphores. Data moves between devices by JAX's collectives and lax.ppermute only.
A program may use at most 64 MiB of HBM per device.

v0:
```python
import math

import jax
import jax.numpy as jnp
from jax import lax
from jax.sharding import PartitionSpec as P

R2 = 256


def phases(left_index, right_index, period):
    product = left_index[:, None] * right_index[None, :] % period
    return 2.0 * math.pi / period * product.astype(jnp.float32)


def padded_rows(ctx_count, block_rows):
    order_rows = jnp.arange(2 * ctx_count * block_rows, dtype=jnp.int32)
    upper = order_rows // block_rows % 2 * (ctx_count * block_rows)
    return upper + order_rows // (2 * block_rows) * block_rows + order_rows % block_rows


def forward_spectra(signal, ctx_count, ctx_index, period):
    item_count, block_rows, columns, channels = signal.shape
    signal = jnp.concatenate([signal, jnp.zeros_like(signal)], axis=1)
    source_rows = padded_rows(ctx_count, block_rows)
    gathered = lax.all_to_all(signal, "ctx", split_axis=2, concat_axis=1, tiled=True)
    radix_one = 2 * ctx_count * block_rows
    group_two = columns // ctx_count
    freq_one = jnp.arange(radix_one, dtype=jnp.int32)
    angles_one = phases(freq_one, source_rows, radix_one)
    matrix_one = jnp.concatenate([jnp.cos(angles_one), -jnp.sin(angles_one)], axis=0).astype(
        jnp.bfloat16
    )
    section_one = jnp.einsum(
        "kn,snjc->skjc", matrix_one, gathered, preferred_element_type=jnp.float32
    )
    real_part = section_one[:, :radix_one]
    imag_part = section_one[:, radix_one:]
    local_columns = ctx_index * group_two + jnp.arange(group_two, dtype=jnp.int32)
    twiddle = phases(freq_one, local_columns, period)[None, :, :, None]
    cosines = jnp.cos(twiddle)
    sines = jnp.sin(twiddle)
    section_out = jnp.stack(
        [real_part * cosines + imag_part * sines, imag_part * cosines - real_part * sines], axis=1
    ).astype(jnp.bfloat16)
    turned = lax.all_to_all(section_out, "ctx", split_axis=2, concat_axis=3, tiled=True)
    freq_two = jnp.arange(columns, dtype=jnp.int32)
    angles_two = phases(freq_two, freq_two, columns)
    basis_two = jnp.stack([jnp.cos(angles_two), jnp.sin(angles_two)]).astype(jnp.bfloat16)
    products_two = jnp.einsum(
        "tmj,srkjc->strkmc", basis_two, turned, preferred_element_type=jnp.float32
    )
    spectra = jnp.stack(
        [
            products_two[:, 0, 0] + products_two[:, 1, 1],
            products_two[:, 0, 1] - products_two[:, 1, 0],
        ],
        axis=1,
    )
    return spectra.astype(jnp.bfloat16)


def inverse_signal(spectrum, ctx_count, ctx_index, period, factor, block_rows):
    item_count, halves, group_one, columns, channels = spectrum.shape
    radix_one = group_one * ctx_count
    group_two = columns // ctx_count
    freq_two = jnp.arange(columns, dtype=jnp.int32)
    angles_two = phases(freq_two, freq_two, columns)
    basis_two = jnp.stack([jnp.cos(angles_two), jnp.sin(angles_two)]).astype(jnp.bfloat16)
    products_two = jnp.einsum(
        "tmj,srkjc->strkmc", basis_two, spectrum, preferred_element_type=jnp.float32
    )
    back_real = products_two[:, 0, 0] - products_two[:, 1, 1]
    back_imag = products_two[:, 0, 1] + products_two[:, 1, 0]
    local_freq = ctx_index * group_one + jnp.arange(group_one, dtype=jnp.int32)
    twiddle = phases(local_freq, freq_two, period)[None, :, :, None]
    cosines = jnp.cos(twiddle)
    sines = jnp.sin(twiddle)
    section_out = jnp.stack(
        [back_real * cosines - back_imag * sines, back_imag * cosines + back_real * sines], axis=1
    ).astype(jnp.bfloat16)
    turned = lax.all_to_all(section_out, "ctx", split_axis=3, concat_axis=2, tiled=True)
    target_rows = padded_rows(ctx_count, block_rows)
    angles_one = phases(target_rows, jnp.arange(radix_one, dtype=jnp.int32), radix_one)
    matrix_one = jnp.concatenate([jnp.cos(angles_one), -jnp.sin(angles_one)], axis=1).astype(
        jnp.bfloat16
    )
    flattened = turned.reshape(item_count, 2 * radix_one, group_two, channels)
    signal = (
        jnp.einsum("nk,skjc->snjc", matrix_one, flattened, preferred_element_type=jnp.float32)
        * factor
    )
    returned = lax.all_to_all(
        signal.astype(jnp.bfloat16), "ctx", split_axis=1, concat_axis=2, tiled=True
    )
    return returned[:, :block_rows]


def complex_product(left_spec, right_spec, conjugate):
    left_real = left_spec[:, 0].astype(jnp.float32)
    left_imag = left_spec[:, 1].astype(jnp.float32)
    right_real = right_spec[:, 0].astype(jnp.float32)
    right_imag = right_spec[:, 1].astype(jnp.float32)
    if conjugate:
        real_out = left_real * right_real + left_imag * right_imag
        imag_out = left_imag * right_real - left_real * right_imag
    else:
        real_out = left_real * right_real - left_imag * right_imag
        imag_out = left_real * right_imag + left_imag * right_real
    return jnp.stack([real_out, imag_out], axis=1).astype(jnp.bfloat16)


def local(
    values,
    gate_first,
    gate_second,
    filter_features,
    filter_weight,
    decay_rate,
    skip_bias,
    output_grad,
):
    batch_size, tokens, channels = values.shape
    ctx_count = lax.axis_size("ctx")
    ctx_index = lax.axis_index("ctx")
    length = tokens * ctx_count
    period = 2 * length
    block_rows = tokens // R2
    positions = (ctx_index * tokens + jnp.arange(tokens, dtype=jnp.int32)).astype(
        jnp.float32
    ) / length
    window = jnp.exp(-decay_rate[None, :] * positions[:, None])
    raw_kernel = jnp.dot(filter_features.T, filter_weight, preferred_element_type=jnp.float32)
    kernel = (raw_kernel * window).astype(jnp.bfloat16)
    mixed_in = (values.astype(jnp.float32) * gate_first.astype(jnp.float32)).astype(jnp.bfloat16)
    scaled_grad = (output_grad.astype(jnp.float32) * gate_second.astype(jnp.float32)).astype(
        jnp.bfloat16
    )
    signal = jnp.concatenate([mixed_in, kernel[None], scaled_grad], axis=0)
    signal = signal.reshape(2 * batch_size + 1, block_rows, R2, channels)
    spectra = forward_spectra(signal, ctx_count, ctx_index, period)
    mixed_spec = spectra[:batch_size]
    kernel_spec = spectra[batch_size : batch_size + 1]
    grad_spec = spectra[batch_size + 1 :]
    products = jnp.concatenate(
        [
            complex_product(mixed_spec, kernel_spec, False),
            complex_product(grad_spec, kernel_spec, True),
            complex_product(grad_spec, mixed_spec, True),
        ],
        axis=0,
    )
    factor = 1.0 / (period * math.sqrt(length))
    signals = inverse_signal(products, ctx_count, ctx_index, period, factor, block_rows)
    signals = signals.reshape(3 * batch_size, tokens, channels)
    conv = signals[:batch_size].astype(jnp.float32)
    grad_conv = signals[batch_size : 2 * batch_size].astype(jnp.float32)
    filter_conv = signals[2 * batch_size :].astype(jnp.float32)
    total = conv + skip_bias * mixed_in.astype(jnp.float32)
    output = (gate_second.astype(jnp.float32) * total).astype(jnp.bfloat16)
    second_grad = (output_grad.astype(jnp.float32) * total).astype(jnp.bfloat16)
    delta = grad_conv + skip_bias * scaled_grad.astype(jnp.float32)
    values_grad = (delta * gate_first.astype(jnp.float32)).astype(jnp.bfloat16)
    first_grad = (delta * values.astype(jnp.float32)).astype(jnp.bfloat16)
    kernel_grad = (filter_conv * window).astype(jnp.bfloat16)
    weight_part = jnp.einsum(
        "ot,btc->oc", filter_features, kernel_grad, preferred_element_type=jnp.float32
    )
    feature_part = jnp.einsum(
        "oc,btc->ot", filter_weight, kernel_grad, preferred_element_type=jnp.float32
    )
    weight_grad = lax.psum(weight_part.astype(jnp.bfloat16), ("dp", "ctx")).astype(jnp.float32)
    feature_grad = lax.psum(feature_part.astype(jnp.bfloat16), ("dp", "chan")).astype(jnp.float32)
    return (output, values_grad, first_grad, second_grad, weight_grad, feature_grad)


def solution(mesh):
    in_specs = (
        P("dp", "ctx", "chan"),
        P("dp", "ctx", "chan"),
        P("dp", "ctx", "chan"),
        P(None, "ctx"),
        P(None, "chan"),
        P("chan"),
        P("chan"),
        P("dp", "ctx", "chan"),
    )
    out_specs = (
        P("dp", "ctx", "chan"),
        P("dp", "ctx", "chan"),
        P("dp", "ctx", "chan"),
        P("dp", "ctx", "chan"),
        P(None, "chan"),
        P(None, "ctx"),
    )
    return jax.shard_map(local, mesh=mesh, in_specs=in_specs, out_specs=out_specs, check_vma=False)
```

profile of v0, /device:TPU:6, one launch (start us, length us, event | category | flops | bytes accessed | tf_op | source)
XLA Modules:
  0.0 466.2 jit_solution(14884198198056976095)
XLA Ops:
  7.2 0.7 neg.10
  7.9 0.6 copy-done.12
  8.5 1.0 fusion.19
  9.5 1.3 fusion.37
  10.8 0.7 copy-done.1
  11.6 0.8 copy.105
  12.4 1.8 concatenate.55.clone
  14.2 9.4 %all-to-all-start = ((bf16[3,4,256,256]{3,1,0,2:T(4,128)(2,1)}), bf16[3,4,256,256]{3,1,0,2:T(4,128)(2,1)S(1)}, u32[]{:S(2)}, u32[]{:S(2)}) async-start(bf16[3,4,256,256]{3,1,0,2:T(4,128)(2,1)} %concatenate.55.clone), calls=%async_computation | async-start | bytes 3145728 | tf_op jit(solution)/shard_map/all_to_all | solution.py:26
  23.8 0.3 cosine_convert_fusion.1
  24.1 19.4 %all-to-all-done = bf16[3,4,256,256]{3,1,0,2:T(4,128)(2,1)S(1)} async-done(((bf16[3,4,256,256]{3,1,0,2:T(4,128)(2,1)}), bf16[3,4,256,256]{3,1,0,2:T(4,128)(2,1)S(1)}, u32[]{:S(2)}, u32[]{:S(2)}) %all-to-all-start) | async-done | bytes 1572896 | tf_op jit(solution)/shard_map/all_to_all | solution.py:26
  43.5 0.8 copy.107
  44.4 0.4 all_to_all.53
  44.8 1.1 convolution_bitcast_fusion.2
  45.9 0.9 fusion.16
  46.8 0.3 pad_maximum_fusion
  47.1 3.4 copy.71
  50.5 6.2 %all-to-all-start.1 = ((bf16[3,2,64,16,256]{4,3,0,1,2:T(8,128)(2,1)}), bf16[3,2,64,16,256]{4,3,0,1,2:T(8,128)(2,1)S(1)}, u32[]{:S(2)}, u32[]{:S(2)}) async-start(bf16[3,2,64,16,256]{4,3,0,1,2:T(8,128)(2,1)} %copy.71), calls=%async_computation.1 | async-start | bytes 6291456 | tf_op jit(solution)/shard_map/all_to_all | solution.py:46
  56.7 0.2 all-reduce.3.cloned.1.call-start
  57.0 1.7 sine_convert_fusion
  58.8 38.8 %all-to-all-done.1 = bf16[3,2,64,16,256]{4,3,0,1,2:T(8,128)(2,1)S(1)} async-done(((bf16[3,2,64,16,256]{4,3,0,1,2:T(8,128)(2,1)}), bf16[3,2,64,16,256]{4,3,0,1,2:T(8,128)(2,1)S(1)}, u32[]{:S(2)}, u32[]{:S(2)}) %all-to-all-start.1) | async-done | bytes 3145760 | tf_op jit(solution)/shard_map/all_to_all | solution.py:46
  97.6 0.3 copy.73
  98.0 0.6 copy-done.7
  98.6 1.9 convolution_bitcast_fusion.1
  100.4 0.6 fusion.102
  101.1 0.4 fusion.5
  101.5 0.6 fusion.3
  102.1 0.3 fusion.46
  102.4 0.7 fusion.41
  103.2 0.3 fusion.42
  103.5 1.8 convolution_bitcast_fusion
  105.3 1.3 subtract_convert_fusion
  106.6 0.3 pad_maximum_fusion.1
  106.9 4.5 copy.86
  111.5 43.5 %all_to_all.69 = bf16[3,2,4,256,256]{4,2,0,1,3:T(4,128)(2,1)S(1)} all-to-all(bf16[3,2,4,256,256]{4,2,0,1,3:T(4,128)(2,1)} %copy.86), channel_id=1, replica_groups=mesh['dp'=2,'chan'=16,'ctx'=16] {'ctx'}, dimensions={3} | all-to-all | bytes 6291456 | tf_op jit(solution)/shard_map/all_to_all | solution.py:82
  154.9 0.8 copy.87
  155.7 4.1 copy.88
  159.8 3.8 reshape.620
  163.5 0.7 fusion.18
  164.3 0.9 copy.90
  165.1 24.7 %all_to_all.70 = bf16[3,64,16,256]{3,2,0,1:T(8,128)(2,1)S(1)} all-to-all(bf16[3,64,16,256]{3,2,0,1:T(8,128)(2,1)S(1)} %copy.90), channel_id=1, replica_groups=mesh['dp'=2,'chan'=16,'ctx'=16] {'ctx'}, dimensions={1} | all-to-all | bytes 3145728 | tf_op jit(solution)/shard_map/all_to_all | solution.py:93
  190.1 0.4 copy-done.11
  190.7 0.8 fusion.20
  191.6 1.2 fusion.40
  192.9 0.2 fusion.21
  193.0 99.9 %psum.14 = bf16[64,256]{1,0:T(8,128)(2,1)S(1)} all-reduce(bf16[64,256]{1,0:T(8,128)(2,1)S(1)} %fusion.21), channel_id=1, replica_groups=mesh['dp'=2,'chan'=16,'ctx'=16] {'dp','ctx'}, use_global_device_ids=true, to_apply=%region_0.1 | all-reduce | flops 16384 | bytes 65536 | tf_op jit(solution)/shard_map/psum | solution.py:172
  292.9 0.6 convert_element_type.314
  293.6 164.3 %all-reduce.3.cloned.1.call-done = bf16[64,512]{1,0:T(8,128)(2,1)} async-done(((bf16[64,512]{1,0:T(8,128)(2,1)}), bf16[64,512]{1,0:T(8,128)(2,1)}) %all-reduce.3.cloned.1.call-update) | async-done | bytes 65552 | tf_op jit(solution)/shard_map/psum | solution.py:173
  457.8 1.5 convert_element_type.317
  (37 shorter events, 0.9 us)
Async XLA Ops:
  7.2 1.3 copy-start
  7.2 0.7 copy-start.10
  7.9 0.6 copy-start.12
  10.8 0.7 copy-start.1
  14.2 29.3 %all-to-all-start = ((bf16[3,4,256,256]{3,1,0,2:T(4,128)(2,1)}), bf16[3,4,256,256]{3,1,0,2:T(4,128)(2,1)S(1)}, u32[]{:S(2)}, u32[]{:S(2)}) async-start(bf16[3,4,256,256]{3,1,0,2:T(4,128)(2,1)} %concatenate.55.clone), calls=%async_computation | async-start | bytes 3145728 | tf_op jit(solution)/shard_map/all_to_all | solution.py:26
  50.5 47.1 %all-to-all-start.1 = ((bf16[3,2,64,16,256]{4,3,0,1,2:T(8,128)(2,1)}), bf16[3,2,64,16,256]{4,3,0,1,2:T(8,128)(2,1)S(1)}, u32[]{:S(2)}, u32[]{:S(2)}) async-start(bf16[3,2,64,16,256]{4,3,0,1,2:T(8,128)(2,1)} %copy.71), calls=%async_computation.1 | async-start | bytes 6291456 | tf_op jit(solution)/shard_map/all_to_all | solution.py:46
  56.7 401.1 %all-reduce.3.cloned.1.call-start = ((), (), s32[]{:S(2)}) async-start(), calls=%async_computation.4 | async-start | bytes 131072 | tf_op jit(solution)/shard_map/psum | solution.py:173
  97.6 0.9 copy-start.7
  97.6 1.0 copy-start.8
  189.8 0.7 copy-start.11
  189.8 0.7 copy-start.13
  189.8 0.9 copy-start.9
  189.8 1.7 copy-start.2
  189.9 1.7 copy-start.3
  189.9 1.7 copy-start.4
  189.9 1.7 copy-start.5
  189.9 1.7 copy-start.6
  189.9 1.7 copy-start.14
Sparse Core Ops, SparseCore 0:
  191.7 266.0 all-reduce.2
where the time goes:
time: 467 us; the launch traced here: 466 us
  waiting for transfers between devices  222 us (48%)
  blocking collectives  168 us (36%)
  local copies, waits for them, and re-layouts  24.1 us (5%)
  starting transfers between devices  15.8 us (3%)
  between operations  14.4 us (3%)
  other arithmetic  13.8 us (3%)
  matrix products  7.51 us (2%)
    psum x1, waiting for transfers between devices, local(): lax.psum(feature_part.astype(jnp.bfloat16), ('dp', 'chan'))  164 us
    psum x1, blocking collectives, local(): lax.psum(weight_part.astype(jnp.bfloat16), ('dp', 'ctx'))  99.9 us
    all_to_all x1, blocking collectives, inverse_signal(): lax.all_to_all(section_out, 'ctx', split_axis=3, concat_axis=2, tiled=True)  43.5 us
    all_to_all x1, waiting for transfers between devices, forward_spectra(): lax.all_to_all(section_out, 'ctx', split_axis=2, concat_axis=3, tiled=True)  38.8 us
    all_to_all x1, blocking collectives, inverse_signal(): lax.all_to_all(signal.astype(jnp.bfloat16), 'ctx', split_axis=1, concat_a...  24.7 us
    all_to_all x1, waiting for transfers between devices, forward_spectra(): lax.all_to_all(signal, 'ctx', split_axis=2, concat_axis=1, tiled=True)  19.4 us
    all_to_all x1, starting transfers between devices, forward_spectra(): lax.all_to_all(signal, 'ctx', split_axis=2, concat_axis=1, tiled=True)  9.42 us
  transfers between devices with their start and end apart: 3, of which 3 were waited for; matrix products, arithmetic and copies ran while one was open for 1% of the time, Pallas kernels for 0%

commit v1 on v0

v1 whole, which is shorter than its diff:
```python
import functools
import math

import jax
import jax.numpy as jnp
import numpy as np
from jax import lax
from jax.experimental import pallas as pl
from jax.experimental.pallas import tpu as pltpu
from jax.sharding import PartitionSpec as P

LENGTH = 8192
PERIOD = 2 * LENGTH
TOK = 512
RADIX = PERIOD // TOK
BLOCKS = RADIX // 2
HALF = RADIX // 2 + 1
CH = 256
OWN = 8
GROUP = 32
ORDER = 64
PAIRS = (HALF + 1) // 2
ROWS = 2 * HALF + PAIRS
VMEM_LIMIT = 56 * 1024 * 1024


def tables():
    grid = np.arange(TOK)
    angle = 2.0 * np.pi / TOK * (np.outer(grid, grid) % TOK)
    basis = np.concatenate([np.cos(angle), np.sin(angle)], axis=0).astype(jnp.bfloat16)
    turn = 2.0 * np.pi / PERIOD * np.outer(np.arange(HALF), grid)
    forward = np.stack([np.cos(turn), np.sin(turn)]).astype(np.float32)
    factor = 1.0 / (PERIOD * math.sqrt(LENGTH))
    inverse = (np.stack([np.cos(turn), np.sin(turn)]) * factor).astype(np.float32)
    return basis, forward, inverse


def add(a, b):
    if a is None:
        return b
    return a if b is None else a + b


def sub(a, b):
    if b is None:
        return a
    return -b if a is None else a - b


def neg(a):
    return None if a is None else -a


def rotate(value, index, period):
    real, imag = value
    if index == 0:
        return value
    if 4 * index == period:
        return imag, neg(real)
    c = math.cos(2 * math.pi * index / period)
    s = math.sin(2 * math.pi * index / period)
    if imag is None:
        return real * c, real * (-s)
    if 8 * index == period:
        return (real + imag) * c, (imag - real) * c
    return real * c + imag * s, imag * c - real * s


def rotate_back(value, index, period):
    real, imag = value
    if index == 0:
        return value
    if 4 * index == period:
        return neg(imag), real
    c = math.cos(2 * math.pi * index / period)
    s = math.sin(2 * math.pi * index / period)
    if 8 * index == period:
        return (real - imag) * c, (imag + real) * c
    return real * c - imag * s, imag * c + real * s


def real_dft(xs, n):
    if n == 2:
        return [(xs[0], None), (xs[0], None)]
    if n == 4:
        return [(xs[0] + xs[1], None), (xs[0], -xs[1]), (xs[0] - xs[1], None)]
    even = real_dft(xs[0::2], n // 2)
    odd = real_dft(xs[1::2], n // 2)
    out = [None] * (n // 2 + 1)
    for k in range(n // 4 + 1):
        t = rotate(odd[k], k, n)
        e = even[k]
        out[k] = (add(e[0], t[0]), add(e[1], t[1]))
        if 4 * k != n:
            out[n // 2 - k] = (sub(e[0], t[0]), sub(t[1], e[1]))
    return out


def real_inverse(spec, n):
    if n == 4:
        total = spec[0][0] + spec[2][0]
        diff = spec[0][0] - spec[2][0]
        return [total + 2.0 * spec[1][0], diff - 2.0 * spec[1][1]]
    even, odd = [], []
    for k in range(n // 4 + 1):
        a, b = spec[k], spec[n // 2 - k]
        if 4 * k == n:
            even.append((2.0 * a[0], None))
            odd.append((-2.0 * a[1], None))
            continue
        even.append((add(a[0], b[0]), sub(a[1], b[1])))
        odd.append(rotate_back((sub(a[0], b[0]), add(a[1], b[1])), k, n))
    first = real_inverse(even, n // 2)
    second = real_inverse(odd, n // 2)
    return [first[i // 2] if i % 2 == 0 else second[i // 2] for i in range(n // 2)]


def spread_kernel(place, values, gate_first, gate_second, grad, features, weight, decay, out):
    f32 = jnp.float32
    mixed = (values[...].astype(f32) * gate_first[...].astype(f32)).T
    scaled = (grad[...].astype(f32) * gate_second[...].astype(f32)).T
    both = jnp.concatenate(
        [mixed.reshape(GROUP, OWN, TOK), scaled.reshape(GROUP, OWN, TOK)], axis=1
    )
    out[:, :, :TOK] = both.astype(jnp.bfloat16)
    dp = place[0]
    ctx = place[1]
    half = TOK // 2
    mine = jnp.where(dp == 0, features[:, :half].astype(f32), features[:, half:].astype(f32))
    raw = lax.dot_general(
        weight[...],
        mine.astype(jnp.bfloat16),
        (((0,), (0,)), ((), ())),
        preferred_element_type=f32,
    )
    first = ctx * TOK + dp * half
    positions = (first + lax.broadcasted_iota(jnp.int32, (1, half), 1)).astype(f32) / LENGTH
    kernel = (raw * jnp.exp(-decay[...] * positions)).reshape(GROUP, OWN, half)
    folded = jnp.concatenate([kernel[:, :, : half // 2], kernel[:, :, half // 2 :]], axis=1)
    out[:, :, TOK:] = folded.astype(jnp.bfloat16)


def spread(place, values, gate_first, gate_second, grad, features, weight, decay, **kw):
    return pl.pallas_call(
        spread_kernel,
        out_shape=jax.ShapeDtypeStruct((GROUP, 2 * OWN, TOK + 128), jnp.bfloat16),
        in_specs=[pl.BlockSpec(memory_space=pltpu.SMEM)] + [pl.BlockSpec(memory_space=pltpu.VMEM)] * 7,
        out_specs=pl.BlockSpec(memory_space=pltpu.VMEM),
        compiler_params=pltpu.CompilerParams(vmem_limit_bytes=VMEM_LIMIT),
        name="spread",
        **kw,
    )(place, values, gate_first, gate_second, grad, features, weight, decay)


def spectral_kernel(
    got, basis, forward, inverse, features, decay, out, lhs_re, lhs_im, res_re, res_im, filt_re, filt_im, kernel_grad
):
    f32, bf16 = jnp.float32, jnp.bfloat16

    def lanes_of(chunk):
        return pl.ds(pl.multiple_of(chunk * 128, 128), 128)

    def transformed(xs, lanes):
        spec = real_dft(xs, RADIX)
        turned = []
        for k, (real, imag) in enumerate(spec):
            if k == 0:
                turned.append((real, jnp.zeros_like(real)))
                continue
            c = forward[0, k : k + 1, lanes]
            s = forward[1, k : k + 1, lanes]
            if imag is None:
                turned.append((real * c, -(real * s)))
            else:
                turned.append((real * c + imag * s, imag * c - real * s))
        return turned

    def signals_in(step, carry):
        s = step // 4
        lanes = lanes_of(step % 4)
        xs = [got[s * BLOCKS + j, :, lanes].astype(f32) for j in range(BLOCKS)]
        low = transformed([x[:OWN] for x in xs], lanes)
        high = transformed([x[OWN:] for x in xs], lanes)
        for k in range(HALF):
            lhs_re[2 * k + s, :, lanes] = jnp.concatenate([low[k][0], high[k][0]], axis=0).astype(bf16)
            lhs_im[2 * k + s, :, lanes] = jnp.concatenate([low[k][1], high[k][1]], axis=0).astype(bf16)
        return carry

    lax.fori_loop(0, 8, signals_in, 0)

    def kernel_in(s, carry):
        xs = [got[s * BLOCKS + j, :, TOK:].astype(f32) for j in range(BLOCKS)]
        for q in range(2):
            lanes = lanes_of(2 * s + q)
            spec = transformed([x[q * OWN : (q + 1) * OWN] for x in xs], lanes)
            spec.append((jnp.zeros_like(spec[0][0]),) * 2)
            for p in range(PAIRS):
                a, b = spec[2 * p], spec[2 * p + 1]
                lhs_re[2 * HALF + p, :, lanes] = jnp.concatenate([a[0], b[0]], axis=0).astype(bf16)
                lhs_im[2 * HALF + p, :, lanes] = jnp.concatenate([a[1], b[1]], axis=0).astype(bf16)
        return carry

    lax.fori_loop(0, 2, kernel_in, 0)

    def product(first, second):
        lhs = jnp.concatenate([first, second], axis=1)
        res = jnp.dot(lhs, basis[...], preferred_element_type=f32)
        return res.reshape(ROWS, 2 * OWN, TOK)

    real = lhs_re[...].reshape(ROWS * 2 * OWN, TOK)
    imag = lhs_im[...].reshape(ROWS * 2 * OWN, TOK)
    res_re[...] = product(real, imag)
    res_im[...] = product(imag, -real)

    filt_re[...] = jnp.zeros_like(filt_re)
    filt_im[...] = jnp.zeros_like(filt_im)

    def multiply(k, carry):
        pair = k // 2
        rows = pl.ds(pl.multiple_of(k % 2 * OWN, OWN), OWN)
        hr = res_re[2 * HALF + pair, rows, :]
        hi = res_im[2 * HALF + pair, rows, :]
        total_re, total_im = None, None
        for s in range(2):
            zr = res_re[2 * k + s, :OWN, :]
            zi = res_im[2 * k + s, :OWN, :]
            gr = res_re[2 * k + s, OWN:, :]
            gi = res_im[2 * k + s, OWN:, :]
            lhs_re[2 * k + s] = jnp.concatenate(
                [zr * hr - zi * hi, gr * hr + gi * hi], axis=0
            ).astype(bf16)
            lhs_im[2 * k + s] = jnp.concatenate(
                [zr * hi + zi * hr, gi * hr - gr * hi], axis=0
            ).astype(bf16)
            total_re = add(total_re, gr * zr + gi * zi)
            total_im = add(total_im, gi * zr - gr * zi)
        filt_re[pair, rows, :] = total_re
        filt_im[pair, rows, :] = total_im
        return carry

    lax.fori_loop(0, HALF, multiply, 0)
    lhs_re[2 * HALF :] = filt_re[...].astype(bf16)
    lhs_im[2 * HALF :] = filt_im[...].astype(bf16)

    real = lhs_re[...].reshape(ROWS * 2 * OWN, TOK)
    imag = lhs_im[...].reshape(ROWS * 2 * OWN, TOK)
    res_re[...] = product(real, -imag)
    res_im[...] = product(imag, real)

    def returned(spec, lanes):
        turned = []
        for k, (real, imag) in enumerate(spec):
            c = inverse[0, k : k + 1, lanes]
            s = inverse[1, k : k + 1, lanes]
            if k in (0, HALF - 1):
                turned.append((real * c - imag * s, None))
            else:
                turned.append((real * c - imag * s, imag * c + real * s))
        return real_inverse(turned, RADIX)

    def filter_out(chunk, carry):
        rate = decay[...]
        parts = []
        for q in range(2):
            lanes = lanes_of(chunk + 2 * q)
            spec = []
            for k in range(HALF):
                rows = slice(k % 2 * OWN, k % 2 * OWN + OWN)
                block = 2 * HALF + k // 2
                spec.append((res_re[block, rows, lanes], res_im[block, rows, lanes]))
            parts.append(returned(spec, lanes))
        ahead = lax.broadcasted_iota(jnp.int32, (OWN, 128), 1) + chunk * 128
        for j in range(BLOCKS):
            pieces = []
            for q in range(2):
                positions = (ahead + (TOK * j + 256 * q)).astype(f32) / LENGTH
                pieces.append(parts[q][j] * jnp.exp(-rate * positions))
            both = jnp.concatenate(pieces, axis=0).astype(bf16)
            kernel_grad[:, lanes_of(2 * j + chunk)] = both
            out[j, :, lanes_of(4 + chunk)] = both
            out[BLOCKS + j, :, lanes_of(4 + chunk)] = both
        return carry

    lax.fori_loop(0, 2, filter_out, 0)

    def signals_out(step, carry):
        s = step // 4
        lanes = lanes_of(step % 4)
        halves = []
        for rows in (slice(0, OWN), slice(OWN, 2 * OWN)):
            spec = [(res_re[2 * k + s, rows, lanes], res_im[2 * k + s, rows, lanes]) for k in range(HALF)]
            halves.append(returned(spec, lanes))
        for j in range(BLOCKS):
            out[s * BLOCKS + j, :, lanes] = jnp.concatenate([halves[0][j], halves[1][j]], axis=0).astype(bf16)
        return carry

    lax.fori_loop(0, 8, signals_out, 0)

    sums = []
    for q in range(2):
        along = jnp.concatenate(
            [features[j, :, 256 * q : 256 * (q + 1)] for j in range(BLOCKS)], axis=1
        )
        sums.append(
            lax.dot_general(
                kernel_grad[...], along, (((1,), (1,)), ((), ())), preferred_element_type=f32
            )
        )
    own_weight = sums[0][:OWN] + sums[1][OWN:]
    padded = jnp.concatenate([own_weight, jnp.zeros((OWN, 128 - ORDER), f32)], axis=1)
    padded = jnp.concatenate([padded, jnp.zeros((OWN, 128), f32)], axis=0).astype(bf16)
    out[:, :, TOK + 256 :] = jnp.broadcast_to(padded[None], (GROUP, 2 * OWN, 128))


def spectral(got, features, decay, **kw):
    basis, forward, inverse = tables()
    wide = pltpu.VMEM((ROWS, 2 * OWN, TOK), jnp.bfloat16)
    result = pltpu.VMEM((ROWS, 2 * OWN, TOK), jnp.float32)
    filt = pltpu.VMEM((PAIRS, 2 * OWN, TOK), jnp.float32)
    return pl.pallas_call(
        spectral_kernel,
        out_shape=jax.ShapeDtypeStruct((GROUP, 2 * OWN, TOK + 256 + 128), jnp.bfloat16),
        in_specs=[pl.BlockSpec(memory_space=pltpu.VMEM)] * 6,
        out_specs=pl.BlockSpec(memory_space=pltpu.VMEM),
        scratch_shapes=[
            wide, wide, result, result, filt, filt,
            pltpu.VMEM((2 * OWN, BLOCKS * 256), jnp.bfloat16),
        ],
        compiler_params=pltpu.CompilerParams(vmem_limit_bytes=VMEM_LIMIT),
        name="spectral",
        **kw,
    )(got, jnp.asarray(basis), jnp.asarray(forward), jnp.asarray(inverse), features, decay)


def feature_kernel(back, weight, part, weight_grad):
    f32, bf16 = jnp.float32, jnp.bfloat16
    for q in range(2):
        kernel_grad = back[:, :, TOK : TOK + 256].astype(f32)[:, q * OWN : (q + 1) * OWN]
        kernel_grad = kernel_grad.reshape(CH, 256).astype(bf16)
        part[:, 256 * q : 256 * (q + 1)] = jnp.dot(
            weight[...], kernel_grad, preferred_element_type=f32
        ).astype(bf16)
    own = back[:, :, TOK + 256 :].astype(f32)[:, :OWN].reshape(CH, 128)
    weight_grad[...] = own.T[:ORDER]


def feature_part(back, weight, **kw):
    return pl.pallas_call(
        feature_kernel,
        out_shape=(
            jax.ShapeDtypeStruct((ORDER, TOK), jnp.bfloat16),
            jax.ShapeDtypeStruct((ORDER, CH), jnp.float32),
        ),
        in_specs=[pl.BlockSpec(memory_space=pltpu.VMEM)] * 2,
        out_specs=(pl.BlockSpec(memory_space=pltpu.VMEM),) * 2,
        compiler_params=pltpu.CompilerParams(vmem_limit_bytes=VMEM_LIMIT),
        name="feature_part",
        **kw,
    )(back, weight)


def final_kernel(
    back, values, gate_first, gate_second, grad, skip, output, values_grad, first_grad, second_grad
):
    f32, bf16 = jnp.float32, jnp.bfloat16
    both = back[:, :, :TOK].astype(f32)
    conv = both[:, :OWN].reshape(CH, TOK).T
    grad_conv = both[:, OWN:].reshape(CH, TOK).T
    x = values[...].astype(f32)
    g1 = gate_first[...].astype(f32)
    g2 = gate_second[...].astype(f32)
    dy = grad[...].astype(f32)
    bias = skip[...]
    total = conv + bias * (x * g1).astype(bf16).astype(f32)
    output[...] = (g2 * total).astype(bf16)
    second_grad[...] = (dy * total).astype(bf16)
    delta = grad_conv + bias * (dy * g2).astype(bf16).astype(f32)
    values_grad[...] = (delta * g1).astype(bf16)
    first_grad[...] = (delta * x).astype(bf16)


def final(back, values, gate_first, gate_second, grad, skip, **kw):
    shape = jax.ShapeDtypeStruct((TOK, CH), jnp.bfloat16)
    return pl.pallas_call(
        final_kernel,
        out_shape=(shape,) * 4,
        in_specs=[pl.BlockSpec(memory_space=pltpu.VMEM)] * 6,
        out_specs=(pl.BlockSpec(memory_space=pltpu.VMEM),) * 4,
        compiler_params=pltpu.CompilerParams(vmem_limit_bytes=VMEM_LIMIT),
        name="final",
        **kw,
    )(back, values, gate_first, gate_second, grad, skip)


def local(
    values,
    gate_first,
    gate_second,
    filter_features,
    filter_weight,
    decay_rate,
    skip_bias,
    output_grad,
):
    values, gate_first, gate_second, output_grad = (
        a[0] for a in (values, gate_first, gate_second, output_grad)
    )
    dp = lax.axis_index("dp")
    ctx = lax.axis_index("ctx")
    group = ("dp", "ctx")
    place = jnp.stack([dp, ctx]).astype(jnp.int32)
    all_features = lax.all_gather(filter_features, "ctx")
    sent = spread(
        place, values, gate_first, gate_second, output_grad, filter_features, filter_weight, decay_rate[:, None]
    )
    got = lax.all_to_all(sent, group, 0, 0, tiled=True)
    own_decay = lax.dynamic_slice(decay_rate, ((dp * BLOCKS + ctx) * OWN,), (OWN,))
    own_decay = jnp.broadcast_to(own_decay[:, None], (OWN, 128))
    back = lax.all_to_all(spectral(got, all_features, own_decay), group, 0, 0, tiled=True)
    part, weight_grad = feature_part(back, filter_weight)
    pieces = part.reshape(16, 4, TOK)
    pieces = lax.all_to_all(pieces, "chan", 0, 0, tiled=True)
    summed = jnp.sum(pieces.astype(jnp.float32), axis=0).astype(jnp.bfloat16)
    copies = jnp.broadcast_to(summed[None], (16, 4, TOK))
    copies = lax.all_to_all(copies, "chan", 0, 0, tiled=True)
    feature_grad = copies.reshape(ORDER, TOK).astype(jnp.float32)
    outs = final(back, values, gate_first, gate_second, output_grad, skip_bias[None, :])
    output, values_grad, first_grad, second_grad = (a[None] for a in outs)
    return (output, values_grad, first_grad, second_grad, weight_grad, feature_grad)


def solution(mesh):
    in_specs = (
        P("dp", "ctx", "chan"),
        P("dp", "ctx", "chan"),
        P("dp", "ctx", "chan"),
        P(None, "ctx"),
        P(None, "chan"),
        P("chan"),
        P("chan"),
        P("dp", "ctx", "chan"),
    )
    out_specs = (
        P("dp", "ctx", "chan"),
        P("dp", "ctx", "chan"),
        P("dp", "ctx", "chan"),
        P("dp", "ctx", "chan"),
        P(None, "chan"),
        P(None, "ctx"),
    )
    return jax.shard_map(local, mesh=mesh, in_specs=in_specs, out_specs=out_specs, check_vma=False)
```

time: 467 us -> 140 us (0.30)
  waiting for transfers between devices: 222 us -> 42.3 us
  blocking collectives: 168 us -> 46.7 us
  local copies, waits for them, and re-layouts: 24.1 us -> 4.39 us
  Pallas kernels: 0 us -> 16.5 us
  other arithmetic: 13.8 us -> 0.63 us
  matrix products: 7.51 us -> 0 us
    psum x1 -> x0, waiting for transfers between devices: 164 us -> none  [local(): lax.psum(feature_part.astype(jnp.bfloat16), ('dp', 'chan'))]
    psum x1 -> x0, blocking collectives: 99.9 us -> none  [local(): lax.psum(weight_part.astype(jnp.bfloat16), ('dp', 'ctx'))]
    all_to_all x2, waiting for transfers between devices: 58.2 us -> 21.2 us  [the longest x1 11.2 us: local(): got = lax.all_to_all(sent, group, 0, 0, tiled=True)]
    all_to_all x2, blocking collectives: 68.2 us -> 46.7 us  [the longest x1 25.3 us: local(): pieces = lax.all_to_all(pieces, 'chan', 0, 0, tiled=True)]
    all_gather x0 -> x1, waiting for transfers between devices: none -> 20.5 us  [local(): all_features = lax.all_gather(filter_features, 'ctx')]
    pallas_call x0 -> x4, Pallas kernels: none -> 16.5 us  [the longest x1 9.32 us: spectral(): pl.pallas_call(spectral_kernel, out_shape=jax.ShapeDtypeStruct((GROUP, 2...]
    another operation x2 -> x0, local copies, waits for them, and re-layouts: 7.92 us -> none  [the longest x1 4.52 us: inverse_signal(): jnp.stack([back_real * cosines - back_imag * sines, back_imag * cosines +...]
    dot_general x7 -> x0, matrix products: 7.51 us -> none  [the longest x1 1.85 us: forward_spectra(): jnp.einsum('tmj,srkjc->strkmc', basis_two, turned, preferred_element_type...]
  transfers between devices with their start and end apart: 3 -> 3, of which waited for: 3 -> 3; matrix products, arithmetic and copies ran while one was open for 1% -> 1% of each run, Pallas kernels for 0% -> 4%
where the time goes in v1:
time: 140 us; the launch traced here: 138 us
  blocking collectives  46.7 us (33%)
  waiting for transfers between devices  42.3 us (30%)
  Pallas kernels  16.5 us (12%)
  between operations  14.1 us (10%)
  starting transfers between devices  13 us (9%)
  local copies, waits for them, and re-layouts  4.39 us (3%)
    all_to_all x1, blocking collectives, local(): pieces = lax.all_to_all(pieces, 'chan', 0, 0, tiled=True)  25.3 us
    all_to_all x1, blocking collectives, local(): lax.all_to_all(spectral(got, all_features, own_decay), group, 0, 0, tiled...  21.5 us
    all_gather x1, waiting for transfers between devices, local(): all_features = lax.all_gather(filter_features, 'ctx')  20.5 us
    all_to_all x1, waiting for transfers between devices, local(): got = lax.all_to_all(sent, group, 0, 0, tiled=True)  11.2 us
    all_to_all x1, waiting for transfers between devices, local(): copies = lax.all_to_all(copies, 'chan', 0, 0, tiled=True)  9.96 us
    all_to_all x1, starting transfers between devices, local(): got = lax.all_to_all(sent, group, 0, 0, tiled=True)  9.48 us
    pallas_call x1, Pallas kernels, spectral(): pl.pallas_call(spectral_kernel, out_shape=jax.ShapeDtypeStruct((GROUP, 2...  9.32 us
    all_to_all x1, starting transfers between devices, local(): copies = lax.all_to_all(copies, 'chan', 0, 0, tiled=True)  3.5 us
  transfers between devices with their start and end apart: 3, of which 3 were waited for; matrix products, arithmetic and copies ran while one was open for 1% of the time, Pallas kernels for 4%

profile of v1, /device:TPU:6, one launch (start us, length us, event | category | flops | bytes accessed | tf_op | source)
XLA Modules:
  0.0 137.7 jit_solution(16026176192297352632)
XLA Ops:
  7.2 0.0 all-gather.3.cloned.1.call-start
  7.2 0.7 all-gather.3.cloned.1.call-update
  7.9 0.0 copy-start.1
  7.9 0.7 copy-done.1
  8.6 0.8 copy.17.decay
  9.4 0.6 pad_add_fusion.place
  10.0 2.5 %spread.1 = bf16[32,16,640]{2,1,0:T(8,128)(2,1)} custom-call(s32[2]{0:T(128)} %pad_add_fusion.place, bf16[512,256]{1,0:T(8,128)(2,1)} %bitcast.14, bf16[512,256]{1,0:T(8,128)(2,1)} %bitcast.16, bf16[512,256]{1,0:T(8,128)(2,1)} %bitcast.18, bf16[512,256]{1,0:T(8,128)(2,1)} %bitcast.20, bf16[64,512]{1,0:T(8,128)(2,1)} %features.1, bf16[64,256]{1,0:T(8,128)(2,1)} %weight.3, ...), custom_call_target="tpu_custom_call" | custom-call | tf_op jit(solution)/shard_map/spread/pallas_call | solution.py:144
  12.5 9.5 %all-to-all-start = ((bf16[32,16,640]{2,1,0:T(8,128)(2,1)}), bf16[32,16,640]{2,1,0:T(8,128)(2,1)S(1)}, u32[]{:S(2)}, u32[]{:S(2)}) async-start(bf16[32,16,640]{2,1,0:T(8,128)(2,1)} %spread.1), calls=%async_computation | async-start | bytes 1310720 | tf_op jit(solution)/shard_map/all_to_all | solution.py:416
  22.0 0.1 dynamic_slice.3
  22.0 11.2 %all-to-all-done.got = bf16[32,16,640]{2,1,0:T(8,128)(2,1)S(1)} async-done(((bf16[32,16,640]{2,1,0:T(8,128)(2,1)}), bf16[32,16,640]{2,1,0:T(8,128)(2,1)S(1)}, u32[]{:S(2)}, u32[]{:S(2)}) %all-to-all-start) | async-done | bytes 655392 | tf_op jit(solution)/shard_map/all_to_all | solution.py:416
  33.3 0.0 copy-start
  33.3 20.5 %all-gather.3.cloned.1.call-done = bf16[1024,512]{1,0:T(8,128)(2,1)} async-done(((bf16[64,512]{1,0:T(8,128)(2,1)}), bf16[1024,512]{1,0:T(8,128)(2,1)}) %all-gather.3.cloned.1.call-update) | async-done | bytes 1048592 | tf_op jit(solution)/shard_map/all_gather | solution.py:412
  53.7 0.7 broadcast_in_dim.31.decay
  54.4 0.0 copy-done
  54.4 9.3 %spectral.1 = bf16[32,16,896]{2,1,0:T(8,128)(2,1)} custom-call(bf16[32,16,640]{2,1,0:T(8,128)(2,1)} %copy-done, bf16[1024,512]{1,0:T(8,128)(2,1)} %constant.27.clone.basis, f32[2,17,512]{2,1,0:T(8,128)} %constant.28.clone.forward, f32[2,17,512]{2,1,0:T(8,128)} %constant.29.clone.inverse, bf16[16,64,512]{2,1,0:T(8,128)(2,1)} %bitcast.13, ...), custom_call_target="tpu_custom_call" | custom-call | tf_op jit(solution)/shard_map/spectral/pallas_call | solution.py:320
  63.7 21.5 %all_to_all.20.back = bf16[32,16,896]{2,1,0:T(8,128)(2,1)} all-to-all(bf16[32,16,896]{2,1,0:T(8,128)(2,1)} %spectral.1), channel_id=1, replica_groups=mesh['dp'=2,'chan'=16,'ctx'=16] {'dp','ctx'}, dimensions={0} | all-to-all | bytes 1835008 | tf_op jit(solution)/shard_map/all_to_all | solution.py:419
  85.2 2.0 %feature_part.1 = (bf16[64,512]{1,0:T(8,128)(2,1)}, f32[64,256]{1,0:T(8,128)}) custom-call(bf16[32,16,896]{2,1,0:T(8,128)(2,1)} %all_to_all.20.back, bf16[64,256]{1,0:T(8,128)(2,1)} %weight.3), custom_call_target="tpu_custom_call" | custom-call | tf_op jit(solution)/shard_map/feature_part/pallas_call | solution.py:348
  87.2 0.9 reshape.20
  88.0 25.3 %all_to_all.21 = bf16[16,4,512]{2,1,0:T(4,128)(2,1)S(1)} all-to-all(bf16[16,4,512]{2,1,0:T(4,128)(2,1)S(1)} %reshape.20), channel_id=1, replica_groups=mesh['dp'=2,'chan'=16,'ctx'=16] {'chan'}, dimensions={0} | all-to-all | bytes 131072 | tf_op jit(solution)/shard_map/all_to_all | solution.py:422
  113.4 0.7 broadcast_in_dim.37
  114.0 3.5 %all-to-all-start.3 = ((bf16[16,4,512]{2,1,0:T(4,128)(2,1)}), bf16[16,4,512]{2,1,0:T(4,128)(2,1)S(1)}, u32[]{:S(2)}, u32[]{:S(2)}) async-start(bf16[16,4,512]{2,1,0:T(4,128)(2,1)} %broadcast_in_dim.37), calls=%async_computation.3 | async-start | bytes 131072 | tf_op jit(solution)/shard_map/all_to_all | solution.py:425
  117.5 2.8 %final.1 = (bf16[512,256]{1,0:T(8,128)(2,1)}, bf16[512,256]{1,0:T(8,128)(2,1)}, bf16[512,256]{1,0:T(8,128)(2,1)}, bf16[512,256]{1,0:T(8,128)(2,1)}) custom-call(bf16[32,16,896]{2,1,0:T(8,128)(2,1)} %all_to_all.20.back, bf16[512,256]{1,0:T(8,128)(2,1)} %bitcast.15, bf16[512,256]{1,0:T(8,128)(2,1)} %bitcast.17, bf16[512,256]{1,0:T(8,128)(2,1)} %bitcast.19, ...), custom_call_target="tpu_custom_call" | custom-call | tf_op jit(solution)/shard_map/final/pallas_call | solution.py:384
  120.3 10.0 %all-to-all-done.3 = bf16[16,4,512]{2,1,0:T(4,128)(2,1)S(1)} async-done(((bf16[16,4,512]{2,1,0:T(4,128)(2,1)}), bf16[16,4,512]{2,1,0:T(4,128)(2,1)S(1)}, u32[]{:S(2)}, u32[]{:S(2)}) %all-to-all-start.3) | async-done | bytes 65568 | tf_op jit(solution)/shard_map/all_to_all | solution.py:425
  130.2 0.7 reshape.21
  (1 shorter events, 0.0 us)
Async XLA Ops:
  7.2 46.6 %all-gather.3.cloned.1.call-start = ((), (), s32[]{:S(2)}) async-start(), calls=%async_computation.4 | async-start | bytes 1114112 | tf_op jit(solution)/shard_map/all_gather | solution.py:412
  7.9 0.7 copy-start.1
  12.5 20.8 %all-to-all-start = ((bf16[32,16,640]{2,1,0:T(8,128)(2,1)}), bf16[32,16,640]{2,1,0:T(8,128)(2,1)S(1)}, u32[]{:S(2)}, u32[]{:S(2)}) async-start(bf16[32,16,640]{2,1,0:T(8,128)(2,1)} %spread.1), calls=%async_computation | async-start | bytes 1310720 | tf_op jit(solution)/shard_map/all_to_all | solution.py:416
  33.3 21.1 %copy-start = (bf16[32,16,640]{2,1,0:T(8,128)(2,1)}, bf16[32,16,640]{2,1,0:T(8,128)(2,1)S(1)}, u32[]{:S(2)}) copy-start(bf16[32,16,640]{2,1,0:T(8,128)(2,1)S(1)} %all-to-all-done.got) | copy-start | bytes 1966084
  114.0 16.2 %all-to-all-start.3 = ((bf16[16,4,512]{2,1,0:T(4,128)(2,1)}), bf16[16,4,512]{2,1,0:T(4,128)(2,1)S(1)}, u32[]{:S(2)}, u32[]{:S(2)}) async-start(bf16[16,4,512]{2,1,0:T(4,128)(2,1)} %broadcast_in_dim.37), calls=%async_computation.3 | async-start | bytes 131072 | tf_op jit(solution)/shard_map/all_to_all | solution.py:425
Sparse Core Ops, SparseCore 0:
  10.1 43.5 all-gather.2

commit v2 on v1

--- a/solution.py
+++ b/solution.py
@@ -115,7 +115,7 @@
     return [first[i // 2] if i % 2 == 0 else second[i // 2] for i in range(n // 2)]
 
 
-def spread_kernel(place, values, gate_first, gate_second, grad, features, weight, decay, out):
+def spread_kernel(values, gate_first, gate_second, grad, features, weight, decay, out):
     f32 = jnp.float32
     mixed = (values[...].astype(f32) * gate_first[...].astype(f32)).T
     scaled = (grad[...].astype(f32) * gate_second[...].astype(f32)).T
@@ -123,39 +123,41 @@
         [mixed.reshape(GROUP, OWN, TOK), scaled.reshape(GROUP, OWN, TOK)], axis=1
     )
     out[:, :, :TOK] = both.astype(jnp.bfloat16)
-    dp = place[0]
-    ctx = place[1]
+    dp = lax.axis_index("dp")
+    ctx = lax.axis_index("ctx")
     half = TOK // 2
     mine = jnp.where(dp == 0, features[:, :half].astype(f32), features[:, half:].astype(f32))
     raw = lax.dot_general(
+        mine.astype(jnp.bfloat16),
         weight[...],
-        mine.astype(jnp.bfloat16),
         (((0,), (0,)), ((), ())),
         preferred_element_type=f32,
     )
     first = ctx * TOK + dp * half
-    positions = (first + lax.broadcasted_iota(jnp.int32, (1, half), 1)).astype(f32) / LENGTH
-    kernel = (raw * jnp.exp(-decay[...] * positions)).reshape(GROUP, OWN, half)
+    positions = (first + lax.broadcasted_iota(jnp.int32, (half, 1), 0)).astype(f32) / LENGTH
+    kernel = (raw * jnp.exp(-decay[...] * positions)).T.reshape(GROUP, OWN, half)
     folded = jnp.concatenate([kernel[:, :, : half // 2], kernel[:, :, half // 2 :]], axis=1)
     out[:, :, TOK:] = folded.astype(jnp.bfloat16)
 
 
-def spread(place, values, gate_first, gate_second, grad, features, weight, decay, **kw):
+def spread(values, gate_first, gate_second, grad, features, weight, decay, **kw):
     return pl.pallas_call(
         spread_kernel,
         out_shape=jax.ShapeDtypeStruct((GROUP, 2 * OWN, TOK + 128), jnp.bfloat16),
-        in_specs=[pl.BlockSpec(memory_space=pltpu.SMEM)] + [pl.BlockSpec(memory_space=pltpu.VMEM)] * 7,
+        in_specs=[pl.BlockSpec(memory_space=pltpu.VMEM)] * 7,
         out_specs=pl.BlockSpec(memory_space=pltpu.VMEM),
         compiler_params=pltpu.CompilerParams(vmem_limit_bytes=VMEM_LIMIT),
         name="spread",
         **kw,
-    )(place, values, gate_first, gate_second, grad, features, weight, decay)
+    )(values, gate_first, gate_second, grad, features, weight, decay)
 
 
 def spectral_kernel(
-    got, basis, forward, inverse, features, decay, out, lhs_re, lhs_im, res_re, res_im, filt_re, filt_im, kernel_grad
+    got, basis, forward, inverse, decay, out, lhs_re, lhs_im, res_re, res_im, filt_re, filt_im, rates
 ):
     f32, bf16 = jnp.float32, jnp.bfloat16
+    rates[...] = jnp.broadcast_to(decay[...], (128, CH)).T
+    first = (lax.axis_index("dp") * BLOCKS + lax.axis_index("ctx")) * OWN
 
     def lanes_of(chunk):
         return pl.ds(pl.multiple_of(chunk * 128, 128), 128)
@@ -259,7 +261,7 @@
         return real_inverse(turned, RADIX)
 
     def filter_out(chunk, carry):
-        rate = decay[...]
+        rate = rates[pl.ds(pl.multiple_of(first, OWN), OWN), :]
         parts = []
         for q in range(2):
             lanes = lanes_of(chunk + 2 * q)
@@ -276,7 +278,6 @@
                 positions = (ahead + (TOK * j + 256 * q)).astype(f32) / LENGTH
                 pieces.append(parts[q][j] * jnp.exp(-rate * positions))
             both = jnp.concatenate(pieces, axis=0).astype(bf16)
-            kernel_grad[:, lanes_of(2 * j + chunk)] = both
             out[j, :, lanes_of(4 + chunk)] = both
             out[BLOCKS + j, :, lanes_of(4 + chunk)] = both
         return carry
@@ -296,67 +297,63 @@
 
     lax.fori_loop(0, 8, signals_out, 0)
 
-    sums = []
-    for q in range(2):
-        along = jnp.concatenate(
-            [features[j, :, 256 * q : 256 * (q + 1)] for j in range(BLOCKS)], axis=1
-        )
-        sums.append(
-            lax.dot_general(
-                kernel_grad[...], along, (((1,), (1,)), ((), ())), preferred_element_type=f32
-            )
-        )
-    own_weight = sums[0][:OWN] + sums[1][OWN:]
-    padded = jnp.concatenate([own_weight, jnp.zeros((OWN, 128 - ORDER), f32)], axis=1)
-    padded = jnp.concatenate([padded, jnp.zeros((OWN, 128), f32)], axis=0).astype(bf16)
-    out[:, :, TOK + 256 :] = jnp.broadcast_to(padded[None], (GROUP, 2 * OWN, 128))
-
-
-def spectral(got, features, decay, **kw):
+
+def spectral(got, decay, **kw):
     basis, forward, inverse = tables()
     wide = pltpu.VMEM((ROWS, 2 * OWN, TOK), jnp.bfloat16)
     result = pltpu.VMEM((ROWS, 2 * OWN, TOK), jnp.float32)
     filt = pltpu.VMEM((PAIRS, 2 * OWN, TOK), jnp.float32)
     return pl.pallas_call(
         spectral_kernel,
-        out_shape=jax.ShapeDtypeStruct((GROUP, 2 * OWN, TOK + 256 + 128), jnp.bfloat16),
-        in_specs=[pl.BlockSpec(memory_space=pltpu.VMEM)] * 6,
+        out_shape=jax.ShapeDtypeStruct((GROUP, 2 * OWN, TOK + 256), jnp.bfloat16),
+        in_specs=[pl.BlockSpec(memory_space=pltpu.VMEM)] * 5,
         out_specs=pl.BlockSpec(memory_space=pltpu.VMEM),
         scratch_shapes=[
             wide, wide, result, result, filt, filt,
-            pltpu.VMEM((2 * OWN, BLOCKS * 256), jnp.bfloat16),
+            pltpu.VMEM((CH, 128), jnp.float32),
         ],
         compiler_params=pltpu.CompilerParams(vmem_limit_bytes=VMEM_LIMIT),
         name="spectral",
         **kw,
-    )(got, jnp.asarray(basis), jnp.asarray(forward), jnp.asarray(inverse), features, decay)
-
-
-def feature_kernel(back, weight, part, weight_grad):
+    )(got, jnp.asarray(basis), jnp.asarray(forward), jnp.asarray(inverse), decay)
+
+
+def parts_kernel(back, features, weight, feature_part, weight_part):
     f32, bf16 = jnp.float32, jnp.bfloat16
+    half = TOK // 2
+    own = back[:, :, TOK:].astype(f32)
+    weight_sum = None
     for q in range(2):
-        kernel_grad = back[:, :, TOK : TOK + 256].astype(f32)[:, q * OWN : (q + 1) * OWN]
-        kernel_grad = kernel_grad.reshape(CH, 256).astype(bf16)
-        part[:, 256 * q : 256 * (q + 1)] = jnp.dot(
-            weight[...], kernel_grad, preferred_element_type=f32
-        ).astype(bf16)
-    own = back[:, :, TOK + 256 :].astype(f32)[:, :OWN].reshape(CH, 128)
-    weight_grad[...] = own.T[:ORDER]
-
-
-def feature_part(back, weight, **kw):
+        kernel_grad = own[:, q * OWN : (q + 1) * OWN].reshape(CH, half).astype(bf16)
+        along = jnp.dot(weight[...], kernel_grad, preferred_element_type=f32).astype(bf16)
+        for p in range(2):
+            for r in range(4):
+                feature_part[4 * r + 2 * q + p] = along[16 * r : 16 * (r + 1), 128 * p : 128 * (p + 1)]
+        weight_sum = add(
+            weight_sum,
+            lax.dot_general(
+                features[:, half * q : half * (q + 1)],
+                kernel_grad,
+                (((1,), (1,)), ((), ())),
+                preferred_element_type=f32,
+            ),
+        )
+    weight_part[...] = weight_sum.astype(bf16)
+
+
+def parts(back, features, weight, **kw):
     return pl.pallas_call(
-        feature_kernel,
+        parts_kernel,
         out_shape=(
-            jax.ShapeDtypeStruct((ORDER, TOK), jnp.bfloat16),
-            jax.ShapeDtypeStruct((ORDER, CH), jnp.float32),
+            jax.ShapeDtypeStruct((16, 16, 128), jnp.bfloat16),
+            jax.ShapeDtypeStruct((ORDER, CH), jnp.bfloat16),
         ),
-        in_specs=[pl.BlockSpec(memory_space=pltpu.VMEM)] * 2,
+        in_specs=[pl.BlockSpec(memory_space=pltpu.VMEM)] * 3,
         out_specs=(pl.BlockSpec(memory_space=pltpu.VMEM),) * 2,
         compiler_params=pltpu.CompilerParams(vmem_limit_bytes=VMEM_LIMIT),
-        name="feature_part",
+        name="parts",
         **kw,
-    )(back, weight)
+    )(back, features, weight)
 
 
 def final_kernel(
@@ -405,25 +402,22 @@
     values, gate_first, gate_second, output_grad = (
         a[0] for a in (values, gate_first, gate_second, output_grad)
     )
-    dp = lax.axis_index("dp")
-    ctx = lax.axis_index("ctx")
     group = ("dp", "ctx")
-    place = jnp.stack([dp, ctx]).astype(jnp.int32)
-    all_features = lax.all_gather(filter_features, "ctx")
-    sent = spread(
-        place, values, gate_first, gate_second, output_grad, filter_features, filter_weight, decay_rate[:, None]
-    )
+    decay = decay_rate[None, :]
+    sent = spread(values, gate_first, gate_second, output_grad, filter_features, filter_weight, decay)
     got = lax.all_to_all(sent, group, 0, 0, tiled=True)
-    own_decay = lax.dynamic_slice(decay_rate, ((dp * BLOCKS + ctx) * OWN,), (OWN,))
-    own_decay = jnp.broadcast_to(own_decay[:, None], (OWN, 128))
-    back = lax.all_to_all(spectral(got, all_features, own_decay), group, 0, 0, tiled=True)
-    part, weight_grad = feature_part(back, filter_weight)
-    pieces = part.reshape(16, 4, TOK)
-    pieces = lax.all_to_all(pieces, "chan", 0, 0, tiled=True)
+    back = lax.all_to_all(spectral(got, decay), group, 0, 0, tiled=True)
+    feature_part, weight_part = parts(back, filter_features, filter_weight)
+    pieces = lax.all_to_all(feature_part, "chan", 0, 0, tiled=True)
     summed = jnp.sum(pieces.astype(jnp.float32), axis=0).astype(jnp.bfloat16)
-    copies = jnp.broadcast_to(summed[None], (16, 4, TOK))
-    copies = lax.all_to_all(copies, "chan", 0, 0, tiled=True)
-    feature_grad = copies.reshape(ORDER, TOK).astype(jnp.float32)
+    copies = lax.all_to_all(jnp.broadcast_to(summed[None], (16, 16, 128)), "chan", 0, 0, tiled=True)
+    feature_grad = copies.reshape(4, 4, 16, 128).transpose(0, 2, 1, 3).reshape(ORDER, TOK)
+    feature_grad = feature_grad.astype(jnp.float32)
+    for distance in (1, 2, 4, 8):
+        other = lax.ppermute(weight_part, "ctx", [(i, i ^ distance) for i in range(BLOCKS)])
+        weight_sum = weight_part.astype(jnp.float32) + other.astype(jnp.float32)
+        weight_part = weight_sum.astype(jnp.bfloat16)
+    weight_grad = weight_sum
     outs = final(back, values, gate_first, gate_second, output_grad, skip_bias[None, :])
     output, values_grad, first_grad, second_grad = (a[None] for a in outs)
     return (output, values_grad, first_grad, second_grad, weight_grad, feature_grad)

time: 140 us -> 113 us (0.81)
  waiting for transfers between devices: 42.3 us -> 21.6 us
  starting transfers between devices: 13 us -> 29.5 us
  between operations: 14.1 us -> 0.72 us
  blocking collectives: 46.7 us -> 41.1 us
  local copies, waits for them, and re-layouts: 4.39 us -> 1.36 us
    all_gather x1 -> x0, waiting for transfers between devices: 20.5 us -> none  [local(): all_features = lax.all_gather(filter_features, 'ctx')]
    ppermute x0 -> x4, starting transfers between devices: none -> 12.3 us  [local(): lax.ppermute(weight_part, 'ctx', [(i, i ^ distance) for i in range(BLOCKS)])]
    all_to_all x2, blocking collectives: 46.7 us -> 41.1 us  [the longest x1 21.5 us: local(): got = lax.all_to_all(sent, group, 0, 0, tiled=True)]
    ppermute x0 -> x4, waiting for transfers between devices: none -> 4.62 us  [local(): lax.ppermute(weight_part, 'ctx', [(i, i ^ distance) for i in range(BLOCKS)])]
    all_to_all x2, waiting for transfers between devices: 21.2 us -> 16.9 us  [the longest x1 9.46 us: local(): lax.all_to_all(jnp.broadcast_to(summed[None], (16, 16, 128)), 'chan', 0,...]
    all_to_all x2, starting transfers between devices: 13 us -> 17.2 us  [the longest x1 12.7 us: local(): pieces = lax.all_to_all(feature_part, 'chan', 0, 0, tiled=True)]
    broadcast_in_dim x3 -> x1, local copies, waits for them, and re-layouts: 2.11 us -> 0.64 us  [local(): jnp.broadcast_to(summed[None], (16, 16, 128))]
  transfers between devices with their start and end apart: 3 -> 6, of which waited for: 3 -> 4; matrix products, arithmetic and copies ran while one was open for 1% -> 1% of each run, Pallas kernels for 4% -> 2%
where the time goes in v2:
time: 113 us; the launch traced here: 112 us
  blocking collectives  41.1 us (36%)
  starting transfers between devices  29.5 us (26%)
  waiting for transfers between devices  21.6 us (19%)
  Pallas kernels  15.7 us (14%)
  other arithmetic  1.47 us (1%)
  local copies, waits for them, and re-layouts  1.36 us (1%)
    all_to_all x1, blocking collectives, local(): got = lax.all_to_all(sent, group, 0, 0, tiled=True)  21.5 us
    all_to_all x1, blocking collectives, local(): back = lax.all_to_all(spectral(got, decay), group, 0, 0, tiled=True)  19.7 us
    all_to_all x1, starting transfers between devices, local(): pieces = lax.all_to_all(feature_part, 'chan', 0, 0, tiled=True)  12.7 us
    ppermute x4, starting transfers between devices, local(): lax.ppermute(weight_part, 'ctx', [(i, i ^ distance) for i in range(BLOCKS)])  12.3 us
    all_to_all x1, waiting for transfers between devices, local(): lax.all_to_all(jnp.broadcast_to(summed[None], (16, 16, 128)), 'chan', 0,...  9.46 us
    pallas_call x1, Pallas kernels, spectral(): pl.pallas_call(spectral_kernel, out_shape=jax.ShapeDtypeStruct((GROUP, 2...  8.57 us
    all_to_all x1, waiting for transfers between devices, local(): pieces = lax.all_to_all(feature_part, 'chan', 0, 0, tiled=True)  7.48 us
    ppermute x4, waiting for transfers between devices, local(): lax.ppermute(weight_part, 'ctx', [(i, i ^ distance) for i in range(BLOCKS)])  4.62 us
  transfers between devices with their start and end apart: 6, of which 4 were waited for; matrix products, arithmetic and copies ran while one was open for 1% of the time, Pallas kernels for 2%

profile of v2, /device:TPU:6, one launch (start us, length us, event | category | flops | bytes accessed | tf_op | source)
XLA Modules:
  0.0 111.5 jit_solution(10233599912431289871)
XLA Ops:
  0.6 2.4 %spread.1 = bf16[32,16,640]{2,1,0:T(8,128)(2,1)} custom-call(bf16[512,256]{1,0:T(8,128)(2,1)} %bitcast.19, bf16[512,256]{1,0:T(8,128)(2,1)} %bitcast.21, bf16[512,256]{1,0:T(8,128)(2,1)} %bitcast.23, bf16[512,256]{1,0:T(8,128)(2,1)} %bitcast.25, bf16[64,512]{1,0:T(8,128)(2,1)} %features.3, bf16[64,256]{1,0:T(8,128)(2,1)} %weight.3, f32[1,256]{1,0:T(1,128)} %bitcast.30), custom_call_target="tpu_custom_call" | custom-call | tf_op jit(solution)/shard_map/spread/pallas_call | solution.py:144
  3.1 21.5 %all_to_all.20.got = bf16[32,16,640]{2,1,0:T(8,128)(2,1)} all-to-all(bf16[32,16,640]{2,1,0:T(8,128)(2,1)} %spread.1), channel_id=1, replica_groups=mesh['dp'=2,'chan'=16,'ctx'=16] {'dp','ctx'}, dimensions={0} | all-to-all | bytes 1310720 | tf_op jit(solution)/shard_map/all_to_all | solution.py:408
  24.5 8.6 %spectral.1 = bf16[32,16,768]{2,1,0:T(8,128)(2,1)} custom-call(bf16[32,16,640]{2,1,0:T(8,128)(2,1)} %all_to_all.20.got, bf16[1024,512]{1,0:T(8,128)(2,1)} %constant.9.clone.basis, f32[2,17,512]{2,1,0:T(8,128)} %constant.10.clone.forward, f32[2,17,512]{2,1,0:T(8,128)} %constant.11.clone.inverse, f32[1,256]{1,0:T(1,128)} %bitcast.31), custom_call_target="tpu_custom_call" | custom-call | tf_op jit(solution)/shard_map/spectral/pallas_call | solution.py:306
  33.1 19.7 %all_to_all.21.back = bf16[32,16,768]{2,1,0:T(8,128)(2,1)} all-to-all(bf16[32,16,768]{2,1,0:T(8,128)(2,1)} %spectral.1), channel_id=1, replica_groups=mesh['dp'=2,'chan'=16,'ctx'=16] {'dp','ctx'}, dimensions={0} | all-to-all | bytes 1572864 | tf_op jit(solution)/shard_map/all_to_all | solution.py:409
  52.8 2.0 %parts.1 = (bf16[16,16,128]{2,1,0:T(8,128)(2,1)}, bf16[64,256]{1,0:T(8,128)(2,1)}) custom-call(bf16[32,16,768]{2,1,0:T(8,128)(2,1)} %all_to_all.21.back, bf16[64,512]{1,0:T(8,128)(2,1)} %features.3, bf16[64,256]{1,0:T(8,128)(2,1)} %weight.3), custom_call_target="tpu_custom_call" | custom-call | tf_op jit(solution)/shard_map/parts/pallas_call | solution.py:345
  54.8 2.0 %collective-permute-start = (bf16[64,256]{1,0:T(8,128)(2,1)}, bf16[64,256]{1,0:T(8,128)(2,1)S(1)}, u32[]{:S(2)}, u32[]{:S(2)}) collective-permute-start(bf16[64,256]{1,0:T(8,128)(2,1)} %get-tuple-element.16), channel_id=1, source_target_pairs={{0,1},{1,0},{2,3},{3,2},{4,5},{5,4},{6,7},{7,6},{8,9},{9,8},{10,11... | collective-permute-start | bytes 98312 | tf_op jit(solution)/shard_map/ppermute | solution.py:417
  56.8 1.3 %collective-permute-done = bf16[64,256]{1,0:T(8,128)(2,1)S(1)} collective-permute-done((bf16[64,256]{1,0:T(8,128)(2,1)}, bf16[64,256]{1,0:T(8,128)(2,1)S(1)}, u32[]{:S(2)}, u32[]{:S(2)}) %collective-permute-start) | collective-permute-done | bytes 32800 | tf_op jit(solution)/shard_map/ppermute | solution.py:417
  58.1 0.8 add_convert_fusion.2
  58.9 2.5 %collective-permute-start.1 = (bf16[64,256]{1,0:T(8,128)(2,1)S(1)}, bf16[64,256]{1,0:T(8,128)(2,1)S(1)}, u32[]{:S(2)}, u32[]{:S(2)}) collective-permute-start(bf16[64,256]{1,0:T(8,128)(2,1)S(1)} %add_convert_fusion.2), channel_id=1, source_target_pairs={{0,2},{1,3},{2,0},{3,1},{4,6},{5,7},{6,4},{7,5},{8,10},{9,11},{10,... | collective-permute-start | bytes 98312 | tf_op jit(solution)/shard_map/ppermute | solution.py:417
  61.4 3.3 %collective-permute-done.1 = bf16[64,256]{1,0:T(8,128)(2,1)S(1)} collective-permute-done((bf16[64,256]{1,0:T(8,128)(2,1)S(1)}, bf16[64,256]{1,0:T(8,128)(2,1)S(1)}, u32[]{:S(2)}, u32[]{:S(2)}) %collective-permute-start.1) | collective-permute-done | bytes 32800 | tf_op jit(solution)/shard_map/ppermute | solution.py:417
  64.7 2.5 %collective-permute-start.2 = (bf16[64,256]{1,0:T(8,128)(2,1)S(1)}, bf16[64,256]{1,0:T(8,128)(2,1)S(1)}, u32[]{:S(2)}, u32[]{:S(2)}) collective-permute-start(bf16[64,256]{1,0:T(8,128)(2,1)S(1)} %add_convert_fusion.1), channel_id=1, source_target_pairs={{0,4},{1,5},{2,6},{3,7},{4,0},{5,1},{6,2},{7,3},{8,12},{9,13},{10,... | collective-permute-start | bytes 98312 | tf_op jit(solution)/shard_map/ppermute | solution.py:417
  67.2 12.7 %all-to-all-start.2 = ((bf16[16,16,128]{2,1,0:T(8,128)(2,1)}), bf16[16,16,128]{2,1,0:T(8,128)(2,1)S(1)}, u32[]{:S(2)}, u32[]{:S(2)}) async-start(bf16[16,16,128]{2,1,0:T(8,128)(2,1)} %get-tuple-element.17), calls=%async_computation.2 | async-start | bytes 131072 | tf_op jit(solution)/shard_map/all_to_all | solution.py:411
  79.9 0.0 collective-permute-done.2
  79.9 5.3 %collective-permute-start.3 = (bf16[64,256]{1,0:T(8,128)(2,1)S(1)}, bf16[64,256]{1,0:T(8,128)(2,1)S(1)}, u32[]{:S(2)}, u32[]{:S(2)}) collective-permute-start(bf16[64,256]{1,0:T(8,128)(2,1)S(1)} %add_convert_fusion), channel_id=1, source_target_pairs={{0,8},{1,9},{2,10},{3,11},{4,12},{5,13},{6,14},{7,15},{8,0},{9,1},... | collective-permute-start | bytes 98312 | tf_op jit(solution)/shard_map/ppermute | solution.py:417
  85.3 7.5 %all-to-all-done.2 = bf16[16,16,128]{2,1,0:T(8,128)(2,1)S(1)} async-done(((bf16[16,16,128]{2,1,0:T(8,128)(2,1)}), bf16[16,16,128]{2,1,0:T(8,128)(2,1)S(1)}, u32[]{:S(2)}, u32[]{:S(2)}) %all-to-all-start.2) | async-done | bytes 65568 | tf_op jit(solution)/shard_map/all_to_all | solution.py:411
  92.8 0.6 broadcast_in_dim.30
  93.4 4.6 %all-to-all-start.3 = ((bf16[16,16,128]{2,1,0:T(8,128)(2,1)}), bf16[16,16,128]{2,1,0:T(8,128)(2,1)S(1)}, u32[]{:S(2)}, u32[]{:S(2)}) async-start(bf16[16,16,128]{2,1,0:T(8,128)(2,1)} %broadcast_in_dim.30), calls=%async_computation.3 | async-start | bytes 131072 | tf_op jit(solution)/shard_map/all_to_all | solution.py:413
  98.0 2.7 %final.1 = (bf16[512,256]{1,0:T(8,128)(2,1)}, bf16[512,256]{1,0:T(8,128)(2,1)}, bf16[512,256]{1,0:T(8,128)(2,1)}, bf16[512,256]{1,0:T(8,128)(2,1)}) custom-call(bf16[32,16,768]{2,1,0:T(8,128)(2,1)} %all_to_all.21.back, bf16[512,256]{1,0:T(8,128)(2,1)} %bitcast.20, bf16[512,256]{1,0:T(8,128)(2,1)} %bitcast.22, bf16[512,256]{1,0:T(8,128)(2,1)} %bitcast.24, ...), custom_call_target="tpu_custom_call" | custom-call | tf_op jit(solution)/shard_map/final/pallas_call | solution.py:381
  100.7 0.0 collective-permute-done.3
  100.7 0.6 convert_add_fusion
  101.3 9.5 %all-to-all-done.3 = bf16[16,16,128]{2,1,0:T(8,128)(2,1)S(1)} async-done(((bf16[16,16,128]{2,1,0:T(8,128)(2,1)}), bf16[16,16,128]{2,1,0:T(8,128)(2,1)S(1)}, u32[]{:S(2)}, u32[]{:S(2)}) %all-to-all-start.3) | async-done | bytes 65568 | tf_op jit(solution)/shard_map/all_to_all | solution.py:413
  110.8 0.1 copy.17
  110.8 0.7 copy.20
  (4 shorter events, 0.1 us)
Async XLA Ops:
  54.8 3.3 %collective-permute-start = (bf16[64,256]{1,0:T(8,128)(2,1)}, bf16[64,256]{1,0:T(8,128)(2,1)S(1)}, u32[]{:S(2)}, u32[]{:S(2)}) collective-permute-start(bf16[64,256]{1,0:T(8,128)(2,1)} %get-tuple-element.16), channel_id=1, source_target_pairs={{0,1},{1,0},{2,3},{3,2},{4,5},{5,4},{6,7},{7,6},{8,9},{9,8},{10,11... | collective-permute-start | bytes 98312 | tf_op jit(solution)/shard_map/ppermute | solution.py:417
  58.9 5.8 %collective-permute-start.1 = (bf16[64,256]{1,0:T(8,128)(2,1)S(1)}, bf16[64,256]{1,0:T(8,128)(2,1)S(1)}, u32[]{:S(2)}, u32[]{:S(2)}) collective-permute-start(bf16[64,256]{1,0:T(8,128)(2,1)S(1)} %add_convert_fusion.2), channel_id=1, source_target_pairs={{0,2},{1,3},{2,0},{3,1},{4,6},{5,7},{6,4},{7,5},{8,10},{9,11},{10,... | collective-permute-start | bytes 98312 | tf_op jit(solution)/shard_map/ppermute | solution.py:417
  64.7 15.2 %collective-permute-start.2 = (bf16[64,256]{1,0:T(8,128)(2,1)S(1)}, bf16[64,256]{1,0:T(8,128)(2,1)S(1)}, u32[]{:S(2)}, u32[]{:S(2)}) collective-permute-start(bf16[64,256]{1,0:T(8,128)(2,1)S(1)} %add_convert_fusion.1), channel_id=1, source_target_pairs={{0,4},{1,5},{2,6},{3,7},{4,0},{5,1},{6,2},{7,3},{8,12},{9,13},{10,... | collective-permute-start | bytes 98312 | tf_op jit(solution)/shard_map/ppermute | solution.py:417
  67.2 25.5 %all-to-all-start.2 = ((bf16[16,16,128]{2,1,0:T(8,128)(2,1)}), bf16[16,16,128]{2,1,0:T(8,128)(2,1)S(1)}, u32[]{:S(2)}, u32[]{:S(2)}) async-start(bf16[16,16,128]{2,1,0:T(8,128)(2,1)} %get-tuple-element.17), calls=%async_computation.2 | async-start | bytes 131072 | tf_op jit(solution)/shard_map/all_to_all | solution.py:411
  79.9 20.8 %collective-permute-start.3 = (bf16[64,256]{1,0:T(8,128)(2,1)S(1)}, bf16[64,256]{1,0:T(8,128)(2,1)S(1)}, u32[]{:S(2)}, u32[]{:S(2)}) collective-permute-start(bf16[64,256]{1,0:T(8,128)(2,1)S(1)} %add_convert_fusion), channel_id=1, source_target_pairs={{0,8},{1,9},{2,10},{3,11},{4,12},{5,13},{6,14},{7,15},{8,0},{9,1},... | collective-permute-start | bytes 98312 | tf_op jit(solution)/shard_map/ppermute | solution.py:417
  93.4 17.4 %all-to-all-start.3 = ((bf16[16,16,128]{2,1,0:T(8,128)(2,1)}), bf16[16,16,128]{2,1,0:T(8,128)(2,1)S(1)}, u32[]{:S(2)}, u32[]{:S(2)}) async-start(bf16[16,16,128]{2,1,0:T(8,128)(2,1)} %broadcast_in_dim.30), calls=%async_computation.3 | async-start | bytes 131072 | tf_op jit(solution)/shard_map/all_to_all | solution.py:413

commit v3 on v2

--- a/solution.py
+++ b/solution.py
@@ -115,17 +115,23 @@
     return [first[i // 2] if i % 2 == 0 else second[i // 2] for i in range(n // 2)]
 
 
-def spread_kernel(values, gate_first, gate_second, grad, features, weight, decay, out):
+def spread_kernel(
+    values, gate_first, gate_second, grad, features, weight, decay, out, held, ready, arrived, left
+):
     f32 = jnp.float32
-    mixed = (values[...].astype(f32) * gate_first[...].astype(f32)).T
-    scaled = (grad[...].astype(f32) * gate_second[...].astype(f32)).T
-    both = jnp.concatenate(
-        [mixed.reshape(GROUP, OWN, TOK), scaled.reshape(GROUP, OWN, TOK)], axis=1
-    )
-    out[:, :, :TOK] = both.astype(jnp.bfloat16)
+    half = TOK // 2
+    wide = CH // 2
+    loads = []
+    for part in range(2):
+        lanes = pl.ds(part * wide, wide)
+        for slot, source in enumerate((values, gate_first, grad, gate_second)):
+            copy = pltpu.make_async_copy(
+                source.at[:, lanes], held.at[part, slot], arrived.at[part, slot]
+            )
+            copy.start()
+            loads.append(copy)
     dp = lax.axis_index("dp")
     ctx = lax.axis_index("ctx")
-    half = TOK // 2
     mine = jnp.where(dp == 0, features[:, :half].astype(f32), features[:, half:].astype(f32))
     raw = lax.dot_general(
         mine.astype(jnp.bfloat16),
@@ -137,15 +143,40 @@
     positions = (first + lax.broadcasted_iota(jnp.int32, (half, 1), 0)).astype(f32) / LENGTH
     kernel = (raw * jnp.exp(-decay[...] * positions)).T.reshape(GROUP, OWN, half)
     folded = jnp.concatenate([kernel[:, :, : half // 2], kernel[:, :, half // 2 :]], axis=1)
-    out[:, :, TOK:] = folded.astype(jnp.bfloat16)
+    ready[:, :, TOK:] = folded.astype(jnp.bfloat16)
+    stores = []
+    owners = GROUP // 2
+    for part in range(2):
+        for copy in loads[4 * part : 4 * part + 4]:
+            copy.wait()
+        mixed = (held[part, 0].astype(f32) * held[part, 1].astype(f32)).T
+        scaled = (held[part, 2].astype(f32) * held[part, 3].astype(f32)).T
+        both = jnp.concatenate(
+            [mixed.reshape(owners, OWN, TOK), scaled.reshape(owners, OWN, TOK)], axis=1
+        )
+        rows = pl.ds(part * owners, owners)
+        ready[part * owners : (part + 1) * owners, :, :TOK] = both.astype(jnp.bfloat16)
+        copy = pltpu.make_async_copy(ready.at[rows], out.at[rows], left.at[part])
+        copy.start()
+        stores.append(copy)
+    for copy in stores:
+        copy.wait()
 
 
 def spread(values, gate_first, gate_second, grad, features, weight, decay, **kw):
+    shape = (GROUP, 2 * OWN, TOK + 128)
+    anywhere = pl.BlockSpec(memory_space=pl.ANY)
     return pl.pallas_call(
         spread_kernel,
-        out_shape=jax.ShapeDtypeStruct((GROUP, 2 * OWN, TOK + 128), jnp.bfloat16),
-        in_specs=[pl.BlockSpec(memory_space=pltpu.VMEM)] * 7,
-        out_specs=pl.BlockSpec(memory_space=pltpu.VMEM),
+        out_shape=jax.ShapeDtypeStruct(shape, jnp.bfloat16),
+        in_specs=[anywhere] * 4 + [pl.BlockSpec(memory_space=pltpu.VMEM)] * 3,
+        out_specs=anywhere,
+        scratch_shapes=[
+            pltpu.VMEM((2, 4, TOK, CH // 2), jnp.bfloat16),
+            pltpu.VMEM(shape, jnp.bfloat16),
+            pltpu.SemaphoreType.DMA((2, 4)),
+            pltpu.SemaphoreType.DMA((2,)),
+        ],
         compiler_params=pltpu.CompilerParams(vmem_limit_bytes=VMEM_LIMIT),
         name="spread",
         **kw,
@@ -153,9 +184,23 @@
 
 
 def spectral_kernel(
-    got, basis, forward, inverse, decay, out, lhs_re, lhs_im, res_re, res_im, filt_re, filt_im, rates
+    source, table, forward, inverse, decay, target,
+    got, basis, out, lhs_re, lhs_im, res_re, res_im, rates, arrived, left,
 ):
     f32, bf16 = jnp.float32, jnp.bfloat16
+
+    def load(s):
+        rows = pl.ds(s * BLOCKS, BLOCKS)
+        return pltpu.make_async_copy(source.at[rows], got.at[rows], arrived.at[s])
+
+    def store(s):
+        rows = pl.ds(s * BLOCKS, BLOCKS)
+        return pltpu.make_async_copy(out.at[rows], target.at[rows], left.at[s])
+
+    table_load = pltpu.make_async_copy(table, basis, arrived.at[2])
+    load(0).start()
+    load(1).start()
+    table_load.start()
     rates[...] = jnp.broadcast_to(decay[...], (128, CH)).T
     first = (lax.axis_index("dp") * BLOCKS + lax.axis_index("ctx")) * OWN
 
@@ -177,20 +222,16 @@
                 turned.append((real * c + imag * s, imag * c - real * s))
         return turned
 
-    def signals_in(step, carry):
-        s = step // 4
-        lanes = lanes_of(step % 4)
+    def signals_in(s, chunk):
+        lanes = lanes_of(chunk)
         xs = [got[s * BLOCKS + j, :, lanes].astype(f32) for j in range(BLOCKS)]
         low = transformed([x[:OWN] for x in xs], lanes)
         high = transformed([x[OWN:] for x in xs], lanes)
         for k in range(HALF):
             lhs_re[2 * k + s, :, lanes] = jnp.concatenate([low[k][0], high[k][0]], axis=0).astype(bf16)
             lhs_im[2 * k + s, :, lanes] = jnp.concatenate([low[k][1], high[k][1]], axis=0).astype(bf16)
-        return carry
-
-    lax.fori_loop(0, 8, signals_in, 0)
-
-    def kernel_in(s, carry):
+
+    def kernel_in(s):
         xs = [got[s * BLOCKS + j, :, TOK:].astype(f32) for j in range(BLOCKS)]
         for q in range(2):
             lanes = lanes_of(2 * s + q)
@@ -200,9 +241,20 @@
                 a, b = spec[2 * p], spec[2 * p + 1]
                 lhs_re[2 * HALF + p, :, lanes] = jnp.concatenate([a[0], b[0]], axis=0).astype(bf16)
                 lhs_im[2 * HALF + p, :, lanes] = jnp.concatenate([a[1], b[1]], axis=0).astype(bf16)
+
+    def sequence_in(s, carry):
+        load(s).wait()
+
+        def chunk_in(chunk, inner):
+            signals_in(s, chunk)
+            return inner
+
+        lax.fori_loop(0, 4, chunk_in, 0)
+        kernel_in(s)
         return carry
 
-    lax.fori_loop(0, 2, kernel_in, 0)
+    lax.fori_loop(0, 2, sequence_in, 0)
+    table_load.wait()
 
     def product(first, second):
         lhs = jnp.concatenate([first, second], axis=1)
@@ -214,12 +266,7 @@
     res_re[...] = product(real, imag)
     res_im[...] = product(imag, -real)
 
-    filt_re[...] = jnp.zeros_like(filt_re)
-    filt_im[...] = jnp.zeros_like(filt_im)
-
-    def multiply(k, carry):
-        pair = k // 2
-        rows = pl.ds(pl.multiple_of(k % 2 * OWN, OWN), OWN)
+    def multiply(k, pair, rows):
         hr = res_re[2 * HALF + pair, rows, :]
         hi = res_im[2 * HALF + pair, rows, :]
         total_re, total_im = None, None
@@ -236,13 +283,21 @@
             ).astype(bf16)
             total_re = add(total_re, gr * zr + gi * zi)
             total_im = add(total_im, gi * zr - gr * zi)
-        filt_re[pair, rows, :] = total_re
-        filt_im[pair, rows, :] = total_im
+        return total_re, total_im
+
+    def multiply_pair(pair, carry):
+        a = multiply(2 * pair, pair, slice(0, OWN))
+        b = multiply(2 * pair + 1, pair, slice(OWN, 2 * OWN))
+        lhs_re[2 * HALF + pair] = jnp.concatenate([a[0], b[0]], axis=0).astype(bf16)
+        lhs_im[2 * HALF + pair] = jnp.concatenate([a[1], b[1]], axis=0).astype(bf16)
         return carry
 
-    lax.fori_loop(0, HALF, multiply, 0)
-    lhs_re[2 * HALF :] = filt_re[...].astype(bf16)
-    lhs_im[2 * HALF :] = filt_im[...].astype(bf16)
+    lax.fori_loop(0, PAIRS - 1, multiply_pair, 0, unroll=2)
+    last = PAIRS - 1
+    a = multiply(2 * last, last, slice(0, OWN))
+    blank = jnp.zeros_like(a[0])
+    lhs_re[2 * HALF + last] = jnp.concatenate([a[0], blank], axis=0).astype(bf16)
+    lhs_im[2 * HALF + last] = jnp.concatenate([a[1], blank], axis=0).astype(bf16)
 
     real = lhs_re[...].reshape(ROWS * 2 * OWN, TOK)
     imag = lhs_im[...].reshape(ROWS * 2 * OWN, TOK)
@@ -260,9 +315,11 @@
                 turned.append((real * c - imag * s, imag * c + real * s))
         return real_inverse(turned, RADIX)
 
+    rate = rates[pl.ds(pl.multiple_of(first, OWN), OWN), :]
+    steps = [jnp.exp(-rate * (TOK * j / LENGTH)) for j in range(BLOCKS)]
+
     def filter_out(chunk, carry):
-        rate = rates[pl.ds(pl.multiple_of(first, OWN), OWN), :]
-        parts = []
+        pieces = []
         for q in range(2):
             lanes = lanes_of(chunk + 2 * q)
             spec = []
@@ -270,47 +327,59 @@
                 rows = slice(k % 2 * OWN, k % 2 * OWN + OWN)
                 block = 2 * HALF + k // 2
                 spec.append((res_re[block, rows, lanes], res_im[block, rows, lanes]))
-            parts.append(returned(spec, lanes))
-        ahead = lax.broadcasted_iota(jnp.int32, (OWN, 128), 1) + chunk * 128
+            ahead = lax.broadcasted_iota(jnp.int32, (OWN, 128), 1) + (chunk * 128 + 256 * q)
+            fine = jnp.exp(-rate * (ahead.astype(f32) / LENGTH))
+            pieces.append([y * (fine * steps[j]) for j, y in enumerate(returned(spec, lanes))])
         for j in range(BLOCKS):
-            pieces = []
-            for q in range(2):
-                positions = (ahead + (TOK * j + 256 * q)).astype(f32) / LENGTH
-                pieces.append(parts[q][j] * jnp.exp(-rate * positions))
-            both = jnp.concatenate(pieces, axis=0).astype(bf16)
+            both = jnp.concatenate([pieces[0][j], pieces[1][j]], axis=0).astype(bf16)
             out[j, :, lanes_of(4 + chunk)] = both
             out[BLOCKS + j, :, lanes_of(4 + chunk)] = both
         return carry
 
     lax.fori_loop(0, 2, filter_out, 0)
 
-    def signals_out(step, carry):
-        s = step // 4
-        lanes = lanes_of(step % 4)
-        halves = []
-        for rows in (slice(0, OWN), slice(OWN, 2 * OWN)):
-            spec = [(res_re[2 * k + s, rows, lanes], res_im[2 * k + s, rows, lanes]) for k in range(HALF)]
-            halves.append(returned(spec, lanes))
-        for j in range(BLOCKS):
-            out[s * BLOCKS + j, :, lanes] = jnp.concatenate([halves[0][j], halves[1][j]], axis=0).astype(bf16)
+    def sequence_out(s, carry):
+        def chunk_out(chunk, inner):
+            lanes = lanes_of(chunk)
+            halves = []
+            for rows in (slice(0, OWN), slice(OWN, 2 * OWN)):
+                spec = [
+                    (res_re[2 * k + s, rows, lanes], res_im[2 * k + s, rows, lanes]) for k in range(HALF)
+                ]
+                halves.append(returned(spec, lanes))
+            for j in range(BLOCKS):
+                both = jnp.concatenate([halves[0][j], halves[1][j]], axis=0).astype(bf16)
+                out[s * BLOCKS + j, :, lanes] = both
+            return inner
+
+        lax.fori_loop(0, 4, chunk_out, 0)
+        store(s).start()
         return carry
 
-    lax.fori_loop(0, 8, signals_out, 0)
+    lax.fori_loop(0, 2, sequence_out, 0)
+    store(0).wait()
+    store(1).wait()
 
 
 def spectral(got, decay, **kw):
     basis, forward, inverse = tables()
     wide = pltpu.VMEM((ROWS, 2 * OWN, TOK), jnp.bfloat16)
     result = pltpu.VMEM((ROWS, 2 * OWN, TOK), jnp.float32)
-    filt = pltpu.VMEM((PAIRS, 2 * OWN, TOK), jnp.float32)
+    shape = (GROUP, 2 * OWN, TOK + 256)
+    anywhere = pl.BlockSpec(memory_space=pl.ANY)
     return pl.pallas_call(
         spectral_kernel,
-        out_shape=jax.ShapeDtypeStruct((GROUP, 2 * OWN, TOK + 256), jnp.bfloat16),
-        in_specs=[pl.BlockSpec(memory_space=pltpu.VMEM)] * 5,
-        out_specs=pl.BlockSpec(memory_space=pltpu.VMEM),
+        out_shape=jax.ShapeDtypeStruct(shape, jnp.bfloat16),
+        in_specs=[anywhere] * 2 + [pl.BlockSpec(memory_space=pltpu.VMEM)] * 3,
+        out_specs=anywhere,
         scratch_shapes=[
-            wide, wide, result, result, filt, filt,
+            pltpu.VMEM(got.shape, jnp.bfloat16),
+            pltpu.VMEM(basis.shape, jnp.bfloat16),
+            pltpu.VMEM(shape, jnp.bfloat16),
+            wide, wide, result, result,
             pltpu.VMEM((CH, 128), jnp.float32),
+            pltpu.SemaphoreType.DMA((3,)),
+            pltpu.SemaphoreType.DMA((2,)),
         ],
         compiler_params=pltpu.CompilerParams(vmem_limit_bytes=VMEM_LIMIT),
         name="spectral",
@@ -318,42 +387,76 @@
     )(got, jnp.asarray(basis), jnp.asarray(forward), jnp.asarray(inverse), decay)
 
 
-def parts_kernel(back, features, weight, feature_part, weight_part):
+def parts_kernel(back, features, weight, sums, own, arrived):
     f32, bf16 = jnp.float32, jnp.bfloat16
     half = TOK // 2
-    own = back[:, :, TOK:].astype(f32)
-    weight_sum = None
+    copy = pltpu.make_async_copy(back.at[:, :, pl.ds(TOK, half)], own, arrived)
+    copy.start()
+    copy.wait()
+    is_feature = lax.axis_index("dp") == 0
+    alongs, weight_sum = [], None
     for q in range(2):
-        kernel_grad = own[:, q * OWN : (q + 1) * OWN].reshape(CH, half).astype(bf16)
-        along = jnp.dot(weight[...], kernel_grad, preferred_element_type=f32).astype(bf16)
-        for p in range(2):
-            for r in range(4):
-                feature_part[4 * r + 2 * q + p] = along[16 * r : 16 * (r + 1), 128 * p : 128 * (p + 1)]
-        weight_sum = add(
-            weight_sum,
-            lax.dot_general(
-                features[:, half * q : half * (q + 1)],
-                kernel_grad,
-                (((1,), (1,)), ((), ())),
-                preferred_element_type=f32,
-            ),
+        kernel_grad = own[...].astype(f32)[:, q * OWN : (q + 1) * OWN].reshape(CH, half).astype(bf16)
+        alongs.append(jnp.dot(weight[...], kernel_grad, preferred_element_type=f32))
+        share = lax.dot_general(
+            features[:, half * q : half * (q + 1)],
+            kernel_grad,
+            (((1,), (1,)), ((), ())),
+            preferred_element_type=f32,
         )
-    weight_part[...] = weight_sum.astype(bf16)
+        weight_sum = add(weight_sum, share)
+    blank = jnp.zeros((8, 128), f32)
+    for piece in range(16):
+        r, c = piece // 4, piece % 4
+        feature = alongs[c // 2][16 * r : 16 * (r + 1), 128 * (c % 2) : 128 * (c % 2 + 1)]
+        r, c = piece // 2, piece % 2
+        other = weight_sum[8 * r : 8 * (r + 1), 128 * c : 128 * (c + 1)]
+        other = jnp.concatenate([other, blank], axis=0)
+        sums[piece] = jnp.where(is_feature, feature, other).astype(bf16)
 
 
 def parts(back, features, weight, **kw):
     return pl.pallas_call(
         parts_kernel,
-        out_shape=(
-            jax.ShapeDtypeStruct((16, 16, 128), jnp.bfloat16),
-            jax.ShapeDtypeStruct((ORDER, CH), jnp.bfloat16),
-        ),
-        in_specs=[pl.BlockSpec(memory_space=pltpu.VMEM)] * 3,
-        out_specs=(pl.BlockSpec(memory_space=pltpu.VMEM),) * 2,
+        out_shape=jax.ShapeDtypeStruct((16, 16, 128), jnp.bfloat16),
+        in_specs=[pl.BlockSpec(memory_space=pl.ANY)] + [pl.BlockSpec(memory_space=pltpu.VMEM)] * 2,
+        out_specs=pl.BlockSpec(memory_space=pltpu.VMEM),
+        scratch_shapes=[
+            pltpu.VMEM((GROUP, 2 * OWN, TOK // 2), jnp.bfloat16),
+            pltpu.SemaphoreType.DMA(()),
+        ],
         compiler_params=pltpu.CompilerParams(vmem_limit_bytes=VMEM_LIMIT),
         name="parts",
         **kw,
     )(back, features, weight)
+
+
+def assemble_kernel(own, other, feature_grad, weight_grad):
+    f32 = jnp.float32
+    is_feature = lax.axis_index("dp") == 0
+    for piece in range(16):
+        a = own[piece].astype(f32)
+        b = other[piece].astype(f32)
+        feature = jnp.where(is_feature, a, b)
+        weight = jnp.where(is_feature, b, a)[:8]
+        r, c = piece // 4, piece % 4
+        feature_grad[16 * r : 16 * (r + 1), 128 * c : 128 * (c + 1)] = feature
+        r, c = piece // 2, piece % 2
+        weight_grad[8 * r : 8 * (r + 1), 128 * c : 128 * (c + 1)] = weight
+
+
+def assemble(own, other, **kw):
+    return pl.pallas_call(
+        assemble_kernel,
+        out_shape=(
+            jax.ShapeDtypeStruct((ORDER, TOK), jnp.float32),
+            jax.ShapeDtypeStruct((ORDER, CH), jnp.float32),
+        ),
+        in_specs=[pl.BlockSpec(memory_space=pltpu.VMEM)] * 2,
+        out_specs=(pl.BlockSpec(memory_space=pltpu.VMEM),) * 2,
+        name="assemble",
+        **kw,
+    )(own, other)
 
 
 def final_kernel(
@@ -407,18 +510,20 @@
     sent = spread(values, gate_first, gate_second, output_grad, filter_features, filter_weight, decay)
     got = lax.all_to_all(sent, group, 0, 0, tiled=True)
     back = lax.all_to_all(spectral(got, decay), group, 0, 0, tiled=True)
-    feature_part, weight_part = parts(back, filter_features, filter_weight)
-    pieces = lax.all_to_all(feature_part, "chan", 0, 0, tiled=True)
+    everywhere = ("dp", "chan", "ctx")
+    groups = [[16 * z + j for z in range(16)] for j in range(16)]
+    groups += [[256 + 16 * z + j for j in range(16)] for z in range(16)]
+
+    def exchange(pieces):
+        return lax.all_to_all(pieces, everywhere, 0, 0, axis_index_groups=groups, tiled=True)
+
+    pieces = exchange(parts(back, filter_features, filter_weight))
     summed = jnp.sum(pieces.astype(jnp.float32), axis=0).astype(jnp.bfloat16)
-    copies = lax.all_to_all(jnp.broadcast_to(summed[None], (16, 16, 128)), "chan", 0, 0, tiled=True)
-    feature_grad = copies.reshape(4, 4, 16, 128).transpose(0, 2, 1, 3).reshape(ORDER, TOK)
-    feature_grad = feature_grad.astype(jnp.float32)
-    for distance in (1, 2, 4, 8):
-        other = lax.ppermute(weight_part, "ctx", [(i, i ^ distance) for i in range(BLOCKS)])
-        weight_sum = weight_part.astype(jnp.float32) + other.astype(jnp.float32)
-        weight_part = weight_sum.astype(jnp.bfloat16)
-    weight_grad = weight_sum
+    copies = exchange(jnp.broadcast_to(summed[None], (16, 16, 128)))
+    back, copies = lax.optimization_barrier((back, copies))
+    other = lax.ppermute(copies, "dp", [(0, 1), (1, 0)])
     outs = final(back, values, gate_first, gate_second, output_grad, skip_bias[None, :])
+    feature_grad, weight_grad = assemble(copies, other)
     output, values_grad, first_grad, second_grad = (a[None] for a in outs)
     return (output, values_grad, first_grad, second_grad, weight_grad, feature_grad)
 

time: 113 us -> 109 us (0.965)
  blocking collectives: 41.1 us -> 82.3 us
  starting transfers between devices: 29.5 us -> 1.91 us
  waiting for transfers between devices: 21.6 us -> 3.02 us
  Pallas kernels: 15.7 us -> 18.7 us
  other arithmetic: 1.47 us -> 0.02 us
    all_to_all x0 -> x2, blocking collectives: none -> 41.1 us  [exchange(): lax.all_to_all(pieces, everywhere, 0, 0, axis_index_groups=groups, tiled=...]
    all_to_all x2 -> x0, starting transfers between devices: 17.2 us -> none  [the longest x1 12.7 us: local(): pieces = lax.all_to_all(feature_part, 'chan', 0, 0, tiled=True)]
    all_to_all x2 -> x0, waiting for transfers between devices: 16.9 us -> none  [the longest x1 9.46 us: local(): lax.all_to_all(jnp.broadcast_to(summed[None], (16, 16, 128)), 'chan', 0,...]
    ppermute x4 -> x1, starting transfers between devices: 12.3 us -> 1.91 us  [local(): other = lax.ppermute(copies, 'dp', [(0, 1), (1, 0)])]
    pallas_call x3 -> x4, Pallas kernels: 13 us -> 16 us  [the longest x1 8.6 us: spectral(): pl.pallas_call(spectral_kernel, out_shape=jax.ShapeDtypeStruct(shape, jnp...]
    ppermute x4 -> x1, waiting for transfers between devices: 4.62 us -> 3.02 us  [local(): other = lax.ppermute(copies, 'dp', [(0, 1), (1, 0)])]
  transfers between devices with their start and end apart: 6 -> 1, of which waited for: 4 -> 1; matrix products, arithmetic and copies ran while one was open for 1% -> 0% of each run, Pallas kernels for 2% -> 3%
where the time goes in v3:
time: 109 us; the launch traced here: 107 us
  blocking collectives  82.3 us (76%)
  Pallas kernels  18.7 us (17%)
  waiting for transfers between devices  3.02 us (3%)
  starting transfers between devices  1.91 us (2%)
    all_to_all x2, blocking collectives, exchange(): lax.all_to_all(pieces, everywhere, 0, 0, axis_index_groups=groups, tiled=...  41.1 us
    all_to_all x1, blocking collectives, local(): got = lax.all_to_all(sent, group, 0, 0, tiled=True)  21.5 us
    all_to_all x1, blocking collectives, local(): back = lax.all_to_all(spectral(got, decay), group, 0, 0, tiled=True)  19.7 us
    pallas_call x1, Pallas kernels, spectral(): pl.pallas_call(spectral_kernel, out_shape=jax.ShapeDtypeStruct(shape, jnp...  8.6 us
    pallas_call x1, Pallas kernels, spread(): pl.pallas_call(spread_kernel, out_shape=jax.ShapeDtypeStruct(shape, jnp.b...  3.1 us
    ppermute x1, waiting for transfers between devices, local(): other = lax.ppermute(copies, 'dp', [(0, 1), (1, 0)])  3.02 us
    pallas_call x1, Pallas kernels, final(): pl.pallas_call(final_kernel, out_shape=(shape,) * 4, in_specs=[pl.BlockSp...  2.71 us
    pallas_call x1, Pallas kernels, parts(): pl.pallas_call(parts_kernel, out_shape=jax.ShapeDtypeStruct((16, 16, 128)...  2.68 us
  transfers between devices with their start and end apart: 1, of which 1 were waited for; matrix products, arithmetic and copies ran while one was open for 0% of the time, Pallas kernels for 3%

profile of v3, /device:TPU:6, one launch (start us, length us, event | category | flops | bytes accessed | tf_op | source)
XLA Modules:
  0.0 107.3 jit_solution(11616651743714307999)
XLA Ops:
  0.6 3.1 %spread.1 = bf16[32,16,640]{2,1,0:T(8,128)(2,1)} custom-call(bf16[512,256]{1,0:T(8,128)(2,1)} %bitcast.10, bf16[512,256]{1,0:T(8,128)(2,1)} %bitcast.12, bf16[512,256]{1,0:T(8,128)(2,1)} %bitcast.14, bf16[512,256]{1,0:T(8,128)(2,1)} %bitcast.16, bf16[64,512]{1,0:T(8,128)(2,1)} %features.3, bf16[64,256]{1,0:T(8,128)(2,1)} %weight.3, f32[1,256]{1,0:T(1,128)} %bitcast.18), custom_call_target="tpu_custom_call" | custom-call | tf_op jit(solution)/shard_map/spread/pallas_call | solution.py:169
  3.7 21.5 %all_to_all.20.source = bf16[32,16,640]{2,1,0:T(8,128)(2,1)} all-to-all(bf16[32,16,640]{2,1,0:T(8,128)(2,1)} %spread.1), channel_id=1, replica_groups=mesh['dp'=2,'chan'=16,'ctx'=16] {'dp','ctx'}, dimensions={0} | all-to-all | bytes 1310720 | tf_op jit(solution)/shard_map/all_to_all | solution.py:511
  25.2 8.6 %spectral.1 = bf16[32,16,768]{2,1,0:T(8,128)(2,1)} custom-call(bf16[32,16,640]{2,1,0:T(8,128)(2,1)} %all_to_all.20.source, bf16[1024,512]{1,0:T(8,128)(2,1)} %constant.9.clone.table, f32[2,17,512]{2,1,0:T(8,128)} %constant.10.clone.forward, f32[2,17,512]{2,1,0:T(8,128)} %constant.11.clone.inverse, f32[1,256]{1,0:T(1,128)} %bitcast.19), custom_call_target="tpu_custom_call" | custom-call | tf_op jit(solution)/shard_map/spectral/pallas_call | solution.py:370
  33.9 19.7 %all_to_all.21.back = bf16[32,16,768]{2,1,0:T(8,128)(2,1)} all-to-all(bf16[32,16,768]{2,1,0:T(8,128)(2,1)} %spectral.1), channel_id=1, replica_groups=mesh['dp'=2,'chan'=16,'ctx'=16] {'dp','ctx'}, dimensions={0} | all-to-all | bytes 1572864 | tf_op jit(solution)/shard_map/all_to_all | solution.py:512
  53.5 2.7 %parts.1 = bf16[16,16,128]{2,1,0:T(8,128)(2,1)} custom-call(bf16[32,16,768]{2,1,0:T(8,128)(2,1)} %all_to_all.21.back, bf16[64,512]{1,0:T(8,128)(2,1)} %features.3, bf16[64,256]{1,0:T(8,128)(2,1)} %weight.3), custom_call_target="tpu_custom_call" | custom-call | tf_op jit(solution)/shard_map/parts/pallas_call | solution.py:419
  56.2 25.7 %all_to_all.22 = bf16[16,16,128]{2,1,0:T(8,128)(2,1)S(1)} all-to-all(bf16[16,16,128]{2,1,0:T(8,128)(2,1)} %parts.1), channel_id=1, replica_groups={{0,16,32,48,64,80,96,112,128,144,160,176,192,208,224,240},{1,17,33,49,6..., dimensions={0} | all-to-all | bytes 131072 | tf_op jit(solution)/shard_map/all_to_all | solution.py:518
  81.9 15.5 %all_to_all.23.own = bf16[16,16,128]{2,1,0:T(8,128)(2,1)S(1)} all-to-all(bf16[16,16,128]{2,1,0:T(8,128)(2,1)S(1)} %broadcast_in_dim.25), channel_id=1, replica_groups={{0,16,32,48,64,80,96,112,128,144,160,176,192,208,224,240},{1,17,33,49,6..., dimensions={0} | all-to-all | bytes 131072 | tf_op jit(solution)/shard_map/all_to_all | solution.py:518
  97.4 0.0 copy-start
  97.4 1.9 %collective-permute-start = (bf16[16,16,128]{2,1,0:T(8,128)(2,1)S(1)}, bf16[16,16,128]{2,1,0:T(8,128)(2,1)S(1)}, u32[]{:S(2)}, u32[]{:S(2)}) collective-permute-start(bf16[16,16,128]{2,1,0:T(8,128)(2,1)S(1)} %all_to_all.23.own), channel_id=1, source_target_pairs={{0,256},{256,0},{1,257},{257,1},{2,258},{258,2},{3,259},{259,3},{4... | collective-permute-start | bytes 196616 | tf_op jit(solution)/shard_map/ppermute | solution.py:524
  99.3 2.7 %final.1 = (bf16[512,256]{1,0:T(8,128)(2,1)}, bf16[512,256]{1,0:T(8,128)(2,1)}, bf16[512,256]{1,0:T(8,128)(2,1)}, bf16[512,256]{1,0:T(8,128)(2,1)}) custom-call(bf16[32,16,768]{2,1,0:T(8,128)(2,1)} %all_to_all.21.back, bf16[512,256]{1,0:T(8,128)(2,1)} %bitcast.11, bf16[512,256]{1,0:T(8,128)(2,1)} %bitcast.13, bf16[512,256]{1,0:T(8,128)(2,1)} %bitcast.15, ...), custom_call_target="tpu_custom_call" | custom-call | tf_op jit(solution)/shard_map/final/pallas_call | solution.py:484
  102.0 0.0 copy-done
  102.0 3.0 %collective-permute-done.other = bf16[16,16,128]{2,1,0:T(8,128)(2,1)S(1)} collective-permute-done((bf16[16,16,128]{2,1,0:T(8,128)(2,1)S(1)}, bf16[16,16,128]{2,1,0:T(8,128)(2,1)S(1)}, u32[]{:S(2)}, u32[]{:S(2)}) %collective-permute-start) | collective-permute-done | bytes 65568 | tf_op jit(solution)/shard_map/ppermute | solution.py:524
  105.1 0.0 copy-start.1
  105.1 0.6 copy-done.1
  105.7 1.6 %assemble.1 = (f32[64,512]{1,0:T(8,128)}, f32[64,256]{1,0:T(8,128)}) custom-call(bf16[16,16,128]{2,1,0:T(8,128)(2,1)} %copy-done, bf16[16,16,128]{2,1,0:T(8,128)(2,1)} %copy-done.1), custom_call_target="tpu_custom_call" | custom-call | tf_op jit(solution)/shard_map/assemble/pallas_call | solution.py:449
  (2 shorter events, 0.0 us)
Async XLA Ops:
  97.4 4.6 %copy-start = (bf16[16,16,128]{2,1,0:T(8,128)(2,1)}, bf16[16,16,128]{2,1,0:T(8,128)(2,1)S(1)}, u32[]{:S(2)}) copy-start(bf16[16,16,128]{2,1,0:T(8,128)(2,1)S(1)} %all_to_all.23.own) | copy-start | bytes 196612
  97.4 7.7 %collective-permute-start = (bf16[16,16,128]{2,1,0:T(8,128)(2,1)S(1)}, bf16[16,16,128]{2,1,0:T(8,128)(2,1)S(1)}, u32[]{:S(2)}, u32[]{:S(2)}) collective-permute-start(bf16[16,16,128]{2,1,0:T(8,128)(2,1)S(1)} %all_to_all.23.own), channel_id=1, source_target_pairs={{0,256},{256,0},{1,257},{257,1},{2,258},{258,2},{3,259},{259,3},{4... | collective-permute-start | bytes 196616 | tf_op jit(solution)/shard_map/ppermute | solution.py:524
  105.1 0.6 copy-start.1

commit v4 on v3

v4 whole, which is shorter than its diff:
```python
import functools
import math

import jax
import jax.numpy as jnp
import numpy as np
from jax import lax
from jax.experimental import pallas as pl
from jax.experimental.pallas import tpu as pltpu
from jax.sharding import PartitionSpec as P

LENGTH = 8192
PERIOD = 2 * LENGTH
TOK = 512
RADIX = 64
COLS = PERIOD // RADIX
BLOCKS = LENGTH // TOK
HALF = RADIX // 2 + 1
CH = 256
OWN = 8
GROUP = 32
ORDER = 64
TILE = 16
LANE = 128
CHUNKS = TOK // LANE
PAIRS = (HALF + 1) // 2
ROWS = 2 * HALF + PAIRS
VMEM_LIMIT = 24 * 1024 * 1024


def tables():
    grid = np.arange(COLS)
    angle = 2.0 * np.pi / COLS * (np.outer(grid, grid) % COLS)
    basis = np.concatenate([np.cos(angle), np.sin(angle)], axis=0).astype(jnp.bfloat16)
    turn = 2.0 * np.pi / PERIOD * np.outer(np.arange(HALF), grid)
    forward = np.stack([np.cos(turn), np.sin(turn)]).astype(np.float32)
    factor = 1.0 / (PERIOD * math.sqrt(LENGTH))
    inverse = (np.stack([np.cos(turn), np.sin(turn)]) * factor).astype(np.float32)
    return basis, forward, inverse


def add(a, b):
    if a is None:
        return b
    return a if b is None else a + b


def sub(a, b):
    if b is None:
        return a
    return -b if a is None else a - b


def neg(a):
    return None if a is None else -a


def rotate(value, index, period):
    real, imag = value
    if index == 0:
        return value
    if 4 * index == period:
        return imag, neg(real)
    c = math.cos(2 * math.pi * index / period)
    s = math.sin(2 * math.pi * index / period)
    if imag is None:
        return real * c, real * (-s)
    if 8 * index == period:
        return (real + imag) * c, (imag - real) * c
    return real * c + imag * s, imag * c - real * s


def rotate_back(value, index, period):
    real, imag = value
    if index == 0:
        return value
    if 4 * index == period:
        return neg(imag), real
    c = math.cos(2 * math.pi * index / period)
    s = math.sin(2 * math.pi * index / period)
    if 8 * index == period:
        return (real - imag) * c, (imag + real) * c
    return real * c - imag * s, imag * c + real * s


def real_dft(xs, n):
    if n == 2:
        return [(xs[0], None), (xs[0], None)]
    if n == 4:
        return [(xs[0] + xs[1], None), (xs[0], -xs[1]), (xs[0] - xs[1], None)]
    even = real_dft(xs[0::2], n // 2)
    odd = real_dft(xs[1::2], n // 2)
    out = [None] * (n // 2 + 1)
    for k in range(n // 4 + 1):
        t = rotate(odd[k], k, n)
        e = even[k]
        out[k] = (add(e[0], t[0]), add(e[1], t[1]))
        if 4 * k != n:
            out[n // 2 - k] = (sub(e[0], t[0]), sub(t[1], e[1]))
    return out


def real_inverse(spec, n):
    if n == 4:
        total = spec[0][0] + spec[2][0]
        diff = spec[0][0] - spec[2][0]
        return [total + 2.0 * spec[1][0], diff - 2.0 * spec[1][1]]
    even, odd = [], []
    for k in range(n // 4 + 1):
        a, b = spec[k], spec[n // 2 - k]
        if 4 * k == n:
            even.append((2.0 * a[0], None))
            odd.append((-2.0 * a[1], None))
            continue
        even.append((add(a[0], b[0]), sub(a[1], b[1])))
        odd.append(rotate_back((sub(a[0], b[0]), add(a[1], b[1])), k, n))
    first = real_inverse(even, n // 2)
    second = real_inverse(odd, n // 2)
    return [first[i // 2] if i % 2 == 0 else second[i // 2] for i in range(n // 2)]


def identity(size):
    row = lax.broadcasted_iota(jnp.int32, (size, size), 0)
    column = lax.broadcasted_iota(jnp.int32, (size, size), 1)
    return jnp.where(row == column, 1.0, 0.0).astype(jnp.bfloat16)


def turned_over(eye, block):
    return lax.dot_general(eye, block, (((1,), (1,)), ((), ())), preferred_element_type=jnp.float32)


def in_vmem(array):
    return pltpu.with_memory_space_constraint(array, pltpu.VMEM)


def in_hbm(array):
    return pltpu.with_memory_space_constraint(array, pltpu.HBM)


def spread_kernel(values, gate_first, gate_second, grad, features, weight, decay, ready):
    f32, bf16 = jnp.float32, jnp.bfloat16
    half = TOK // 2
    dp = lax.axis_index("dp")
    ctx = lax.axis_index("ctx")
    eye = identity(CH)
    mine = jnp.where(dp == 0, features[:, :half].astype(f32), features[:, half:].astype(f32))
    raw = lax.dot_general(
        mine.astype(bf16), weight[...], (((0,), (0,)), ((), ())), preferred_element_type=f32
    )
    first = ctx * TOK + dp * half
    positions = (first + lax.broadcasted_iota(jnp.int32, (half, 1), 0)).astype(f32) / LENGTH
    kernel = (raw * jnp.exp(-decay[...] * positions)).astype(bf16)
    kernel = turned_over(eye, kernel).reshape(GROUP, OWN, half)
    folded = jnp.concatenate([kernel[:, :, :LANE], kernel[:, :, LANE:]], axis=1)
    ready[:, CHUNKS * TILE :] = folded.astype(bf16)
    for part in range(2):
        rows = slice(part * half, (part + 1) * half)
        mixed = (values[rows].astype(f32) * gate_first[rows].astype(f32)).astype(bf16)
        scaled = (grad[rows].astype(f32) * gate_second[rows].astype(f32)).astype(bf16)
        mixed = turned_over(eye, mixed).reshape(GROUP, OWN, half)
        scaled = turned_over(eye, scaled).reshape(GROUP, OWN, half)
        both = jnp.concatenate([mixed, scaled], axis=1).astype(bf16)
        for c in range(2):
            row = (2 * part + c) * TILE
            ready[:, row : row + TILE] = both[:, :, c * LANE : (c + 1) * LANE]


def spread(values, gate_first, gate_second, grad, features, weight, decay, **kw):
    return pl.pallas_call(
        spread_kernel,
        out_shape=pltpu.VMEM((GROUP, (CHUNKS + 1) * TILE, LANE), jnp.bfloat16),
        in_specs=[pl.BlockSpec(memory_space=pltpu.VMEM)] * 7,
        out_specs=pl.BlockSpec(memory_space=pltpu.VMEM),
        compiler_params=pltpu.CompilerParams(vmem_limit_bytes=VMEM_LIMIT),
        name="spread",
        **kw,
    )(*(in_hbm(a) for a in (values, gate_first, gate_second, grad, features, weight, decay)))


def spectral_kernel(
    got, basis, forward, inverse, decay, out, lhs_re, lhs_im, res_re, res_im, rates
):
    f32, bf16 = jnp.float32, jnp.bfloat16
    rates[...] = jnp.broadcast_to(decay[...], (LANE, CH)).T
    first = (lax.axis_index("dp") * BLOCKS + lax.axis_index("ctx")) * OWN

    def lanes_of(chunk):
        return pl.ds(pl.multiple_of(chunk * LANE, LANE), LANE)

    def tile_of(chunk):
        return pl.ds(pl.multiple_of(chunk * TILE, TILE), TILE)

    def transformed(xs, lanes):
        turned = []
        for k, (real, imag) in enumerate(real_dft(xs, RADIX)):
            if k == 0:
                turned.append((real, jnp.zeros_like(real)))
                continue
            c = forward[0, k : k + 1, lanes]
            s = forward[1, k : k + 1, lanes]
            if imag is None:
                turned.append((real * c, -(real * s)))
            else:
                turned.append((real * c + imag * s, imag * c - real * s))
        return turned

    def joined(a, b):
        return jnp.concatenate([a, b], axis=0).astype(bf16)

    def signals_in(s, chunk):
        lanes = lanes_of(chunk)
        xs = [
            got[s * BLOCKS + j, tile_of(2 * h + chunk)].astype(f32)
            for j in range(BLOCKS)
            for h in range(2)
        ]
        low = transformed([x[:OWN] for x in xs], lanes)
        high = transformed([x[OWN:] for x in xs], lanes)
        for k in range(HALF):
            lhs_re[2 * k + s, :, lanes] = joined(low[k][0], high[k][0])
            lhs_im[2 * k + s, :, lanes] = joined(low[k][1], high[k][1])

    def sequence_in(s, carry):
        def chunk_in(chunk, inner):
            signals_in(s, chunk)
            return inner

        return lax.fori_loop(0, 2, chunk_in, carry)

    lax.fori_loop(0, 2, sequence_in, 0)

    blocks = [got[s * BLOCKS + j, CHUNKS * TILE :].astype(f32) for j in range(BLOCKS) for s in range(2)]
    for chunk in range(2):
        lanes = pl.ds(chunk * LANE, LANE)
        spec = transformed([x[chunk * OWN : (chunk + 1) * OWN] for x in blocks], lanes)
        spec.append((jnp.zeros_like(spec[0][0]),) * 2)
        for p in range(PAIRS):
            a, b = spec[2 * p], spec[2 * p + 1]
            lhs_re[2 * HALF + p, :, lanes] = joined(a[0], b[0])
            lhs_im[2 * HALF + p, :, lanes] = joined(a[1], b[1])

    def product(first, second):
        lhs = jnp.concatenate([first, second], axis=1)
        res = jnp.dot(lhs, basis[...], preferred_element_type=f32)
        return res.reshape(ROWS, TILE, COLS)

    real = lhs_re[...].reshape(ROWS * TILE, COLS)
    imag = lhs_im[...].reshape(ROWS * TILE, COLS)
    res_re[...] = product(real, imag)
    res_im[...] = product(imag, -real)

    def multiply(k, pair, rows):
        hr = res_re[2 * HALF + pair, rows, :]
        hi = res_im[2 * HALF + pair, rows, :]
        total_re, total_im = None, None
        for s in range(2):
            zr = res_re[2 * k + s, :OWN, :]
            zi = res_im[2 * k + s, :OWN, :]
            gr = res_re[2 * k + s, OWN:, :]
            gi = res_im[2 * k + s, OWN:, :]
            lhs_re[2 * k + s] = joined(zr * hr - zi * hi, gr * hr + gi * hi)
            lhs_im[2 * k + s] = joined(zr * hi + zi * hr, gi * hr - gr * hi)
            total_re = add(total_re, gr * zr + gi * zi)
            total_im = add(total_im, gi * zr - gr * zi)
        return total_re, total_im

    def multiply_pair(pair, carry):
        a = multiply(2 * pair, pair, slice(0, OWN))
        b = multiply(2 * pair + 1, pair, slice(OWN, TILE))
        lhs_re[2 * HALF + pair] = joined(a[0], b[0])
        lhs_im[2 * HALF + pair] = joined(a[1], b[1])
        return carry

    lax.fori_loop(0, PAIRS - 1, multiply_pair, 0, unroll=4)
    last = PAIRS - 1
    a = multiply(2 * last, last, slice(0, OWN))
    blank = jnp.zeros_like(a[0])
    lhs_re[2 * HALF + last] = joined(a[0], blank)
    lhs_im[2 * HALF + last] = joined(a[1], blank)

    real = lhs_re[...].reshape(ROWS * TILE, COLS)
    imag = lhs_im[...].reshape(ROWS * TILE, COLS)
    res_re[...] = product(real, -imag)
    res_im[...] = product(imag, real)

    def returned(spec, lanes):
        turned = []
        for k, (real, imag) in enumerate(spec):
            c = inverse[0, k : k + 1, lanes]
            s = inverse[1, k : k + 1, lanes]
            if k in (0, HALF - 1):
                turned.append((real * c - imag * s, None))
            else:
                turned.append((real * c - imag * s, imag * c + real * s))
        return real_inverse(turned, RADIX)

    rate = rates[pl.ds(pl.multiple_of(first, OWN), OWN), :]
    steps = [jnp.exp(-rate * (COLS * n / LENGTH)) for n in range(RADIX // 2)]
    ahead = lax.broadcasted_iota(jnp.int32, (OWN, LANE), 1).astype(f32)

    for chunk in range(2):
        lanes = pl.ds(chunk * LANE, LANE)
        spec = []
        for k in range(HALF):
            rows = slice(k % 2 * OWN, k % 2 * OWN + OWN)
            block = 2 * HALF + k // 2
            spec.append((res_re[block, rows, lanes], res_im[block, rows, lanes]))
        fine = jnp.exp(-rate * ((ahead + chunk * LANE) / LENGTH))
        pieces = [y * (fine * steps[n]) for n, y in enumerate(returned(spec, lanes))]
        row = (CHUNKS + chunk) * TILE
        for j in range(BLOCKS):
            both = joined(pieces[2 * j], pieces[2 * j + 1])
            out[j, row : row + TILE] = both
            out[BLOCKS + j, row : row + TILE] = both

    def sequence_out(s, carry):
        def chunk_out(chunk, inner):
            lanes = lanes_of(chunk)
            halves = []
            for rows in (slice(0, OWN), slice(OWN, TILE)):
                spec = [
                    (res_re[2 * k + s, rows, lanes], res_im[2 * k + s, rows, lanes]) for k in range(HALF)
                ]
                halves.append(returned(spec, lanes))
            for n in range(RADIX // 2):
                out[s * BLOCKS + n // 2, tile_of(n % 2 * 2 + chunk)] = joined(halves[0][n], halves[1][n])
            return inner

        lax.fori_loop(0, 2, chunk_out, 0)
        return carry

    lax.fori_loop(0, 2, sequence_out, 0)


def spectral(got, decay, **kw):
    basis, forward, inverse = (in_vmem(jnp.asarray(table)) for table in tables())
    wide = pltpu.VMEM((ROWS, TILE, COLS), jnp.bfloat16)
    result = pltpu.VMEM((ROWS, TILE, COLS), jnp.float32)
    return pl.pallas_call(
        spectral_kernel,
        out_shape=pltpu.VMEM((GROUP, (CHUNKS + 2) * TILE, LANE), jnp.bfloat16),
        in_specs=[pl.BlockSpec(memory_space=pltpu.VMEM)] * 5,
        out_specs=pl.BlockSpec(memory_space=pltpu.VMEM),
        scratch_shapes=[wide, wide, result, result, pltpu.VMEM((CH, LANE), jnp.float32)],
        compiler_params=pltpu.CompilerParams(vmem_limit_bytes=VMEM_LIMIT),
        name="spectral",
        **kw,
    )(in_vmem(got), basis, forward, inverse, in_vmem(decay))


def parts_kernel(back, features, weight, sums):
    f32, bf16 = jnp.float32, jnp.bfloat16
    half = TOK // 2
    first = CHUNKS * TILE
    is_feature = lax.axis_index("dp") == 0
    alongs, weight_sum = [], None
    for h in range(2):
        pieces = []
        for c in range(2):
            piece = back[:, first + c * TILE : first + (c + 1) * TILE].astype(f32)[:, h * OWN : (h + 1) * OWN]
            pieces.append(piece.reshape(CH, LANE))
        kernel_grad = jnp.concatenate(pieces, axis=1).astype(bf16)
        alongs.append(jnp.dot(weight[...], kernel_grad, preferred_element_type=f32))
        share = lax.dot_general(
            features[:, half * h : half * (h + 1)],
            kernel_grad,
            (((1,), (1,)), ((), ())),
            preferred_element_type=f32,
        )
        weight_sum = add(weight_sum, share)
    blank = jnp.zeros((8, LANE), f32)
    for piece in range(16):
        r, c = piece // 4, piece % 4
        feature = alongs[c // 2][16 * r : 16 * (r + 1), LANE * (c % 2) : LANE * (c % 2 + 1)]
        r, c = piece // 2, piece % 2
        other = weight_sum[8 * r : 8 * (r + 1), LANE * c : LANE * (c + 1)]
        other = jnp.concatenate([other, blank], axis=0)
        sums[piece] = jnp.where(is_feature, feature, other).astype(bf16)


def parts(back, features, weight, **kw):
    return pl.pallas_call(
        parts_kernel,
        out_shape=pltpu.VMEM((16, TILE, LANE), jnp.bfloat16),
        in_specs=[pl.BlockSpec(memory_space=pltpu.VMEM)] * 3,
        out_specs=pl.BlockSpec(memory_space=pltpu.VMEM),
        compiler_params=pltpu.CompilerParams(vmem_limit_bytes=VMEM_LIMIT),
        name="parts",
        **kw,
    )(in_vmem(back), in_vmem(features), in_vmem(weight))


def assemble_kernel(own, other, feature_grad, weight_grad):
    f32 = jnp.float32
    is_feature = lax.axis_index("dp") == 0
    for piece in range(16):
        a = own[piece].astype(f32)
        b = other[piece].astype(f32)
        feature = jnp.where(is_feature, a, b)
        weight = jnp.where(is_feature, b, a)[:8]
        r, c = piece // 4, piece % 4
        feature_grad[16 * r : 16 * (r + 1), 128 * c : 128 * (c + 1)] = feature
        r, c = piece // 2, piece % 2
        weight_grad[8 * r : 8 * (r + 1), 128 * c : 128 * (c + 1)] = weight


def assemble(own, other, **kw):
    return pl.pallas_call(
        assemble_kernel,
        out_shape=(
            jax.ShapeDtypeStruct((ORDER, TOK), jnp.float32),
            jax.ShapeDtypeStruct((ORDER, CH), jnp.float32),
        ),
        in_specs=[pl.BlockSpec(memory_space=pltpu.VMEM)] * 2,
        out_specs=(pl.BlockSpec(memory_space=pltpu.VMEM),) * 2,
        name="assemble",
        **kw,
    )(in_vmem(own), in_vmem(other))


def final_kernel(
    back, values, gate_first, gate_second, grad, skip, output, values_grad, first_grad, second_grad
):
    f32, bf16 = jnp.float32, jnp.bfloat16
    eye = identity(LANE)
    bias = skip[...]
    for chunk in range(CHUNKS):
        both = back[:, chunk * TILE : (chunk + 1) * TILE].astype(f32)
        conv = turned_over(eye, both[:, :OWN].reshape(CH, LANE).astype(bf16))
        grad_conv = turned_over(eye, both[:, OWN:].reshape(CH, LANE).astype(bf16))
        rows = slice(chunk * LANE, (chunk + 1) * LANE)
        x = values[rows].astype(f32)
        g1 = gate_first[rows].astype(f32)
        g2 = gate_second[rows].astype(f32)
        dy = grad[rows].astype(f32)
        total = conv + bias * (x * g1).astype(bf16).astype(f32)
        output[rows] = (g2 * total).astype(bf16)
        second_grad[rows] = (dy * total).astype(bf16)
        delta = grad_conv + bias * (dy * g2).astype(bf16).astype(f32)
        values_grad[rows] = (delta * g1).astype(bf16)
        first_grad[rows] = (delta * x).astype(bf16)


def final(back, values, gate_first, gate_second, grad, skip, **kw):
    shape = jax.ShapeDtypeStruct((TOK, CH), jnp.bfloat16)
    return pl.pallas_call(
        final_kernel,
        out_shape=(shape,) * 4,
        in_specs=[pl.BlockSpec(memory_space=pltpu.VMEM)] * 6,
        out_specs=(pl.BlockSpec(memory_space=pltpu.VMEM),) * 4,
        compiler_params=pltpu.CompilerParams(vmem_limit_bytes=VMEM_LIMIT),
        name="final",
        **kw,
    )(*(in_vmem(a) for a in (back, values, gate_first, gate_second, grad, skip)))


def local(
    values,
    gate_first,
    gate_second,
    filter_features,
    filter_weight,
    decay_rate,
    skip_bias,
    output_grad,
):
    values, gate_first, gate_second, output_grad = (
        a[0] for a in (values, gate_first, gate_second, output_grad)
    )
    group = ("dp", "ctx")
    decay = decay_rate[None, :]
    sent = spread(values, gate_first, gate_second, output_grad, filter_features, filter_weight, decay)
    got = lax.all_to_all(sent, group, 0, 0, tiled=True)
    back = lax.all_to_all(spectral(got, decay), group, 0, 0, tiled=True)
    everywhere = ("dp", "chan", "ctx")
    groups = [[16 * z + j for z in range(16)] for j in range(16)]
    groups += [[256 + 16 * z + j for j in range(16)] for z in range(16)]

    def exchange(pieces):
        return lax.all_to_all(pieces, everywhere, 0, 0, axis_index_groups=groups, tiled=True)

    pieces = exchange(parts(back, filter_features, filter_weight))
    summed = jnp.sum(pieces.astype(jnp.float32), axis=0).astype(jnp.bfloat16)
    copies = exchange(jnp.broadcast_to(summed[None], (16, 16, 128)))
    back, copies = lax.optimization_barrier((back, copies))
    other = lax.ppermute(copies, "dp", [(0, 1), (1, 0)])
    outs = final(back, values, gate_first, gate_second, output_grad, skip_bias[None, :])
    feature_grad, weight_grad = assemble(copies, other)
    output, values_grad, first_grad, second_grad = (a[None] for a in outs)
    return (output, values_grad, first_grad, second_grad, weight_grad, feature_grad)


def solution(mesh):
    in_specs = (
        P("dp", "ctx", "chan"),
        P("dp", "ctx", "chan"),
        P("dp", "ctx", "chan"),
        P(None, "ctx"),
        P(None, "chan"),
        P("chan"),
        P("chan"),
        P("dp", "ctx", "chan"),
    )
    out_specs = (
        P("dp", "ctx", "chan"),
        P("dp", "ctx", "chan"),
        P("dp", "ctx", "chan"),
        P("dp", "ctx", "chan"),
        P(None, "chan"),
        P(None, "ctx"),
    )
    return jax.shard_map(local, mesh=mesh, in_specs=in_specs, out_specs=out_specs, check_vma=False)
```

time: 109 us -> 98.6 us (0.905)
  Pallas kernels: 18.7 us -> 8.87 us
  blocking collectives: 82.3 us -> 80.9 us
  waiting for transfers between devices: 3.02 us -> 4.23 us
    pallas_call x3, Pallas kernels: 14.4 us -> 6.71 us  [the longest x1 4.72 us: spectral(): pl.pallas_call(spectral_kernel, out_shape=pltpu.VMEM((GROUP, (CHUNKS + 2)...]
    all_to_all x1, blocking collectives: 21.5 us -> 20 us  [local(): got = lax.all_to_all(sent, group, 0, 0, tiled=True)]
    pallas_call x1, Pallas kernels: 2.71 us -> 1.46 us  [final(): pl.pallas_call(final_kernel, out_shape=(shape,) * 4, in_specs=[pl.BlockSp...]
    all_to_all x2, blocking collectives: 41.1 us -> 42.4 us  [exchange(): lax.all_to_all(pieces, everywhere, 0, 0, axis_index_groups=groups, tiled=...]
    all_to_all x1, blocking collectives: 19.7 us -> 18.5 us  [local(): back = lax.all_to_all(spectral(got, decay), group, 0, 0, tiled=True)]
    ppermute x1, waiting for transfers between devices: 3.02 us -> 4.23 us  [local(): other = lax.ppermute(copies, 'dp', [(0, 1), (1, 0)])]
  transfers between devices with their start and end apart: 1 -> 1, of which waited for: 1 -> 1; matrix products, arithmetic and copies ran while one was open for 0% -> 0% of each run, Pallas kernels for 3% -> 2%
where the time goes in v4:
time: 98.6 us; the launch traced here: 96.9 us
  blocking collectives  80.9 us (82%)
  Pallas kernels  8.87 us (9%)
  waiting for transfers between devices  4.23 us (4%)
  starting transfers between devices  2.04 us (2%)
    all_to_all x2, blocking collectives, exchange(): lax.all_to_all(pieces, everywhere, 0, 0, axis_index_groups=groups, tiled=...  42.4 us
    all_to_all x1, blocking collectives, local(): got = lax.all_to_all(sent, group, 0, 0, tiled=True)  20 us
    all_to_all x1, blocking collectives, local(): back = lax.all_to_all(spectral(got, decay), group, 0, 0, tiled=True)  18.5 us
    pallas_call x1, Pallas kernels, spectral(): pl.pallas_call(spectral_kernel, out_shape=pltpu.VMEM((GROUP, (CHUNKS + 2)...  4.72 us
    ppermute x1, waiting for transfers between devices, local(): other = lax.ppermute(copies, 'dp', [(0, 1), (1, 0)])  4.23 us
    ppermute x1, starting transfers between devices, local(): other = lax.ppermute(copies, 'dp', [(0, 1), (1, 0)])  2.04 us
  transfers between devices with their start and end apart: 1, of which 1 were waited for; matrix products, arithmetic and copies ran while one was open for 0% of the time, Pallas kernels for 2%

profile of v4, /device:TPU:6, one launch (start us, length us, event | category | flops | bytes accessed | tf_op | source)
XLA Modules:
  0.0 96.9 jit_solution(3487934349403550812)
XLA Ops:
  0.6 1.8 %spread.1 = bf16[32,80,128]{2,1,0:T(8,128)(2,1)S(1)} custom-call(bf16[512,256]{1,0:T(8,128)(2,1)} %bitcast.10, bf16[512,256]{1,0:T(8,128)(2,1)} %bitcast.12, bf16[512,256]{1,0:T(8,128)(2,1)} %bitcast.14, bf16[512,256]{1,0:T(8,128)(2,1)} %bitcast.16, bf16[64,512]{1,0:T(8,128)(2,1)} %features.3, bf16[64,256]{1,0:T(8,128)(2,1)} %weight.3, f32[1,256]{1,0:T(1,128)} %bitcast.18), custom_call_target="tpu_custom_call" | custom-call | tf_op jit(solution)/shard_map/spread/pallas_call | solution.py:169
  2.4 0.0 copy-start.4
  2.4 0.0 copy-start.7
  2.4 0.0 copy-start.8
  2.4 0.0 copy-start.9
  2.4 20.0 %all_to_all.20.got = bf16[32,80,128]{2,1,0:T(8,128)(2,1)S(1)} all-to-all(bf16[32,80,128]{2,1,0:T(8,128)(2,1)S(1)} %spread.1), channel_id=1, replica_groups=mesh['dp'=2,'chan'=16,'ctx'=16] {'dp','ctx'}, dimensions={0} | all-to-all | bytes 1310720 | tf_op jit(solution)/shard_map/all_to_all | solution.py:473
  22.5 0.0 copy-done.4
  22.5 0.0 copy-done.7
  22.5 0.0 copy-done.8
  22.5 0.0 copy-done.9
  22.5 4.7 %spectral.1 = bf16[32,96,128]{2,1,0:T(8,128)(2,1)S(1)} custom-call(bf16[32,80,128]{2,1,0:T(8,128)(2,1)S(1)} %all_to_all.20.got, bf16[512,256]{1,0:T(8,128)(2,1)S(1)} %copy-done.4, f32[2,33,256]{2,1,0:T(8,128)S(1)} %copy-done.7, f32[2,33,256]{2,1,0:T(8,128)S(1)} %copy-done.8, f32[1,256]{1,0:T(1,128)S(1)} %bitcast.19), custom_call_target="tpu_custom_call" | custom-call | tf_op jit(solution)/shard_map/spectral/pallas_call | solution.py:339
  27.2 0.0 copy-start.5
  27.2 0.0 copy-start.6
  27.2 18.5 %all_to_all.21.back = bf16[32,96,128]{2,1,0:T(8,128)(2,1)S(1)} all-to-all(bf16[32,96,128]{2,1,0:T(8,128)(2,1)S(1)} %spectral.1), channel_id=1, replica_groups=mesh['dp'=2,'chan'=16,'ctx'=16] {'dp','ctx'}, dimensions={0} | all-to-all | bytes 1572864 | tf_op jit(solution)/shard_map/all_to_all | solution.py:474
  45.7 0.0 copy-done.5
  45.7 0.0 copy-done.6
  45.7 0.0 copy-start.1
  45.7 0.0 copy-start.2
  45.7 0.0 copy-start.3
  45.7 0.2 parts.1
  46.0 0.0 copy-start
  46.0 26.9 %all_to_all.22 = bf16[16,16,128]{2,1,0:T(8,128)(2,1)S(1)} all-to-all(bf16[16,16,128]{2,1,0:T(8,128)(2,1)S(1)} %parts.1), channel_id=1, replica_groups={{0,16,32,48,64,80,96,112,128,144,160,176,192,208,224,240},{1,17,33,49,6..., dimensions={0} | all-to-all | bytes 131072 | tf_op jit(solution)/shard_map/all_to_all | solution.py:480
  72.9 15.5 %all_to_all.23.own = bf16[16,16,128]{2,1,0:T(8,128)(2,1)S(1)} all-to-all(bf16[16,16,128]{2,1,0:T(8,128)(2,1)S(1)} %broadcast_in_dim.25), channel_id=1, replica_groups={{0,16,32,48,64,80,96,112,128,144,160,176,192,208,224,240},{1,17,33,49,6..., dimensions={0} | all-to-all | bytes 131072 | tf_op jit(solution)/shard_map/all_to_all | solution.py:480
  88.4 0.0 copy-start.10
  88.4 2.0 %collective-permute-start = (bf16[16,16,128]{2,1,0:T(8,128)(2,1)S(1)}, bf16[16,16,128]{2,1,0:T(8,128)(2,1)S(1)}, u32[]{:S(2)}, u32[]{:S(2)}) collective-permute-start(bf16[16,16,128]{2,1,0:T(8,128)(2,1)S(1)} %all_to_all.23.own), channel_id=1, source_target_pairs={{0,256},{256,0},{1,257},{257,1},{2,258},{258,2},{3,259},{259,3},{4... | collective-permute-start | bytes 196616 | tf_op jit(solution)/shard_map/ppermute | solution.py:486
  90.5 0.0 copy-done.1
  90.5 0.0 copy-done.2
  90.5 0.0 copy-done.3
  90.5 0.0 copy-done
  90.5 0.0 copy-done.10
  90.5 1.5 %final.1 = (bf16[512,256]{1,0:T(8,128)(2,1)}, bf16[512,256]{1,0:T(8,128)(2,1)}, bf16[512,256]{1,0:T(8,128)(2,1)}, bf16[512,256]{1,0:T(8,128)(2,1)}) custom-call(bf16[32,96,128]{2,1,0:T(8,128)(2,1)S(1)} %all_to_all.21.back, bf16[512,256]{1,0:T(8,128)(2,1)S(1)} %bitcast.11, bf16[512,256]{1,0:T(8,128)(2,1)S(1)} %bitcast.13, bf16[512,256]{1,0:T(8,128)(2,1)S(1)} %bitcast.15, ...), custom_call_target="tpu_custom_call" | custom-call | tf_op jit(solution)/shard_map/final/pallas_call | solution.py:446
  92.0 4.2 %collective-permute-done.other = bf16[16,16,128]{2,1,0:T(8,128)(2,1)S(1)} collective-permute-done((bf16[16,16,128]{2,1,0:T(8,128)(2,1)S(1)}, bf16[16,16,128]{2,1,0:T(8,128)(2,1)S(1)}, u32[]{:S(2)}, u32[]{:S(2)}) %collective-permute-start) | collective-permute-done | bytes 65568 | tf_op jit(solution)/shard_map/ppermute | solution.py:486
  96.2 0.7 assemble.1
  (2 shorter events, 0.0 us)
Async XLA Ops:
  2.4 20.1 %copy-start.4 = (bf16[512,256]{1,0:T(8,128)(2,1)S(1)}, bf16[512,256]{1,0:T(8,128)(2,1)}, u32[]{:S(2)}) copy-start(bf16[512,256]{1,0:T(8,128)(2,1)} %constant.9.clone.basis) | copy-start | bytes 786436
  2.4 20.1 %copy-start.7 = (f32[2,33,256]{2,1,0:T(8,128)S(1)}, f32[2,33,256]{2,1,0:T(8,128)}, u32[]{:S(2)}) copy-start(f32[2,33,256]{2,1,0:T(8,128)} %constant.10.clone.forward) | copy-start | bytes 202756
  2.4 20.1 %copy-start.8 = (f32[2,33,256]{2,1,0:T(8,128)S(1)}, f32[2,33,256]{2,1,0:T(8,128)}, u32[]{:S(2)}) copy-start(f32[2,33,256]{2,1,0:T(8,128)} %constant.11.clone.inverse) | copy-start | bytes 202756
  2.4 20.0 %copy-start.9 = (f32[256]{0:T(256)S(1)}, f32[256]{0:T(256)}, u32[]{:S(2)}) copy-start(f32[256]{0:T(256)} %param.16) | copy-start | bytes 3076
  27.2 18.5 %copy-start.5 = (bf16[64,512]{1,0:T(8,128)(2,1)S(1)}, bf16[64,512]{1,0:T(8,128)(2,1)}, u32[]{:S(2)}) copy-start(bf16[64,512]{1,0:T(8,128)(2,1)} %features.3) | copy-start | bytes 196612
  27.2 18.5 %copy-start.6 = (bf16[64,256]{1,0:T(8,128)(2,1)S(1)}, bf16[64,256]{1,0:T(8,128)(2,1)}, u32[]{:S(2)}) copy-start(bf16[64,256]{1,0:T(8,128)(2,1)} %weight.3) | copy-start | bytes 98308
  45.7 44.7 %copy-start.1 = (bf16[1,512,256]{2,1,0:T(8,128)(2,1)S(1)}, bf16[1,512,256]{2,1,0:T(8,128)(2,1)}, u32[]{:S(2)}) copy-start(bf16[1,512,256]{2,1,0:T(8,128)(2,1)} %param.12) | copy-start | bytes 786436
  45.7 44.8 %copy-start.2 = (bf16[1,512,256]{2,1,0:T(8,128)(2,1)S(1)}, bf16[1,512,256]{2,1,0:T(8,128)(2,1)}, u32[]{:S(2)}) copy-start(bf16[1,512,256]{2,1,0:T(8,128)(2,1)} %param.13) | copy-start | bytes 786436
  45.7 44.8 %copy-start.3 = (bf16[1,512,256]{2,1,0:T(8,128)(2,1)S(1)}, bf16[1,512,256]{2,1,0:T(8,128)(2,1)}, u32[]{:S(2)}) copy-start(bf16[1,512,256]{2,1,0:T(8,128)(2,1)} %param.18) | copy-start | bytes 786436
  46.0 44.5 %copy-start = (bf16[1,512,256]{2,1,0:T(8,128)(2,1)S(1)}, bf16[1,512,256]{2,1,0:T(8,128)(2,1)}, u32[]{:S(2)}) copy-start(bf16[1,512,256]{2,1,0:T(8,128)(2,1)} %param.11) | copy-start | bytes 786436
  88.4 2.1 %copy-start.10 = (f32[256]{0:T(256)S(1)}, f32[256]{0:T(256)}, u32[]{:S(2)}) copy-start(f32[256]{0:T(256)} %param.17) | copy-start | bytes 3076
  88.4 7.8 %collective-permute-start = (bf16[16,16,128]{2,1,0:T(8,128)(2,1)S(1)}, bf16[16,16,128]{2,1,0:T(8,128)(2,1)S(1)}, u32[]{:S(2)}, u32[]{:S(2)}) collective-permute-start(bf16[16,16,128]{2,1,0:T(8,128)(2,1)S(1)} %all_to_all.23.own), channel_id=1, source_target_pairs={{0,256},{256,0},{1,257},{257,1},{2,258},{258,2},{3,259},{259,3},{4... | collective-permute-start | bytes 196616 | tf_op jit(solution)/shard_map/ppermute | solution.py:486

commit v5 on v4

--- a/solution.py
+++ b/solution.py
@@ -184,12 +184,6 @@
     rates[...] = jnp.broadcast_to(decay[...], (LANE, CH)).T
     first = (lax.axis_index("dp") * BLOCKS + lax.axis_index("ctx")) * OWN
 
-    def lanes_of(chunk):
-        return pl.ds(pl.multiple_of(chunk * LANE, LANE), LANE)
-
-    def tile_of(chunk):
-        return pl.ds(pl.multiple_of(chunk * TILE, TILE), TILE)
-
     def transformed(xs, lanes):
         turned = []
         for k, (real, imag) in enumerate(real_dft(xs, RADIX)):
@@ -207,32 +201,30 @@
     def joined(a, b):
         return jnp.concatenate([a, b], axis=0).astype(bf16)
 
+    def place(s):
+        return slice(s * HALF, (s + 1) * HALF)
+
     def signals_in(s, chunk):
-        lanes = lanes_of(chunk)
+        lanes = slice(chunk * LANE, (chunk + 1) * LANE)
         xs = [
-            got[s * BLOCKS + j, tile_of(2 * h + chunk)].astype(f32)
+            got[s * BLOCKS + j, (2 * h + chunk) * TILE : (2 * h + chunk + 1) * TILE].astype(f32)
             for j in range(BLOCKS)
             for h in range(2)
         ]
         low = transformed([x[:OWN] for x in xs], lanes)
         high = transformed([x[OWN:] for x in xs], lanes)
         for k in range(HALF):
-            lhs_re[2 * k + s, :, lanes] = joined(low[k][0], high[k][0])
-            lhs_im[2 * k + s, :, lanes] = joined(low[k][1], high[k][1])
-
-    def sequence_in(s, carry):
-        def chunk_in(chunk, inner):
-            signals_in(s, chunk)
-            return inner
-
-        return lax.fori_loop(0, 2, chunk_in, carry)
-
-    lax.fori_loop(0, 2, sequence_in, 0)
-
-    blocks = [got[s * BLOCKS + j, CHUNKS * TILE :].astype(f32) for j in range(BLOCKS) for s in range(2)]
-    for chunk in range(2):
-        lanes = pl.ds(chunk * LANE, LANE)
-        spec = transformed([x[chunk * OWN : (chunk + 1) * OWN] for x in blocks], lanes)
+            lhs_re[s * HALF + k, :, lanes] = joined(low[k][0], high[k][0])
+            lhs_im[s * HALF + k, :, lanes] = joined(low[k][1], high[k][1])
+
+    def kernel_in(chunk):
+        xs = [
+            got[s * BLOCKS + j, CHUNKS * TILE :].astype(f32)[chunk * OWN : (chunk + 1) * OWN]
+            for j in range(BLOCKS)
+            for s in range(2)
+        ]
+        lanes = slice(chunk * LANE, (chunk + 1) * LANE)
+        spec = transformed(xs, lanes)
         spec.append((jnp.zeros_like(spec[0][0]),) * 2)
         for p in range(PAIRS):
             a, b = spec[2 * p], spec[2 * p + 1]
@@ -240,48 +232,55 @@
             lhs_im[2 * HALF + p, :, lanes] = joined(a[1], b[1])
 
     def product(first, second):
-        lhs = jnp.concatenate([first, second], axis=1)
+        count = first.shape[0]
+        lhs = jnp.concatenate([first, second], axis=2).reshape(count * TILE, 2 * COLS)
         res = jnp.dot(lhs, basis[...], preferred_element_type=f32)
-        return res.reshape(ROWS, TILE, COLS)
-
-    real = lhs_re[...].reshape(ROWS * TILE, COLS)
-    imag = lhs_im[...].reshape(ROWS * TILE, COLS)
-    res_re[...] = product(real, imag)
-    res_im[...] = product(imag, -real)
-
-    def multiply(k, pair, rows):
+        return res.reshape(count, TILE, COLS)
+
+    def forth(tiles):
+        real, imag = lhs_re[tiles], lhs_im[tiles]
+        res_re[tiles] = product(real, imag)
+        res_im[tiles] = product(imag, -real)
+
+    def back(tiles):
+        real, imag = lhs_re[tiles], lhs_im[tiles]
+        res_re[tiles] = product(real, -imag)
+        res_im[tiles] = product(imag, real)
+
+    rest = slice(2 * HALF, ROWS)
+    kernel_in(0)
+    kernel_in(1)
+    forth(rest)
+    for s in range(2):
+        signals_in(s, 0)
+        signals_in(s, 1)
+        forth(place(s))
+
+    def multiply(k):
+        pair, rows = k // 2, slice(k % 2 * OWN, k % 2 * OWN + OWN)
         hr = res_re[2 * HALF + pair, rows, :]
         hi = res_im[2 * HALF + pair, rows, :]
         total_re, total_im = None, None
         for s in range(2):
-            zr = res_re[2 * k + s, :OWN, :]
-            zi = res_im[2 * k + s, :OWN, :]
-            gr = res_re[2 * k + s, OWN:, :]
-            gi = res_im[2 * k + s, OWN:, :]
-            lhs_re[2 * k + s] = joined(zr * hr - zi * hi, gr * hr + gi * hi)
-            lhs_im[2 * k + s] = joined(zr * hi + zi * hr, gi * hr - gr * hi)
+            tile = s * HALF + k
+            zr = res_re[tile, :OWN, :]
+            zi = res_im[tile, :OWN, :]
+            gr = res_re[tile, OWN:, :]
+            gi = res_im[tile, OWN:, :]
+            lhs_re[tile] = joined(zr * hr - zi * hi, gr * hr + gi * hi)
+            lhs_im[tile] = joined(zr * hi + zi * hr, gi * hr - gr * hi)
             total_re = add(total_re, gr * zr + gi * zi)
             total_im = add(total_im, gi * zr - gr * zi)
         return total_re, total_im
 
-    def multiply_pair(pair, carry):
-        a = multiply(2 * pair, pair, slice(0, OWN))
-        b = multiply(2 * pair + 1, pair, slice(OWN, TILE))
+    for pair in range(PAIRS):
+        a = multiply(2 * pair)
+        if 2 * pair + 1 < HALF:
+            b = multiply(2 * pair + 1)
+        else:
+            b = (jnp.zeros_like(a[0]),) * 2
         lhs_re[2 * HALF + pair] = joined(a[0], b[0])
         lhs_im[2 * HALF + pair] = joined(a[1], b[1])
-        return carry
-
-    lax.fori_loop(0, PAIRS - 1, multiply_pair, 0, unroll=4)
-    last = PAIRS - 1
-    a = multiply(2 * last, last, slice(0, OWN))
-    blank = jnp.zeros_like(a[0])
-    lhs_re[2 * HALF + last] = joined(a[0], blank)
-    lhs_im[2 * HALF + last] = joined(a[1], blank)
-
-    real = lhs_re[...].reshape(ROWS * TILE, COLS)
-    imag = lhs_im[...].reshape(ROWS * TILE, COLS)
-    res_re[...] = product(real, -imag)
-    res_im[...] = product(imag, real)
 
     def returned(spec, lanes):
         turned = []
@@ -298,13 +297,13 @@
     steps = [jnp.exp(-rate * (COLS * n / LENGTH)) for n in range(RADIX // 2)]
     ahead = lax.broadcasted_iota(jnp.int32, (OWN, LANE), 1).astype(f32)
 
-    for chunk in range(2):
-        lanes = pl.ds(chunk * LANE, LANE)
+    def filter_out(chunk):
+        lanes = slice(chunk * LANE, (chunk + 1) * LANE)
         spec = []
         for k in range(HALF):
             rows = slice(k % 2 * OWN, k % 2 * OWN + OWN)
-            block = 2 * HALF + k // 2
-            spec.append((res_re[block, rows, lanes], res_im[block, rows, lanes]))
+            tile = 2 * HALF + k // 2
+            spec.append((res_re[tile, rows, lanes], res_im[tile, rows, lanes]))
         fine = jnp.exp(-rate * ((ahead + chunk * LANE) / LENGTH))
         pieces = [y * (fine * steps[n]) for n, y in enumerate(returned(spec, lanes))]
         row = (CHUNKS + chunk) * TILE
@@ -313,23 +312,27 @@
             out[j, row : row + TILE] = both
             out[BLOCKS + j, row : row + TILE] = both
 
-    def sequence_out(s, carry):
-        def chunk_out(chunk, inner):
-            lanes = lanes_of(chunk)
-            halves = []
-            for rows in (slice(0, OWN), slice(OWN, TILE)):
-                spec = [
-                    (res_re[2 * k + s, rows, lanes], res_im[2 * k + s, rows, lanes]) for k in range(HALF)
-                ]
-                halves.append(returned(spec, lanes))
-            for n in range(RADIX // 2):
-                out[s * BLOCKS + n // 2, tile_of(n % 2 * 2 + chunk)] = joined(halves[0][n], halves[1][n])
-            return inner
-
-        lax.fori_loop(0, 2, chunk_out, 0)
-        return carry
-
-    lax.fori_loop(0, 2, sequence_out, 0)
+    def signals_out(s, chunk):
+        lanes = slice(chunk * LANE, (chunk + 1) * LANE)
+        halves = []
+        for rows in (slice(0, OWN), slice(OWN, TILE)):
+            spec = [
+                (res_re[s * HALF + k, rows, lanes], res_im[s * HALF + k, rows, lanes])
+                for k in range(HALF)
+            ]
+            halves.append(returned(spec, lanes))
+        for n in range(RADIX // 2):
+            row = (n % 2 * 2 + chunk) * TILE
+            out[s * BLOCKS + n // 2, row : row + TILE] = joined(halves[0][n], halves[1][n])
+
+    back(rest)
+    back(place(0))
+    filter_out(0)
+    filter_out(1)
+    back(place(1))
+    for s in range(2):
+        signals_out(s, 0)
+        signals_out(s, 1)
 
 
 def spectral(got, decay, **kw):

time: 98.6 us -> 97.6 us (0.990)
  Pallas kernels: 8.87 us -> 7.88 us
where the time goes in v5:
time: 97.6 us; the launch traced here: 95.9 us
  blocking collectives  80.9 us (83%)
  Pallas kernels  7.88 us (8%)
  waiting for transfers between devices  4.23 us (4%)
  starting transfers between devices  2.04 us (2%)
    all_to_all x2, blocking collectives, exchange(): lax.all_to_all(pieces, everywhere, 0, 0, axis_index_groups=groups, tiled=...  42.4 us
    all_to_all x1, blocking collectives, local(): got = lax.all_to_all(sent, group, 0, 0, tiled=True)  20 us
    all_to_all x1, blocking collectives, local(): back = lax.all_to_all(spectral(got, decay), group, 0, 0, tiled=True)  18.5 us
    ppermute x1, waiting for transfers between devices, local(): other = lax.ppermute(copies, 'dp', [(0, 1), (1, 0)])  4.23 us
    pallas_call x1, Pallas kernels, spectral(): pl.pallas_call(spectral_kernel, out_shape=pltpu.VMEM((GROUP, (CHUNKS + 2)...  3.74 us
    ppermute x1, starting transfers between devices, local(): other = lax.ppermute(copies, 'dp', [(0, 1), (1, 0)])  2.04 us
  transfers between devices with their start and end apart: 1, of which 1 were waited for; matrix products, arithmetic and copies ran while one was open for 0% of the time, Pallas kernels for 2%

profile of v5, /device:TPU:6, one launch (start us, length us, event | category | flops | bytes accessed | tf_op | source)
XLA Modules:
  0.0 95.9 jit_solution(11842312220194875775)
XLA Ops:
  0.6 1.8 %spread.1 = bf16[32,80,128]{2,1,0:T(8,128)(2,1)S(1)} custom-call(bf16[512,256]{1,0:T(8,128)(2,1)} %bitcast.10, bf16[512,256]{1,0:T(8,128)(2,1)} %bitcast.12, bf16[512,256]{1,0:T(8,128)(2,1)} %bitcast.14, bf16[512,256]{1,0:T(8,128)(2,1)} %bitcast.16, bf16[64,512]{1,0:T(8,128)(2,1)} %features.3, bf16[64,256]{1,0:T(8,128)(2,1)} %weight.3, f32[1,256]{1,0:T(1,128)} %bitcast.18), custom_call_target="tpu_custom_call" | custom-call | tf_op jit(solution)/shard_map/spread/pallas_call | solution.py:169
  2.4 0.0 copy-start.4
  2.4 0.0 copy-start.7
  2.4 0.0 copy-start.8
  2.4 0.0 copy-start.9
  2.4 20.0 %all_to_all.20.got = bf16[32,80,128]{2,1,0:T(8,128)(2,1)S(1)} all-to-all(bf16[32,80,128]{2,1,0:T(8,128)(2,1)S(1)} %spread.1), channel_id=1, replica_groups=mesh['dp'=2,'chan'=16,'ctx'=16] {'dp','ctx'}, dimensions={0} | all-to-all | bytes 1310720 | tf_op jit(solution)/shard_map/all_to_all | solution.py:476
  22.5 0.0 copy-done.4
  22.5 0.0 copy-done.7
  22.5 0.0 copy-done.8
  22.5 0.0 copy-done.9
  22.5 3.7 %spectral.1 = bf16[32,96,128]{2,1,0:T(8,128)(2,1)S(1)} custom-call(bf16[32,80,128]{2,1,0:T(8,128)(2,1)S(1)} %all_to_all.20.got, bf16[512,256]{1,0:T(8,128)(2,1)S(1)} %copy-done.4, f32[2,33,256]{2,1,0:T(8,128)S(1)} %copy-done.7, f32[2,33,256]{2,1,0:T(8,128)S(1)} %copy-done.8, f32[1,256]{1,0:T(1,128)S(1)} %bitcast.19), custom_call_target="tpu_custom_call" | custom-call | tf_op jit(solution)/shard_map/spectral/pallas_call | solution.py:342
  26.2 0.0 copy-start.5
  26.2 0.0 copy-start.6
  26.2 18.5 %all_to_all.21.back = bf16[32,96,128]{2,1,0:T(8,128)(2,1)S(1)} all-to-all(bf16[32,96,128]{2,1,0:T(8,128)(2,1)S(1)} %spectral.1), channel_id=1, replica_groups=mesh['dp'=2,'chan'=16,'ctx'=16] {'dp','ctx'}, dimensions={0} | all-to-all | bytes 1572864 | tf_op jit(solution)/shard_map/all_to_all | solution.py:477
  44.7 0.0 copy-done.5
  44.7 0.0 copy-done.6
  44.7 0.0 copy-start.1
  44.7 0.0 copy-start.2
  44.7 0.0 copy-start.3
  44.7 0.2 parts.1
  45.0 0.0 copy-start
  45.0 26.9 %all_to_all.22 = bf16[16,16,128]{2,1,0:T(8,128)(2,1)S(1)} all-to-all(bf16[16,16,128]{2,1,0:T(8,128)(2,1)S(1)} %parts.1), channel_id=1, replica_groups={{0,16,32,48,64,80,96,112,128,144,160,176,192,208,224,240},{1,17,33,49,6..., dimensions={0} | all-to-all | bytes 131072 | tf_op jit(solution)/shard_map/all_to_all | solution.py:483
  71.9 15.5 %all_to_all.23.own = bf16[16,16,128]{2,1,0:T(8,128)(2,1)S(1)} all-to-all(bf16[16,16,128]{2,1,0:T(8,128)(2,1)S(1)} %broadcast_in_dim.25), channel_id=1, replica_groups={{0,16,32,48,64,80,96,112,128,144,160,176,192,208,224,240},{1,17,33,49,6..., dimensions={0} | all-to-all | bytes 131072 | tf_op jit(solution)/shard_map/all_to_all | solution.py:483
  87.4 0.0 copy-start.10
  87.4 2.0 %collective-permute-start = (bf16[16,16,128]{2,1,0:T(8,128)(2,1)S(1)}, bf16[16,16,128]{2,1,0:T(8,128)(2,1)S(1)}, u32[]{:S(2)}, u32[]{:S(2)}) collective-permute-start(bf16[16,16,128]{2,1,0:T(8,128)(2,1)S(1)} %all_to_all.23.own), channel_id=1, source_target_pairs={{0,256},{256,0},{1,257},{257,1},{2,258},{258,2},{3,259},{259,3},{4... | collective-permute-start | bytes 196616 | tf_op jit(solution)/shard_map/ppermute | solution.py:489
  89.5 0.0 copy-done.1
  89.5 0.0 copy-done.2
  89.5 0.0 copy-done.3
  89.5 0.0 copy-done
  89.5 0.0 copy-done.10
  89.5 1.5 %final.1 = (bf16[512,256]{1,0:T(8,128)(2,1)}, bf16[512,256]{1,0:T(8,128)(2,1)}, bf16[512,256]{1,0:T(8,128)(2,1)}, bf16[512,256]{1,0:T(8,128)(2,1)}) custom-call(bf16[32,96,128]{2,1,0:T(8,128)(2,1)S(1)} %all_to_all.21.back, bf16[512,256]{1,0:T(8,128)(2,1)S(1)} %bitcast.11, bf16[512,256]{1,0:T(8,128)(2,1)S(1)} %bitcast.13, bf16[512,256]{1,0:T(8,128)(2,1)S(1)} %bitcast.15, ...), custom_call_target="tpu_custom_call" | custom-call | tf_op jit(solution)/shard_map/final/pallas_call | solution.py:449
  91.0 4.2 %collective-permute-done.other = bf16[16,16,128]{2,1,0:T(8,128)(2,1)S(1)} collective-permute-done((bf16[16,16,128]{2,1,0:T(8,128)(2,1)S(1)}, bf16[16,16,128]{2,1,0:T(8,128)(2,1)S(1)}, u32[]{:S(2)}, u32[]{:S(2)}) %collective-permute-start) | collective-permute-done | bytes 65568 | tf_op jit(solution)/shard_map/ppermute | solution.py:489
  95.2 0.7 assemble.1
  (2 shorter events, 0.0 us)
Async XLA Ops:
  2.4 20.1 %copy-start.4 = (bf16[512,256]{1,0:T(8,128)(2,1)S(1)}, bf16[512,256]{1,0:T(8,128)(2,1)}, u32[]{:S(2)}) copy-start(bf16[512,256]{1,0:T(8,128)(2,1)} %constant.9.clone.basis) | copy-start | bytes 786436
  2.4 20.1 %copy-start.7 = (f32[2,33,256]{2,1,0:T(8,128)S(1)}, f32[2,33,256]{2,1,0:T(8,128)}, u32[]{:S(2)}) copy-start(f32[2,33,256]{2,1,0:T(8,128)} %constant.10.clone.forward) | copy-start | bytes 202756
  2.4 20.1 %copy-start.8 = (f32[2,33,256]{2,1,0:T(8,128)S(1)}, f32[2,33,256]{2,1,0:T(8,128)}, u32[]{:S(2)}) copy-start(f32[2,33,256]{2,1,0:T(8,128)} %constant.11.clone.inverse) | copy-start | bytes 202756
  2.4 20.0 %copy-start.9 = (f32[256]{0:T(256)S(1)}, f32[256]{0:T(256)}, u32[]{:S(2)}) copy-start(f32[256]{0:T(256)} %param.16) | copy-start | bytes 3076
  26.2 18.5 %copy-start.5 = (bf16[64,512]{1,0:T(8,128)(2,1)S(1)}, bf16[64,512]{1,0:T(8,128)(2,1)}, u32[]{:S(2)}) copy-start(bf16[64,512]{1,0:T(8,128)(2,1)} %features.3) | copy-start | bytes 196612
  26.2 18.5 %copy-start.6 = (bf16[64,256]{1,0:T(8,128)(2,1)S(1)}, bf16[64,256]{1,0:T(8,128)(2,1)}, u32[]{:S(2)}) copy-start(bf16[64,256]{1,0:T(8,128)(2,1)} %weight.3) | copy-start | bytes 98308
  44.7 44.8 %copy-start.1 = (bf16[1,512,256]{2,1,0:T(8,128)(2,1)S(1)}, bf16[1,512,256]{2,1,0:T(8,128)(2,1)}, u32[]{:S(2)}) copy-start(bf16[1,512,256]{2,1,0:T(8,128)(2,1)} %param.12) | copy-start | bytes 786436
  44.7 44.8 %copy-start.2 = (bf16[1,512,256]{2,1,0:T(8,128)(2,1)S(1)}, bf16[1,512,256]{2,1,0:T(8,128)(2,1)}, u32[]{:S(2)}) copy-start(bf16[1,512,256]{2,1,0:T(8,128)(2,1)} %param.13) | copy-start | bytes 786436
  44.7 44.8 %copy-start.3 = (bf16[1,512,256]{2,1,0:T(8,128)(2,1)S(1)}, bf16[1,512,256]{2,1,0:T(8,128)(2,1)}, u32[]{:S(2)}) copy-start(bf16[1,512,256]{2,1,0:T(8,128)(2,1)} %param.18) | copy-start | bytes 786436
  45.0 44.5 %copy-start = (bf16[1,512,256]{2,1,0:T(8,128)(2,1)S(1)}, bf16[1,512,256]{2,1,0:T(8,128)(2,1)}, u32[]{:S(2)}) copy-start(bf16[1,512,256]{2,1,0:T(8,128)(2,1)} %param.11) | copy-start | bytes 786436
  87.4 2.1 %copy-start.10 = (f32[256]{0:T(256)S(1)}, f32[256]{0:T(256)}, u32[]{:S(2)}) copy-start(f32[256]{0:T(256)} %param.17) | copy-start | bytes 3076
  87.4 7.8 %collective-permute-start = (bf16[16,16,128]{2,1,0:T(8,128)(2,1)S(1)}, bf16[16,16,128]{2,1,0:T(8,128)(2,1)S(1)}, u32[]{:S(2)}, u32[]{:S(2)}) collective-permute-start(bf16[16,16,128]{2,1,0:T(8,128)(2,1)S(1)} %all_to_all.23.own), channel_id=1, source_target_pairs={{0,256},{256,0},{1,257},{257,1},{2,258},{258,2},{3,259},{259,3},{4... | collective-permute-start | bytes 196616 | tf_op jit(solution)/shard_map/ppermute | solution.py:489

commit v6 on v5

--- a/solution.py
+++ b/solution.py
@@ -23,6 +23,7 @@
 TILE = 16
 LANE = 128
 CHUNKS = TOK // LANE
+QUAD = 4
 PAIRS = (HALF + 1) // 2
 ROWS = 2 * HALF + PAIRS
 VMEM_LIMIT = 24 * 1024 * 1024
@@ -371,20 +372,19 @@
             preferred_element_type=f32,
         )
         weight_sum = add(weight_sum, share)
-    blank = jnp.zeros((8, LANE), f32)
-    for piece in range(16):
-        r, c = piece // 4, piece % 4
-        feature = alongs[c // 2][16 * r : 16 * (r + 1), LANE * (c % 2) : LANE * (c % 2 + 1)]
-        r, c = piece // 2, piece % 2
-        other = weight_sum[8 * r : 8 * (r + 1), LANE * c : LANE * (c + 1)]
-        other = jnp.concatenate([other, blank], axis=0)
+    blank = jnp.zeros((ORDER - 2 * TILE, LANE), f32)
+    for piece in range(QUAD):
+        c = piece % 2
+        feature = alongs[piece // 2][:, LANE * c : LANE * (c + 1)]
+        rows = weight_sum[TILE * piece : TILE * (piece + 1)]
+        other = jnp.concatenate([rows[:, :LANE], rows[:, LANE:], blank], axis=0)
         sums[piece] = jnp.where(is_feature, feature, other).astype(bf16)
 
 
 def parts(back, features, weight, **kw):
     return pl.pallas_call(
         parts_kernel,
-        out_shape=pltpu.VMEM((16, TILE, LANE), jnp.bfloat16),
+        out_shape=pltpu.VMEM((QUAD, ORDER, LANE), jnp.bfloat16),
         in_specs=[pl.BlockSpec(memory_space=pltpu.VMEM)] * 3,
         out_specs=pl.BlockSpec(memory_space=pltpu.VMEM),
         compiler_params=pltpu.CompilerParams(vmem_limit_bytes=VMEM_LIMIT),
@@ -396,15 +396,13 @@
 def assemble_kernel(own, other, feature_grad, weight_grad):
     f32 = jnp.float32
     is_feature = lax.axis_index("dp") == 0
-    for piece in range(16):
+    for piece in range(QUAD):
         a = own[piece].astype(f32)
         b = other[piece].astype(f32)
-        feature = jnp.where(is_feature, a, b)
-        weight = jnp.where(is_feature, b, a)[:8]
-        r, c = piece // 4, piece % 4
-        feature_grad[16 * r : 16 * (r + 1), 128 * c : 128 * (c + 1)] = feature
-        r, c = piece // 2, piece % 2
-        weight_grad[8 * r : 8 * (r + 1), 128 * c : 128 * (c + 1)] = weight
+        feature_grad[:, LANE * piece : LANE * (piece + 1)] = jnp.where(is_feature, a, b)
+        rows = jnp.where(is_feature, b, a)
+        weight = jnp.concatenate([rows[:TILE], rows[TILE : 2 * TILE]], axis=1)
+        weight_grad[TILE * piece : TILE * (piece + 1)] = weight
 
 
 def assemble(own, other, **kw):
@@ -457,6 +455,32 @@
     )(*(in_vmem(a) for a in (back, values, gate_first, gate_second, grad, skip)))
 
 
+EVERYWHERE = ("dp", "chan", "ctx")
+
+
+def device(dp, chan, ctx):
+    return dp * 256 + chan * 16 + ctx
+
+
+def exchange(pieces):
+    groups = []
+    for other in range(16):
+        for quad in range(4):
+            groups.append([device(0, QUAD * quad + i, other) for i in range(QUAD)])
+            groups.append([device(1, other, QUAD * quad + i) for i in range(QUAD)])
+    return lax.all_to_all(pieces, EVERYWHERE, 0, 0, axis_index_groups=groups, tiled=True)
+
+
+def rotate_quads(array, step):
+    pairs = []
+    for a in range(16):
+        for b in range(16):
+            after = (a + QUAD * step) % 16
+            pairs.append((device(0, a, b), device(0, after, b)))
+            pairs.append((device(1, b, a), device(1, b, after)))
+    return lax.ppermute(array, EVERYWHERE, pairs)
+
+
 def local(
     values,
     gate_first,
@@ -475,16 +499,13 @@
     sent = spread(values, gate_first, gate_second, output_grad, filter_features, filter_weight, decay)
     got = lax.all_to_all(sent, group, 0, 0, tiled=True)
     back = lax.all_to_all(spectral(got, decay), group, 0, 0, tiled=True)
-    everywhere = ("dp", "chan", "ctx")
-    groups = [[16 * z + j for z in range(16)] for j in range(16)]
-    groups += [[256 + 16 * z + j for j in range(16)] for z in range(16)]
-
-    def exchange(pieces):
-        return lax.all_to_all(pieces, everywhere, 0, 0, axis_index_groups=groups, tiled=True)
-
     pieces = exchange(parts(back, filter_features, filter_weight))
-    summed = jnp.sum(pieces.astype(jnp.float32), axis=0).astype(jnp.bfloat16)
-    copies = exchange(jnp.broadcast_to(summed[None], (16, 16, 128)))
+    near = jnp.sum(pieces.astype(jnp.float32), axis=0)
+    sent = near.astype(jnp.bfloat16)
+    total = near
+    for step in (1, 3, 2):
+        total = total + rotate_quads(sent, step).astype(jnp.float32)
+    copies = exchange(jnp.broadcast_to(total.astype(jnp.bfloat16)[None], (QUAD, ORDER, LANE)))
     back, copies = lax.optimization_barrier((back, copies))
     other = lax.ppermute(copies, "dp", [(0, 1), (1, 0)])
     outs = final(back, values, gate_first, gate_second, output_grad, skip_bias[None, :])

time: 97.6 us -> 99.9 us (1.024)
  blocking collectives: 80.9 us -> 56.9 us
  starting transfers between devices: 2.04 us -> 25 us
  waiting for transfers between devices: 4.23 us -> 7.35 us
    all_to_all x2, blocking collectives: 42.4 us -> 18.4 us  [exchange(): lax.all_to_all(pieces, EVERYWHERE, 0, 0, axis_index_groups=groups, tiled=...]
    ppermute x0 -> x3, starting transfers between devices: none -> 22.9 us  [rotate_quads(): return lax.ppermute(array, EVERYWHERE, pairs)]
    ppermute x0 -> x3, waiting for transfers between devices: none -> 3.13 us  [rotate_quads(): return lax.ppermute(array, EVERYWHERE, pairs)]
  transfers between devices with their start and end apart: 1 -> 4, of which waited for: 1 -> 2; matrix products, arithmetic and copies ran while one was open for 0% -> 0% of each run, Pallas kernels for 2% -> 2%
where the time goes in v6:
time: 99.9 us; the launch traced here: 98 us
  blocking collectives  56.9 us (57%)
  starting transfers between devices  25 us (25%)
  Pallas kernels  7.9 us (8%)
  waiting for transfers between devices  7.35 us (7%)
    ppermute x3, starting transfers between devices, rotate_quads(): return lax.ppermute(array, EVERYWHERE, pairs)  22.9 us
    all_to_all x1, blocking collectives, local(): got = lax.all_to_all(sent, group, 0, 0, tiled=True)  20 us
    all_to_all x1, blocking collectives, local(): back = lax.all_to_all(spectral(got, decay), group, 0, 0, tiled=True)  18.5 us
    all_to_all x2, blocking collectives, exchange(): lax.all_to_all(pieces, EVERYWHERE, 0, 0, axis_index_groups=groups, tiled=...  18.4 us
    ppermute x1, waiting for transfers between devices, local(): other = lax.ppermute(copies, 'dp', [(0, 1), (1, 0)])  4.21 us
    pallas_call x1, Pallas kernels, spectral(): pl.pallas_call(spectral_kernel, out_shape=pltpu.VMEM((GROUP, (CHUNKS + 2)...  3.74 us
    ppermute x3, waiting for transfers between devices, rotate_quads(): return lax.ppermute(array, EVERYWHERE, pairs)  3.13 us
    ppermute x1, starting transfers between devices, local(): other = lax.ppermute(copies, 'dp', [(0, 1), (1, 0)])  2.04 us
  transfers between devices with their start and end apart: 4, of which 2 were waited for; matrix products, arithmetic and copies ran while one was open for 0% of the time, Pallas kernels for 2%

profile of v6, /device:TPU:6, one launch (start us, length us, event | category | flops | bytes accessed | tf_op | source)
XLA Modules:
  0.0 98.0 jit_solution(9712570172401008703)
XLA Ops:
  0.6 1.8 %spread.1 = bf16[32,80,128]{2,1,0:T(8,128)(2,1)S(1)} custom-call(bf16[512,256]{1,0:T(8,128)(2,1)} %bitcast.10, bf16[512,256]{1,0:T(8,128)(2,1)} %bitcast.12, bf16[512,256]{1,0:T(8,128)(2,1)} %bitcast.14, bf16[512,256]{1,0:T(8,128)(2,1)} %bitcast.16, bf16[64,512]{1,0:T(8,128)(2,1)} %features.3, bf16[64,256]{1,0:T(8,128)(2,1)} %weight.3, f32[1,256]{1,0:T(1,128)} %bitcast.18), custom_call_target="tpu_custom_call" | custom-call | tf_op jit(solution)/shard_map/spread/pallas_call | solution.py:170
  2.4 0.0 copy-start.4
  2.4 0.0 copy-start.7
  2.4 0.0 copy-start.8
  2.4 0.0 copy-start.9
  2.4 20.0 %all_to_all.20.got = bf16[32,80,128]{2,1,0:T(8,128)(2,1)S(1)} all-to-all(bf16[32,80,128]{2,1,0:T(8,128)(2,1)S(1)} %spread.1), channel_id=1, replica_groups=mesh['dp'=2,'chan'=16,'ctx'=16] {'dp','ctx'}, dimensions={0} | all-to-all | bytes 1310720 | tf_op jit(solution)/shard_map/all_to_all | solution.py:500
  22.5 0.0 copy-done.4
  22.5 0.0 copy-done.7
  22.5 0.0 copy-done.8
  22.5 0.0 copy-done.9
  22.5 3.7 %spectral.1 = bf16[32,96,128]{2,1,0:T(8,128)(2,1)S(1)} custom-call(bf16[32,80,128]{2,1,0:T(8,128)(2,1)S(1)} %all_to_all.20.got, bf16[512,256]{1,0:T(8,128)(2,1)S(1)} %copy-done.4, f32[2,33,256]{2,1,0:T(8,128)S(1)} %copy-done.7, f32[2,33,256]{2,1,0:T(8,128)S(1)} %copy-done.8, f32[1,256]{1,0:T(1,128)S(1)} %bitcast.19), custom_call_target="tpu_custom_call" | custom-call | tf_op jit(solution)/shard_map/spectral/pallas_call | solution.py:343
  26.2 0.0 copy-start.5
  26.2 0.0 copy-start.6
  26.2 18.5 %all_to_all.21.back = bf16[32,96,128]{2,1,0:T(8,128)(2,1)S(1)} all-to-all(bf16[32,96,128]{2,1,0:T(8,128)(2,1)S(1)} %spectral.1), channel_id=1, replica_groups=mesh['dp'=2,'chan'=16,'ctx'=16] {'dp','ctx'}, dimensions={0} | all-to-all | bytes 1572864 | tf_op jit(solution)/shard_map/all_to_all | solution.py:501
  44.7 0.0 copy-done.5
  44.7 0.0 copy-done.6
  44.7 0.0 copy-start.2
  44.7 0.0 copy-start.3
  44.7 0.2 parts.1
  45.0 0.0 copy-start.1
  45.0 10.3 %all_to_all.22 = bf16[4,64,128]{2,1,0:T(8,128)(2,1)S(1)} all-to-all(bf16[4,64,128]{2,1,0:T(8,128)(2,1)S(1)} %parts.1), channel_id=1, replica_groups={{0,16,32,48},{256,257,258,259},{64,80,96,112},{260,261,262,263},{128,14..., dimensions={0} | all-to-all | bytes 131072 | tf_op jit(solution)/shard_map/all_to_all | solution.py:471
  55.3 0.0 copy-start
  55.3 13.2 %collective-permute-start.2 = (bf16[64,128]{1,0:T(8,128)(2,1)S(1)}, bf16[64,128]{1,0:T(8,128)(2,1)S(1)}, u32[]{:S(2)}, u32[]{:S(2)}) collective-permute-start(bf16[64,128]{1,0:T(8,128)(2,1)S(1)} %convert_element_type.19), channel_id=1, source_target_pairs={{0,128},{256,264},{1,129},{272,280},{2,130},{288,296},{3,131},{304... | collective-permute-start | bytes 49160 | tf_op jit(solution)/shard_map/ppermute | solution.py:481
  68.5 3.3 %collective-permute-start.1 = (bf16[64,128]{1,0:T(8,128)(2,1)S(1)}, bf16[64,128]{1,0:T(8,128)(2,1)S(1)}, u32[]{:S(2)}, u32[]{:S(2)}) collective-permute-start(bf16[64,128]{1,0:T(8,128)(2,1)S(1)} %convert_element_type.19), channel_id=1, source_target_pairs={{0,192},{256,268},{1,193},{272,284},{2,194},{288,300},{3,195},{304... | collective-permute-start | bytes 49160 | tf_op jit(solution)/shard_map/ppermute | solution.py:481
  71.9 6.4 %collective-permute-start = (bf16[64,128]{1,0:T(8,128)(2,1)S(1)}, bf16[64,128]{1,0:T(8,128)(2,1)S(1)}, u32[]{:S(2)}, u32[]{:S(2)}) collective-permute-start(bf16[64,128]{1,0:T(8,128)(2,1)S(1)} %convert_element_type.19), channel_id=1, source_target_pairs={{0,64},{256,260},{1,65},{272,276},{2,66},{288,292},{3,67},{304,308... | collective-permute-start | bytes 49160 | tf_op jit(solution)/shard_map/ppermute | solution.py:481
  78.3 0.0 collective-permute-done.2
  78.3 0.0 collective-permute-done.1
  78.3 3.1 %collective-permute-done = bf16[64,128]{1,0:T(8,128)(2,1)S(1)} collective-permute-done((bf16[64,128]{1,0:T(8,128)(2,1)S(1)}, bf16[64,128]{1,0:T(8,128)(2,1)S(1)}, u32[]{:S(2)}, u32[]{:S(2)}) %collective-permute-start) | collective-permute-done | bytes 16416 | tf_op jit(solution)/shard_map/ppermute | solution.py:481
  81.5 8.1 %all_to_all.23.own = bf16[4,64,128]{2,1,0:T(8,128)(2,1)S(1)} all-to-all(bf16[4,64,128]{2,1,0:T(8,128)(2,1)S(1)} %broadcast_in_dim.25), channel_id=1, replica_groups={{0,16,32,48},{256,257,258,259},{64,80,96,112},{260,261,262,263},{128,14..., dimensions={0} | all-to-all | bytes 131072 | tf_op jit(solution)/shard_map/all_to_all | solution.py:471
  89.6 0.0 copy-start.10
  89.6 2.0 %collective-permute-start.3 = (bf16[4,64,128]{2,1,0:T(8,128)(2,1)S(1)}, bf16[4,64,128]{2,1,0:T(8,128)(2,1)S(1)}, u32[]{:S(2)}, u32[]{:S(2)}) collective-permute-start(bf16[4,64,128]{2,1,0:T(8,128)(2,1)S(1)} %all_to_all.23.own), channel_id=1, source_target_pairs={{0,256},{256,0},{1,257},{257,1},{2,258},{258,2},{3,259},{259,3},{4... | collective-permute-start | bytes 196616 | tf_op jit(solution)/shard_map/ppermute | solution.py:510
  91.6 0.0 copy-done.2
  91.6 0.0 copy-done.3
  91.6 0.0 copy-done.1
  91.6 0.0 copy-done
  91.7 0.0 copy-done.10
  91.7 1.5 %final.1 = (bf16[512,256]{1,0:T(8,128)(2,1)}, bf16[512,256]{1,0:T(8,128)(2,1)}, bf16[512,256]{1,0:T(8,128)(2,1)}, bf16[512,256]{1,0:T(8,128)(2,1)}) custom-call(bf16[32,96,128]{2,1,0:T(8,128)(2,1)S(1)} %all_to_all.21.back, bf16[512,256]{1,0:T(8,128)(2,1)S(1)} %bitcast.11, bf16[512,256]{1,0:T(8,128)(2,1)S(1)} %bitcast.13, bf16[512,256]{1,0:T(8,128)(2,1)S(1)} %bitcast.15, ...), custom_call_target="tpu_custom_call" | custom-call | tf_op jit(solution)/shard_map/final/pallas_call | solution.py:447
  93.1 4.2 %collective-permute-done.3.other = bf16[4,64,128]{2,1,0:T(8,128)(2,1)S(1)} collective-permute-done((bf16[4,64,128]{2,1,0:T(8,128)(2,1)S(1)}, bf16[4,64,128]{2,1,0:T(8,128)(2,1)S(1)}, u32[]{:S(2)}, u32[]{:S(2)}) %collective-permute-start.3) | collective-permute-done | bytes 65568 | tf_op jit(solution)/shard_map/ppermute | solution.py:510
  97.4 0.7 assemble.1
  (4 shorter events, 0.0 us)
Async XLA Ops:
  2.4 20.1 %copy-start.4 = (bf16[512,256]{1,0:T(8,128)(2,1)S(1)}, bf16[512,256]{1,0:T(8,128)(2,1)}, u32[]{:S(2)}) copy-start(bf16[512,256]{1,0:T(8,128)(2,1)} %constant.8.clone.basis) | copy-start | bytes 786436
  2.4 20.1 %copy-start.7 = (f32[2,33,256]{2,1,0:T(8,128)S(1)}, f32[2,33,256]{2,1,0:T(8,128)}, u32[]{:S(2)}) copy-start(f32[2,33,256]{2,1,0:T(8,128)} %constant.9.clone.forward) | copy-start | bytes 202756
  2.4 20.1 %copy-start.8 = (f32[2,33,256]{2,1,0:T(8,128)S(1)}, f32[2,33,256]{2,1,0:T(8,128)}, u32[]{:S(2)}) copy-start(f32[2,33,256]{2,1,0:T(8,128)} %constant.10.clone.inverse) | copy-start | bytes 202756
  2.4 20.0 %copy-start.9 = (f32[256]{0:T(256)S(1)}, f32[256]{0:T(256)}, u32[]{:S(2)}) copy-start(f32[256]{0:T(256)} %param.16) | copy-start | bytes 3076
  26.2 18.5 %copy-start.5 = (bf16[64,512]{1,0:T(8,128)(2,1)S(1)}, bf16[64,512]{1,0:T(8,128)(2,1)}, u32[]{:S(2)}) copy-start(bf16[64,512]{1,0:T(8,128)(2,1)} %features.3) | copy-start | bytes 196612
  26.2 18.5 %copy-start.6 = (bf16[64,256]{1,0:T(8,128)(2,1)S(1)}, bf16[64,256]{1,0:T(8,128)(2,1)}, u32[]{:S(2)}) copy-start(bf16[64,256]{1,0:T(8,128)(2,1)} %weight.3) | copy-start | bytes 98308
  44.7 46.9 %copy-start.2 = (bf16[1,512,256]{2,1,0:T(8,128)(2,1)S(1)}, bf16[1,512,256]{2,1,0:T(8,128)(2,1)}, u32[]{:S(2)}) copy-start(bf16[1,512,256]{2,1,0:T(8,128)(2,1)} %param.13) | copy-start | bytes 786436
  44.7 46.9 %copy-start.3 = (bf16[1,512,256]{2,1,0:T(8,128)(2,1)S(1)}, bf16[1,512,256]{2,1,0:T(8,128)(2,1)}, u32[]{:S(2)}) copy-start(bf16[1,512,256]{2,1,0:T(8,128)(2,1)} %param.18) | copy-start | bytes 786436
  45.0 46.7 %copy-start.1 = (bf16[1,512,256]{2,1,0:T(8,128)(2,1)S(1)}, bf16[1,512,256]{2,1,0:T(8,128)(2,1)}, u32[]{:S(2)}) copy-start(bf16[1,512,256]{2,1,0:T(8,128)(2,1)} %param.12) | copy-start | bytes 786436
  55.3 36.3 %copy-start = (bf16[1,512,256]{2,1,0:T(8,128)(2,1)S(1)}, bf16[1,512,256]{2,1,0:T(8,128)(2,1)}, u32[]{:S(2)}) copy-start(bf16[1,512,256]{2,1,0:T(8,128)(2,1)} %param.11) | copy-start | bytes 786436
  55.3 22.9 %collective-permute-start.2 = (bf16[64,128]{1,0:T(8,128)(2,1)S(1)}, bf16[64,128]{1,0:T(8,128)(2,1)S(1)}, u32[]{:S(2)}, u32[]{:S(2)}) collective-permute-start(bf16[64,128]{1,0:T(8,128)(2,1)S(1)} %convert_element_type.19), channel_id=1, source_target_pairs={{0,128},{256,264},{1,129},{272,280},{2,130},{288,296},{3,131},{304... | collective-permute-start | bytes 49160 | tf_op jit(solution)/shard_map/ppermute | solution.py:481
  68.5 9.8 %collective-permute-start.1 = (bf16[64,128]{1,0:T(8,128)(2,1)S(1)}, bf16[64,128]{1,0:T(8,128)(2,1)S(1)}, u32[]{:S(2)}, u32[]{:S(2)}) collective-permute-start(bf16[64,128]{1,0:T(8,128)(2,1)S(1)} %convert_element_type.19), channel_id=1, source_target_pairs={{0,192},{256,268},{1,193},{272,284},{2,194},{288,300},{3,195},{304... | collective-permute-start | bytes 49160 | tf_op jit(solution)/shard_map/ppermute | solution.py:481
  71.9 9.6 %collective-permute-start = (bf16[64,128]{1,0:T(8,128)(2,1)S(1)}, bf16[64,128]{1,0:T(8,128)(2,1)S(1)}, u32[]{:S(2)}, u32[]{:S(2)}) collective-permute-start(bf16[64,128]{1,0:T(8,128)(2,1)S(1)} %convert_element_type.19), channel_id=1, source_target_pairs={{0,64},{256,260},{1,65},{272,276},{2,66},{288,292},{3,67},{304,308... | collective-permute-start | bytes 49160 | tf_op jit(solution)/shard_map/ppermute | solution.py:481
  89.6 2.1 %copy-start.10 = (f32[256]{0:T(256)S(1)}, f32[256]{0:T(256)}, u32[]{:S(2)}) copy-start(f32[256]{0:T(256)} %param.17) | copy-start | bytes 3076
  89.6 7.8 %collective-permute-start.3 = (bf16[4,64,128]{2,1,0:T(8,128)(2,1)S(1)}, bf16[4,64,128]{2,1,0:T(8,128)(2,1)S(1)}, u32[]{:S(2)}, u32[]{:S(2)}) collective-permute-start(bf16[4,64,128]{2,1,0:T(8,128)(2,1)S(1)} %all_to_all.23.own), channel_id=1, source_target_pairs={{0,256},{256,0},{1,257},{257,1},{2,258},{258,2},{3,259},{259,3},{4... | collective-permute-start | bytes 196616 | tf_op jit(solution)/shard_map/ppermute | solution.py:510

commit v7 on v6

--- a/solution.py
+++ b/solution.py
@@ -471,13 +471,12 @@
     return lax.all_to_all(pieces, EVERYWHERE, 0, 0, axis_index_groups=groups, tiled=True)
 
 
-def rotate_quads(array, step):
+def swap(array, distance):
     pairs = []
     for a in range(16):
         for b in range(16):
-            after = (a + QUAD * step) % 16
-            pairs.append((device(0, a, b), device(0, after, b)))
-            pairs.append((device(1, b, a), device(1, b, after)))
+            pairs.append((device(0, a, b), device(0, a ^ distance, b)))
+            pairs.append((device(1, b, a), device(1, b, a ^ distance)))
     return lax.ppermute(array, EVERYWHERE, pairs)
 
 
@@ -500,11 +499,10 @@
     got = lax.all_to_all(sent, group, 0, 0, tiled=True)
     back = lax.all_to_all(spectral(got, decay), group, 0, 0, tiled=True)
     pieces = exchange(parts(back, filter_features, filter_weight))
-    near = jnp.sum(pieces.astype(jnp.float32), axis=0)
-    sent = near.astype(jnp.bfloat16)
-    total = near
-    for step in (1, 3, 2):
-        total = total + rotate_quads(sent, step).astype(jnp.float32)
+    total = jnp.sum(pieces.astype(jnp.float32), axis=0)
+    for distance in (8, 4):
+        sent = total.astype(jnp.bfloat16)
+        total = sent.astype(jnp.float32) + swap(sent, distance).astype(jnp.float32)
     copies = exchange(jnp.broadcast_to(total.astype(jnp.bfloat16)[None], (QUAD, ORDER, LANE)))
     back, copies = lax.optimization_barrier((back, copies))
     other = lax.ppermute(copies, "dp", [(0, 1), (1, 0)])

time: 99.9 us -> 99 us (level)
  starting transfers between devices: 25 us -> 23.8 us
    ppermute x3 -> x2, starting transfers between devices: 22.9 us -> 21.7 us  [swap(): return lax.ppermute(array, EVERYWHERE, pairs)]
    ppermute x3 -> x2, waiting for transfers between devices: 3.13 us -> 3.41 us  [swap(): return lax.ppermute(array, EVERYWHERE, pairs)]
  transfers between devices with their start and end apart: 4 -> 3, of which waited for: 2 -> 3; matrix products, arithmetic and copies ran while one was open for 0% -> 0% of each run, Pallas kernels for 2% -> 2%
where the time goes in v7:
time: 99 us; the launch traced here: 97.1 us
  blocking collectives  56.9 us (57%)
  starting transfers between devices  23.8 us (24%)
  Pallas kernels  7.89 us (8%)
  waiting for transfers between devices  7.63 us (8%)
    ppermute x2, starting transfers between devices, swap(): return lax.ppermute(array, EVERYWHERE, pairs)  21.7 us
    all_to_all x1, blocking collectives, local(): got = lax.all_to_all(sent, group, 0, 0, tiled=True)  20 us
    all_to_all x1, blocking collectives, local(): back = lax.all_to_all(spectral(got, decay), group, 0, 0, tiled=True)  18.5 us
    all_to_all x2, blocking collectives, exchange(): lax.all_to_all(pieces, EVERYWHERE, 0, 0, axis_index_groups=groups, tiled=...  18.4 us
    ppermute x1, waiting for transfers between devices, local(): other = lax.ppermute(copies, 'dp', [(0, 1), (1, 0)])  4.22 us
    pallas_call x1, Pallas kernels, spectral(): pl.pallas_call(spectral_kernel, out_shape=pltpu.VMEM((GROUP, (CHUNKS + 2)...  3.74 us
    ppermute x2, waiting for transfers between devices, swap(): return lax.ppermute(array, EVERYWHERE, pairs)  3.41 us
    ppermute x1, starting transfers between devices, local(): other = lax.ppermute(copies, 'dp', [(0, 1), (1, 0)])  2.04 us
  transfers between devices with their start and end apart: 3, of which 3 were waited for; matrix products, arithmetic and copies ran while one was open for 0% of the time, Pallas kernels for 2%

profile of v7, /device:TPU:6, one launch (start us, length us, event | category | flops | bytes accessed | tf_op | source)
XLA Modules:
  0.0 97.1 jit_solution(14842143818086551414)
XLA Ops:
  0.6 1.8 %spread.1 = bf16[32,80,128]{2,1,0:T(8,128)(2,1)S(1)} custom-call(bf16[512,256]{1,0:T(8,128)(2,1)} %bitcast.10, bf16[512,256]{1,0:T(8,128)(2,1)} %bitcast.12, bf16[512,256]{1,0:T(8,128)(2,1)} %bitcast.14, bf16[512,256]{1,0:T(8,128)(2,1)} %bitcast.16, bf16[64,512]{1,0:T(8,128)(2,1)} %features.3, bf16[64,256]{1,0:T(8,128)(2,1)} %weight.3, f32[1,256]{1,0:T(1,128)} %bitcast.18), custom_call_target="tpu_custom_call" | custom-call | tf_op jit(solution)/shard_map/spread/pallas_call | solution.py:170
  2.4 0.0 copy-start.4
  2.4 0.0 copy-start.7
  2.4 0.0 copy-start.8
  2.4 0.0 copy-start.9
  2.4 20.0 %all_to_all.20.got = bf16[32,80,128]{2,1,0:T(8,128)(2,1)S(1)} all-to-all(bf16[32,80,128]{2,1,0:T(8,128)(2,1)S(1)} %spread.1), channel_id=1, replica_groups=mesh['dp'=2,'chan'=16,'ctx'=16] {'dp','ctx'}, dimensions={0} | all-to-all | bytes 1310720 | tf_op jit(solution)/shard_map/all_to_all | solution.py:499
  22.5 0.0 copy-done.4
  22.5 0.0 copy-done.7
  22.5 0.0 copy-done.8
  22.5 0.0 copy-done.9
  22.5 3.7 %spectral.1 = bf16[32,96,128]{2,1,0:T(8,128)(2,1)S(1)} custom-call(bf16[32,80,128]{2,1,0:T(8,128)(2,1)S(1)} %all_to_all.20.got, bf16[512,256]{1,0:T(8,128)(2,1)S(1)} %copy-done.4, f32[2,33,256]{2,1,0:T(8,128)S(1)} %copy-done.7, f32[2,33,256]{2,1,0:T(8,128)S(1)} %copy-done.8, f32[1,256]{1,0:T(1,128)S(1)} %bitcast.19), custom_call_target="tpu_custom_call" | custom-call | tf_op jit(solution)/shard_map/spectral/pallas_call | solution.py:343
  26.2 0.0 copy-start.5
  26.2 0.0 copy-start.6
  26.2 18.5 %all_to_all.21.back = bf16[32,96,128]{2,1,0:T(8,128)(2,1)S(1)} all-to-all(bf16[32,96,128]{2,1,0:T(8,128)(2,1)S(1)} %spectral.1), channel_id=1, replica_groups=mesh['dp'=2,'chan'=16,'ctx'=16] {'dp','ctx'}, dimensions={0} | all-to-all | bytes 1572864 | tf_op jit(solution)/shard_map/all_to_all | solution.py:500
  44.7 0.0 copy-done.5
  44.7 0.0 copy-done.6
  44.7 0.0 copy-start.2
  44.7 0.0 copy-start.3
  44.7 0.2 parts.1
  45.0 0.0 copy-start
  45.0 0.0 copy-start.1
  45.0 10.3 %all_to_all.22 = bf16[4,64,128]{2,1,0:T(8,128)(2,1)S(1)} all-to-all(bf16[4,64,128]{2,1,0:T(8,128)(2,1)S(1)} %parts.1), channel_id=1, replica_groups={{0,16,32,48},{256,257,258,259},{64,80,96,112},{260,261,262,263},{128,14..., dimensions={0} | all-to-all | bytes 131072 | tf_op jit(solution)/shard_map/all_to_all | solution.py:471
  55.3 13.0 %collective-permute-start = (bf16[64,128]{1,0:T(8,128)(2,1)S(1)}, bf16[64,128]{1,0:T(8,128)(2,1)S(1)}, u32[]{:S(2)}, u32[]{:S(2)}) collective-permute-start(bf16[64,128]{1,0:T(8,128)(2,1)S(1)} %reduce_sum.12), channel_id=1, source_target_pairs={{0,128},{256,264},{1,129},{272,280},{2,130},{288,296},{3,131},{304... | collective-permute-start | bytes 49160 | tf_op jit(solution)/shard_map/ppermute | solution.py:480
  68.4 1.7 %collective-permute-done = bf16[64,128]{1,0:T(8,128)(2,1)S(1)} collective-permute-done((bf16[64,128]{1,0:T(8,128)(2,1)S(1)}, bf16[64,128]{1,0:T(8,128)(2,1)S(1)}, u32[]{:S(2)}, u32[]{:S(2)}) %collective-permute-start) | collective-permute-done | bytes 16416 | tf_op jit(solution)/shard_map/ppermute | solution.py:480
  70.1 8.7 %collective-permute-start.1 = (bf16[64,128]{1,0:T(8,128)(2,1)S(1)}, bf16[64,128]{1,0:T(8,128)(2,1)S(1)}, u32[]{:S(2)}, u32[]{:S(2)}) collective-permute-start(bf16[64,128]{1,0:T(8,128)(2,1)S(1)} %add_convert_fusion.1), channel_id=1, source_target_pairs={{0,64},{256,260},{1,65},{272,276},{2,66},{288,292},{3,67},{304,308... | collective-permute-start | bytes 49160 | tf_op jit(solution)/shard_map/ppermute | solution.py:480
  78.8 1.7 %collective-permute-done.1 = bf16[64,128]{1,0:T(8,128)(2,1)S(1)} collective-permute-done((bf16[64,128]{1,0:T(8,128)(2,1)S(1)}, bf16[64,128]{1,0:T(8,128)(2,1)S(1)}, u32[]{:S(2)}, u32[]{:S(2)}) %collective-permute-start.1) | collective-permute-done | bytes 16416 | tf_op jit(solution)/shard_map/ppermute | solution.py:480
  80.5 8.1 %all_to_all.23.own = bf16[4,64,128]{2,1,0:T(8,128)(2,1)S(1)} all-to-all(bf16[4,64,128]{2,1,0:T(8,128)(2,1)S(1)} %broadcast_in_dim.25), channel_id=1, replica_groups={{0,16,32,48},{256,257,258,259},{64,80,96,112},{260,261,262,263},{128,14..., dimensions={0} | all-to-all | bytes 131072 | tf_op jit(solution)/shard_map/all_to_all | solution.py:471
  88.6 0.0 copy-start.10
  88.6 2.0 %collective-permute-start.2 = (bf16[4,64,128]{2,1,0:T(8,128)(2,1)S(1)}, bf16[4,64,128]{2,1,0:T(8,128)(2,1)S(1)}, u32[]{:S(2)}, u32[]{:S(2)}) collective-permute-start(bf16[4,64,128]{2,1,0:T(8,128)(2,1)S(1)} %all_to_all.23.own), channel_id=1, source_target_pairs={{0,256},{256,0},{1,257},{257,1},{2,258},{258,2},{3,259},{259,3},{4... | collective-permute-start | bytes 196616 | tf_op jit(solution)/shard_map/ppermute | solution.py:508
  90.7 0.0 copy-done.2
  90.7 0.0 copy-done.3
  90.7 0.0 copy-done
  90.7 0.0 copy-done.1
  90.7 0.0 copy-done.10
  90.7 1.5 %final.1 = (bf16[512,256]{1,0:T(8,128)(2,1)}, bf16[512,256]{1,0:T(8,128)(2,1)}, bf16[512,256]{1,0:T(8,128)(2,1)}, bf16[512,256]{1,0:T(8,128)(2,1)}) custom-call(bf16[32,96,128]{2,1,0:T(8,128)(2,1)S(1)} %all_to_all.21.back, bf16[512,256]{1,0:T(8,128)(2,1)S(1)} %bitcast.11, bf16[512,256]{1,0:T(8,128)(2,1)S(1)} %bitcast.13, bf16[512,256]{1,0:T(8,128)(2,1)S(1)} %bitcast.15, ...), custom_call_target="tpu_custom_call" | custom-call | tf_op jit(solution)/shard_map/final/pallas_call | solution.py:447
  92.2 4.2 %collective-permute-done.2.other = bf16[4,64,128]{2,1,0:T(8,128)(2,1)S(1)} collective-permute-done((bf16[4,64,128]{2,1,0:T(8,128)(2,1)S(1)}, bf16[4,64,128]{2,1,0:T(8,128)(2,1)S(1)}, u32[]{:S(2)}, u32[]{:S(2)}) %collective-permute-start.2) | collective-permute-done | bytes 65568 | tf_op jit(solution)/shard_map/ppermute | solution.py:508
  96.4 0.7 assemble.1
  (4 shorter events, 0.0 us)
Async XLA Ops:
  2.4 20.1 %copy-start.4 = (bf16[512,256]{1,0:T(8,128)(2,1)S(1)}, bf16[512,256]{1,0:T(8,128)(2,1)}, u32[]{:S(2)}) copy-start(bf16[512,256]{1,0:T(8,128)(2,1)} %constant.9.clone.basis) | copy-start | bytes 786436
  2.4 20.1 %copy-start.7 = (f32[2,33,256]{2,1,0:T(8,128)S(1)}, f32[2,33,256]{2,1,0:T(8,128)}, u32[]{:S(2)}) copy-start(f32[2,33,256]{2,1,0:T(8,128)} %constant.10.clone.forward) | copy-start | bytes 202756
  2.4 20.1 %copy-start.8 = (f32[2,33,256]{2,1,0:T(8,128)S(1)}, f32[2,33,256]{2,1,0:T(8,128)}, u32[]{:S(2)}) copy-start(f32[2,33,256]{2,1,0:T(8,128)} %constant.11.clone.inverse) | copy-start | bytes 202756
  2.4 20.0 %copy-start.9 = (f32[256]{0:T(256)S(1)}, f32[256]{0:T(256)}, u32[]{:S(2)}) copy-start(f32[256]{0:T(256)} %param.16) | copy-start | bytes 3076
  26.2 18.5 %copy-start.5 = (bf16[64,512]{1,0:T(8,128)(2,1)S(1)}, bf16[64,512]{1,0:T(8,128)(2,1)}, u32[]{:S(2)}) copy-start(bf16[64,512]{1,0:T(8,128)(2,1)} %features.3) | copy-start | bytes 196612
  26.2 18.5 %copy-start.6 = (bf16[64,256]{1,0:T(8,128)(2,1)S(1)}, bf16[64,256]{1,0:T(8,128)(2,1)}, u32[]{:S(2)}) copy-start(bf16[64,256]{1,0:T(8,128)(2,1)} %weight.3) | copy-start | bytes 98308
  44.7 46.0 %copy-start.2 = (bf16[1,512,256]{2,1,0:T(8,128)(2,1)S(1)}, bf16[1,512,256]{2,1,0:T(8,128)(2,1)}, u32[]{:S(2)}) copy-start(bf16[1,512,256]{2,1,0:T(8,128)(2,1)} %param.13) | copy-start | bytes 786436
  44.7 46.0 %copy-start.3 = (bf16[1,512,256]{2,1,0:T(8,128)(2,1)S(1)}, bf16[1,512,256]{2,1,0:T(8,128)(2,1)}, u32[]{:S(2)}) copy-start(bf16[1,512,256]{2,1,0:T(8,128)(2,1)} %param.18) | copy-start | bytes 786436
  45.0 45.7 %copy-start = (bf16[1,512,256]{2,1,0:T(8,128)(2,1)S(1)}, bf16[1,512,256]{2,1,0:T(8,128)(2,1)}, u32[]{:S(2)}) copy-start(bf16[1,512,256]{2,1,0:T(8,128)(2,1)} %param.11) | copy-start | bytes 786436
  45.0 45.7 %copy-start.1 = (bf16[1,512,256]{2,1,0:T(8,128)(2,1)S(1)}, bf16[1,512,256]{2,1,0:T(8,128)(2,1)}, u32[]{:S(2)}) copy-start(bf16[1,512,256]{2,1,0:T(8,128)(2,1)} %param.12) | copy-start | bytes 786436
  55.3 14.7 %collective-permute-start = (bf16[64,128]{1,0:T(8,128)(2,1)S(1)}, bf16[64,128]{1,0:T(8,128)(2,1)S(1)}, u32[]{:S(2)}, u32[]{:S(2)}) collective-permute-start(bf16[64,128]{1,0:T(8,128)(2,1)S(1)} %reduce_sum.12), channel_id=1, source_target_pairs={{0,128},{256,264},{1,129},{272,280},{2,130},{288,296},{3,131},{304... | collective-permute-start | bytes 49160 | tf_op jit(solution)/shard_map/ppermute | solution.py:480
  70.1 10.4 %collective-permute-start.1 = (bf16[64,128]{1,0:T(8,128)(2,1)S(1)}, bf16[64,128]{1,0:T(8,128)(2,1)S(1)}, u32[]{:S(2)}, u32[]{:S(2)}) collective-permute-start(bf16[64,128]{1,0:T(8,128)(2,1)S(1)} %add_convert_fusion.1), channel_id=1, source_target_pairs={{0,64},{256,260},{1,65},{272,276},{2,66},{288,292},{3,67},{304,308... | collective-permute-start | bytes 49160 | tf_op jit(solution)/shard_map/ppermute | solution.py:480
  88.6 2.1 %copy-start.10 = (f32[256]{0:T(256)S(1)}, f32[256]{0:T(256)}, u32[]{:S(2)}) copy-start(f32[256]{0:T(256)} %param.17) | copy-start | bytes 3076
  88.6 7.8 %collective-permute-start.2 = (bf16[4,64,128]{2,1,0:T(8,128)(2,1)S(1)}, bf16[4,64,128]{2,1,0:T(8,128)(2,1)S(1)}, u32[]{:S(2)}, u32[]{:S(2)}) collective-permute-start(bf16[4,64,128]{2,1,0:T(8,128)(2,1)S(1)} %all_to_all.23.own), channel_id=1, source_target_pairs={{0,256},{256,0},{1,257},{257,1},{2,258},{258,2},{3,259},{259,3},{4... | collective-permute-start | bytes 196616 | tf_op jit(solution)/shard_map/ppermute | solution.py:508

commit v8 on v5

--- a/solution.py
+++ b/solution.py
@@ -25,7 +25,13 @@
 CHUNKS = TOK // LANE
 PAIRS = (HALF + 1) // 2
 ROWS = 2 * HALF + PAIRS
+FIRST_CHAN = 9
+LEADER = 25
 VMEM_LIMIT = 24 * 1024 * 1024
+
+
+def seat(member):
+    return {0: LEADER, LEADER: 0}.get(member, member)
 
 
 def tables():
@@ -182,7 +188,9 @@
 ):
     f32, bf16 = jnp.float32, jnp.bfloat16
     rates[...] = jnp.broadcast_to(decay[...], (LANE, CH)).T
-    first = (lax.axis_index("dp") * BLOCKS + lax.axis_index("ctx")) * OWN
+    member = lax.axis_index("dp") * BLOCKS + lax.axis_index("ctx")
+    place_of = jnp.where(member == 0, LEADER, jnp.where(member == LEADER, 0, member))
+    first = place_of * OWN
 
     def transformed(xs, lanes):
         turned = []
@@ -207,7 +215,7 @@
     def signals_in(s, chunk):
         lanes = slice(chunk * LANE, (chunk + 1) * LANE)
         xs = [
-            got[s * BLOCKS + j, (2 * h + chunk) * TILE : (2 * h + chunk + 1) * TILE].astype(f32)
+            got[seat(s * BLOCKS + j), (2 * h + chunk) * TILE : (2 * h + chunk + 1) * TILE].astype(f32)
             for j in range(BLOCKS)
             for h in range(2)
         ]
@@ -219,7 +227,7 @@
 
     def kernel_in(chunk):
         xs = [
-            got[s * BLOCKS + j, CHUNKS * TILE :].astype(f32)[chunk * OWN : (chunk + 1) * OWN]
+            got[seat(s * BLOCKS + j), CHUNKS * TILE :].astype(f32)[chunk * OWN : (chunk + 1) * OWN]
             for j in range(BLOCKS)
             for s in range(2)
         ]
@@ -309,8 +317,8 @@
         row = (CHUNKS + chunk) * TILE
         for j in range(BLOCKS):
             both = joined(pieces[2 * j], pieces[2 * j + 1])
-            out[j, row : row + TILE] = both
-            out[BLOCKS + j, row : row + TILE] = both
+            out[seat(j), row : row + TILE] = both
+            out[seat(BLOCKS + j), row : row + TILE] = both
 
     def signals_out(s, chunk):
         lanes = slice(chunk * LANE, (chunk + 1) * LANE)
@@ -323,7 +331,7 @@
             halves.append(returned(spec, lanes))
         for n in range(RADIX // 2):
             row = (n % 2 * 2 + chunk) * TILE
-            out[s * BLOCKS + n // 2, row : row + TILE] = joined(halves[0][n], halves[1][n])
+            out[seat(s * BLOCKS + n // 2), row : row + TILE] = joined(halves[0][n], halves[1][n])
 
     back(rest)
     back(place(0))
@@ -470,13 +478,20 @@
     values, gate_first, gate_second, output_grad = (
         a[0] for a in (values, gate_first, gate_second, output_grad)
     )
-    group = ("dp", "ctx")
+    planes = [[256 * (seat(i) // 16) + 16 * z + seat(i) % 16 for i in range(GROUP)] for z in range(16)]
+
+    def trade(array):
+        return lax.all_to_all(
+            array, ("dp", "chan", "ctx"), 0, 0, axis_index_groups=planes, tiled=True
+        )
+
     decay = decay_rate[None, :]
     sent = spread(values, gate_first, gate_second, output_grad, filter_features, filter_weight, decay)
-    got = lax.all_to_all(sent, group, 0, 0, tiled=True)
-    back = lax.all_to_all(spectral(got, decay), group, 0, 0, tiled=True)
+    got = trade(sent)
+    back = trade(spectral(got, decay))
     everywhere = ("dp", "chan", "ctx")
-    groups = [[16 * z + j for z in range(16)] for j in range(16)]
+    around = [(z + FIRST_CHAN) % 16 for z in range(16)]
+    groups = [[16 * z + j for z in around] for j in range(16)]
     groups += [[256 + 16 * z + j for j in range(16)] for z in range(16)]
 
     def exchange(pieces):

time: 97.6 us -> 88.3 us (0.905); the launches traced: 95.9 us -> 87.6 us
  blocking collectives: 80.9 us -> 72.6 us
    all_to_all x2, blocking collectives: 42.4 us -> 34.3 us  [exchange(): lax.all_to_all(pieces, everywhere, 0, 0, axis_index_groups=groups, tiled=...]
where the time goes in v8:
time: 88.3 us; the launch traced here: 87.6 us
  blocking collectives  72.6 us (82%)
  Pallas kernels  7.89 us (9%)
  waiting for transfers between devices  4.23 us (5%)
  starting transfers between devices  2.04 us (2%)
    all_to_all x2, blocking collectives, trade(): lax.all_to_all(array, ('dp', 'chan', 'ctx'), 0, 0, axis_index_groups=plan...  38.3 us
    all_to_all x2, blocking collectives, exchange(): lax.all_to_all(pieces, everywhere, 0, 0, axis_index_groups=groups, tiled=...  34.3 us
    ppermute x1, waiting for transfers between devices, local(): other = lax.ppermute(copies, 'dp', [(0, 1), (1, 0)])  4.23 us
    pallas_call x1, Pallas kernels, spectral(): pl.pallas_call(spectral_kernel, out_shape=pltpu.VMEM((GROUP, (CHUNKS + 2)...  3.73 us
    ppermute x1, starting transfers between devices, local(): other = lax.ppermute(copies, 'dp', [(0, 1), (1, 0)])  2.04 us
  transfers between devices with their start and end apart: 1, of which 1 were waited for; matrix products, arithmetic and copies ran while one was open for 0% of the time, Pallas kernels for 2%

profile of v8, /device:TPU:6, one launch (start us, length us, event | category | flops | bytes accessed | tf_op | source)
XLA Modules:
  0.0 87.6 jit_solution(14325003102903720806)
XLA Ops:
  0.6 1.8 %spread.1 = bf16[32,80,128]{2,1,0:T(8,128)(2,1)S(1)} custom-call(bf16[512,256]{1,0:T(8,128)(2,1)} %bitcast.10, bf16[512,256]{1,0:T(8,128)(2,1)} %bitcast.12, bf16[512,256]{1,0:T(8,128)(2,1)} %bitcast.14, bf16[512,256]{1,0:T(8,128)(2,1)} %bitcast.16, bf16[64,512]{1,0:T(8,128)(2,1)} %features.3, bf16[64,256]{1,0:T(8,128)(2,1)} %weight.3, f32[1,256]{1,0:T(1,128)} %bitcast.18), custom_call_target="tpu_custom_call" | custom-call | tf_op jit(solution)/shard_map/spread/pallas_call | solution.py:175
  2.4 0.0 copy-start.4
  2.4 0.0 copy-start.7
  2.4 0.0 copy-start.8
  2.4 0.0 copy-start.9
  2.4 20.7 %all_to_all.20.got = bf16[32,80,128]{2,1,0:T(8,128)(2,1)S(1)} all-to-all(bf16[32,80,128]{2,1,0:T(8,128)(2,1)S(1)} %spread.1), channel_id=1, replica_groups={{265,1,2,3,4,5,6,7,8,9,10,11,12,13,14,15,256,257,258,259,260,261,262,26..., dimensions={0} | all-to-all | bytes 1310720 | tf_op jit(solution)/shard_map/all_to_all | solution.py:484
  23.1 0.0 copy-done.4
  23.1 0.0 copy-done.7
  23.1 0.0 copy-done.8
  23.1 0.0 copy-done.9
  23.1 3.7 %spectral.1 = bf16[32,96,128]{2,1,0:T(8,128)(2,1)S(1)} custom-call(bf16[32,80,128]{2,1,0:T(8,128)(2,1)S(1)} %all_to_all.20.got, bf16[512,256]{1,0:T(8,128)(2,1)S(1)} %copy-done.4, f32[2,33,256]{2,1,0:T(8,128)S(1)} %copy-done.7, f32[2,33,256]{2,1,0:T(8,128)S(1)} %copy-done.8, f32[1,256]{1,0:T(1,128)S(1)} %bitcast.19), custom_call_target="tpu_custom_call" | custom-call | tf_op jit(solution)/shard_map/spectral/pallas_call | solution.py:350
  26.9 0.0 copy-start.5
  26.9 0.0 copy-start.6
  26.9 17.6 %all_to_all.21.back = bf16[32,96,128]{2,1,0:T(8,128)(2,1)S(1)} all-to-all(bf16[32,96,128]{2,1,0:T(8,128)(2,1)S(1)} %spectral.1), channel_id=1, replica_groups={{265,1,2,3,4,5,6,7,8,9,10,11,12,13,14,15,256,257,258,259,260,261,262,26..., dimensions={0} | all-to-all | bytes 1572864 | tf_op jit(solution)/shard_map/all_to_all | solution.py:484
  44.5 0.0 copy-done.5
  44.5 0.0 copy-done.6
  44.5 0.0 copy-start.1
  44.5 0.0 copy-start.2
  44.6 0.0 copy-start.3
  44.6 0.2 parts.1
  44.8 0.0 copy-start
  44.8 18.8 %all_to_all.22 = bf16[16,16,128]{2,1,0:T(8,128)(2,1)S(1)} all-to-all(bf16[16,16,128]{2,1,0:T(8,128)(2,1)S(1)} %parts.1), channel_id=1, replica_groups={{144,160,176,192,208,224,240,0,16,32,48,64,80,96,112,128},{145,161,177,..., dimensions={0} | all-to-all | bytes 131072 | tf_op jit(solution)/shard_map/all_to_all | solution.py:498
  63.6 15.5 %all_to_all.23.own = bf16[16,16,128]{2,1,0:T(8,128)(2,1)S(1)} all-to-all(bf16[16,16,128]{2,1,0:T(8,128)(2,1)S(1)} %broadcast_in_dim.25), channel_id=1, replica_groups={{144,160,176,192,208,224,240,0,16,32,48,64,80,96,112,128},{145,161,177,..., dimensions={0} | all-to-all | bytes 131072 | tf_op jit(solution)/shard_map/all_to_all | solution.py:498
  79.2 0.0 copy-start.10
  79.2 2.0 %collective-permute-start = (bf16[16,16,128]{2,1,0:T(8,128)(2,1)S(1)}, bf16[16,16,128]{2,1,0:T(8,128)(2,1)S(1)}, u32[]{:S(2)}, u32[]{:S(2)}) collective-permute-start(bf16[16,16,128]{2,1,0:T(8,128)(2,1)S(1)} %all_to_all.23.own), channel_id=1, source_target_pairs={{0,256},{256,0},{1,257},{257,1},{2,258},{258,2},{3,259},{259,3},{4... | collective-permute-start | bytes 196616 | tf_op jit(solution)/shard_map/ppermute | solution.py:504
  81.2 0.0 copy-done.1
  81.2 0.0 copy-done.2
  81.2 0.0 copy-done.3
  81.2 0.0 copy-done
  81.3 0.0 copy-done.10
  81.3 1.5 %final.1 = (bf16[512,256]{1,0:T(8,128)(2,1)}, bf16[512,256]{1,0:T(8,128)(2,1)}, bf16[512,256]{1,0:T(8,128)(2,1)}, bf16[512,256]{1,0:T(8,128)(2,1)}) custom-call(bf16[32,96,128]{2,1,0:T(8,128)(2,1)S(1)} %all_to_all.21.back, bf16[512,256]{1,0:T(8,128)(2,1)S(1)} %bitcast.11, bf16[512,256]{1,0:T(8,128)(2,1)S(1)} %bitcast.13, bf16[512,256]{1,0:T(8,128)(2,1)S(1)} %bitcast.15, ...), custom_call_target="tpu_custom_call" | custom-call | tf_op jit(solution)/shard_map/final/pallas_call | solution.py:457
  82.7 4.2 %collective-permute-done.other = bf16[16,16,128]{2,1,0:T(8,128)(2,1)S(1)} collective-permute-done((bf16[16,16,128]{2,1,0:T(8,128)(2,1)S(1)}, bf16[16,16,128]{2,1,0:T(8,128)(2,1)S(1)}, u32[]{:S(2)}, u32[]{:S(2)}) %collective-permute-start) | collective-permute-done | bytes 65568 | tf_op jit(solution)/shard_map/ppermute | solution.py:504
  86.9 0.7 assemble.1
  (2 shorter events, 0.0 us)
Async XLA Ops:
  2.4 20.7 %copy-start.4 = (bf16[512,256]{1,0:T(8,128)(2,1)S(1)}, bf16[512,256]{1,0:T(8,128)(2,1)}, u32[]{:S(2)}) copy-start(bf16[512,256]{1,0:T(8,128)(2,1)} %constant.9.clone.basis) | copy-start | bytes 786436
  2.4 20.7 %copy-start.7 = (f32[2,33,256]{2,1,0:T(8,128)S(1)}, f32[2,33,256]{2,1,0:T(8,128)}, u32[]{:S(2)}) copy-start(f32[2,33,256]{2,1,0:T(8,128)} %constant.10.clone.forward) | copy-start | bytes 202756
  2.4 20.7 %copy-start.8 = (f32[2,33,256]{2,1,0:T(8,128)S(1)}, f32[2,33,256]{2,1,0:T(8,128)}, u32[]{:S(2)}) copy-start(f32[2,33,256]{2,1,0:T(8,128)} %constant.11.clone.inverse) | copy-start | bytes 202756
  2.4 20.7 %copy-start.9 = (f32[256]{0:T(256)S(1)}, f32[256]{0:T(256)}, u32[]{:S(2)}) copy-start(f32[256]{0:T(256)} %param.16) | copy-start | bytes 3076
  26.9 17.7 %copy-start.5 = (bf16[64,512]{1,0:T(8,128)(2,1)S(1)}, bf16[64,512]{1,0:T(8,128)(2,1)}, u32[]{:S(2)}) copy-start(bf16[64,512]{1,0:T(8,128)(2,1)} %features.3) | copy-start | bytes 196612
  26.9 17.7 %copy-start.6 = (bf16[64,256]{1,0:T(8,128)(2,1)S(1)}, bf16[64,256]{1,0:T(8,128)(2,1)}, u32[]{:S(2)}) copy-start(bf16[64,256]{1,0:T(8,128)(2,1)} %weight.3) | copy-start | bytes 98308
  44.5 36.7 %copy-start.1 = (bf16[1,512,256]{2,1,0:T(8,128)(2,1)S(1)}, bf16[1,512,256]{2,1,0:T(8,128)(2,1)}, u32[]{:S(2)}) copy-start(bf16[1,512,256]{2,1,0:T(8,128)(2,1)} %param.12) | copy-start | bytes 786436
  44.5 36.7 %copy-start.2 = (bf16[1,512,256]{2,1,0:T(8,128)(2,1)S(1)}, bf16[1,512,256]{2,1,0:T(8,128)(2,1)}, u32[]{:S(2)}) copy-start(bf16[1,512,256]{2,1,0:T(8,128)(2,1)} %param.13) | copy-start | bytes 786436
  44.6 36.7 %copy-start.3 = (bf16[1,512,256]{2,1,0:T(8,128)(2,1)S(1)}, bf16[1,512,256]{2,1,0:T(8,128)(2,1)}, u32[]{:S(2)}) copy-start(bf16[1,512,256]{2,1,0:T(8,128)(2,1)} %param.18) | copy-start | bytes 786436
  44.8 36.4 %copy-start = (bf16[1,512,256]{2,1,0:T(8,128)(2,1)S(1)}, bf16[1,512,256]{2,1,0:T(8,128)(2,1)}, u32[]{:S(2)}) copy-start(bf16[1,512,256]{2,1,0:T(8,128)(2,1)} %param.11) | copy-start | bytes 786436
  79.2 2.1 %copy-start.10 = (f32[256]{0:T(256)S(1)}, f32[256]{0:T(256)}, u32[]{:S(2)}) copy-start(f32[256]{0:T(256)} %param.17) | copy-start | bytes 3076
  79.2 7.8 %collective-permute-start = (bf16[16,16,128]{2,1,0:T(8,128)(2,1)S(1)}, bf16[16,16,128]{2,1,0:T(8,128)(2,1)S(1)}, u32[]{:S(2)}, u32[]{:S(2)}) collective-permute-start(bf16[16,16,128]{2,1,0:T(8,128)(2,1)S(1)} %all_to_all.23.own), channel_id=1, source_target_pairs={{0,256},{256,0},{1,257},{257,1},{2,258},{258,2},{3,259},{259,3},{4... | collective-permute-start | bytes 196616 | tf_op jit(solution)/shard_map/ppermute | solution.py:504

commit v9 on v8

--- a/solution.py
+++ b/solution.py
@@ -25,7 +25,9 @@
 CHUNKS = TOK // LANE
 PAIRS = (HALF + 1) // 2
 ROWS = 2 * HALF + PAIRS
-FIRST_CHAN = 9
+QUAD = 4
+CHAN_QUADS = ((2, 1, 0, 3), (6, 5, 4, 7), (9, 8, 10, 11), (13, 12, 14, 15))
+QUAD_ORDER = (2, 3, 1, 0)
 LEADER = 25
 VMEM_LIMIT = 24 * 1024 * 1024
 
@@ -379,20 +381,19 @@
             preferred_element_type=f32,
         )
         weight_sum = add(weight_sum, share)
-    blank = jnp.zeros((8, LANE), f32)
-    for piece in range(16):
-        r, c = piece // 4, piece % 4
-        feature = alongs[c // 2][16 * r : 16 * (r + 1), LANE * (c % 2) : LANE * (c % 2 + 1)]
-        r, c = piece // 2, piece % 2
-        other = weight_sum[8 * r : 8 * (r + 1), LANE * c : LANE * (c + 1)]
-        other = jnp.concatenate([other, blank], axis=0)
+    blank = jnp.zeros((ORDER - 2 * TILE, LANE), f32)
+    for piece in range(QUAD):
+        c = piece % 2
+        feature = alongs[piece // 2][:, LANE * c : LANE * (c + 1)]
+        rows = weight_sum[TILE * piece : TILE * (piece + 1)]
+        other = jnp.concatenate([rows[:, :LANE], rows[:, LANE:], blank], axis=0)
         sums[piece] = jnp.where(is_feature, feature, other).astype(bf16)
 
 
 def parts(back, features, weight, **kw):
     return pl.pallas_call(
         parts_kernel,
-        out_shape=pltpu.VMEM((16, TILE, LANE), jnp.bfloat16),
+        out_shape=pltpu.VMEM((QUAD, ORDER, LANE), jnp.bfloat16),
         in_specs=[pl.BlockSpec(memory_space=pltpu.VMEM)] * 3,
         out_specs=pl.BlockSpec(memory_space=pltpu.VMEM),
         compiler_params=pltpu.CompilerParams(vmem_limit_bytes=VMEM_LIMIT),
@@ -404,15 +405,13 @@
 def assemble_kernel(own, other, feature_grad, weight_grad):
     f32 = jnp.float32
     is_feature = lax.axis_index("dp") == 0
-    for piece in range(16):
+    for piece in range(QUAD):
         a = own[piece].astype(f32)
         b = other[piece].astype(f32)
-        feature = jnp.where(is_feature, a, b)
-        weight = jnp.where(is_feature, b, a)[:8]
-        r, c = piece // 4, piece % 4
-        feature_grad[16 * r : 16 * (r + 1), 128 * c : 128 * (c + 1)] = feature
-        r, c = piece // 2, piece % 2
-        weight_grad[8 * r : 8 * (r + 1), 128 * c : 128 * (c + 1)] = weight
+        feature_grad[:, LANE * piece : LANE * (piece + 1)] = jnp.where(is_feature, a, b)
+        rows = jnp.where(is_feature, b, a)
+        weight = jnp.concatenate([rows[:TILE], rows[TILE : 2 * TILE]], axis=1)
+        weight_grad[TILE * piece : TILE * (piece + 1)] = weight
 
 
 def assemble(own, other, **kw):
@@ -465,6 +464,26 @@
     )(*(in_vmem(a) for a in (back, values, gate_first, gate_second, grad, skip)))
 
 
+def reduction_groups():
+    near, far = [], []
+    for other in range(16):
+        for quad in CHAN_QUADS:
+            near.append([z * 16 + other for z in quad])
+        for seat_in in range(QUAD):
+            far.append([CHAN_QUADS[quad][seat_in] * 16 + other for quad in QUAD_ORDER])
+    for other in range(16):
+        for i in range(QUAD):
+            near.append([256 + other * 16 + QUAD * i + k for k in range(QUAD)])
+            far.append([256 + other * 16 + QUAD * k + i for k in range(QUAD)])
+    return near, far
+
+
+def exchange(pieces, groups):
+    return lax.all_to_all(
+        pieces, ("dp", "chan", "ctx"), 0, 0, axis_index_groups=groups, tiled=True
+    )
+
+
 def local(
     values,
     gate_first,
@@ -489,17 +508,13 @@
     sent = spread(values, gate_first, gate_second, output_grad, filter_features, filter_weight, decay)
     got = trade(sent)
     back = trade(spectral(got, decay))
-    everywhere = ("dp", "chan", "ctx")
-    around = [(z + FIRST_CHAN) % 16 for z in range(16)]
-    groups = [[16 * z + j for z in around] for j in range(16)]
-    groups += [[256 + 16 * z + j for j in range(16)] for z in range(16)]
-
-    def exchange(pieces):
-        return lax.all_to_all(pieces, everywhere, 0, 0, axis_index_groups=groups, tiled=True)
-
-    pieces = exchange(parts(back, filter_features, filter_weight))
+    near, far = reduction_groups()
+    quads = (QUAD, ORDER, LANE)
+    pieces = exchange(parts(back, filter_features, filter_weight), near)
     summed = jnp.sum(pieces.astype(jnp.float32), axis=0).astype(jnp.bfloat16)
-    copies = exchange(jnp.broadcast_to(summed[None], (16, 16, 128)))
+    pieces = exchange(jnp.broadcast_to(summed[None], quads), far)
+    summed = jnp.sum(pieces.astype(jnp.float32), axis=0).astype(jnp.bfloat16)
+    copies = exchange(jnp.broadcast_to(summed[None], quads), near)
     back, copies = lax.optimization_barrier((back, copies))
     other = lax.ppermute(copies, "dp", [(0, 1), (1, 0)])
     outs = final(back, values, gate_first, gate_second, output_grad, skip_bias[None, :])

time: 88.3 us -> 85.8 us (0.972)
  blocking collectives: 72.6 us -> 70.4 us
    all_to_all x2 -> x3, blocking collectives: 34.3 us -> 32.1 us  [exchange(): lax.all_to_all(pieces, ('dp', 'chan', 'ctx'), 0, 0, axis_index_groups=gro...]
where the time goes in v9:
time: 85.8 us; the launch traced here: 85.4 us
  blocking collectives  70.4 us (82%)
  Pallas kernels  7.88 us (9%)
  waiting for transfers between devices  4.23 us (5%)
  starting transfers between devices  2.04 us (2%)
    all_to_all x2, blocking collectives, trade(): lax.all_to_all(array, ('dp', 'chan', 'ctx'), 0, 0, axis_index_groups=plan...  38.3 us
    all_to_all x3, blocking collectives, exchange(): lax.all_to_all(pieces, ('dp', 'chan', 'ctx'), 0, 0, axis_index_groups=gro...  32.1 us
    ppermute x1, waiting for transfers between devices, local(): other = lax.ppermute(copies, 'dp', [(0, 1), (1, 0)])  4.23 us
    pallas_call x1, Pallas kernels, spectral(): pl.pallas_call(spectral_kernel, out_shape=pltpu.VMEM((GROUP, (CHUNKS + 2)...  3.73 us
    ppermute x1, starting transfers between devices, local(): other = lax.ppermute(copies, 'dp', [(0, 1), (1, 0)])  2.04 us
    pallas_call x1, Pallas kernels, spread(): pl.pallas_call(spread_kernel, out_shape=pltpu.VMEM((GROUP, (CHUNKS + 1) *...  1.75 us
  transfers between devices with their start and end apart: 1, of which 1 were waited for; matrix products, arithmetic and copies ran while one was open for 0% of the time, Pallas kernels for 2%

profile of v9, /device:TPU:6, one launch (start us, length us, event | category | flops | bytes accessed | tf_op | source)
XLA Modules:
  0.0 85.4 jit_solution(11698996845786275331)
XLA Ops:
  0.6 1.8 %spread.1 = bf16[32,80,128]{2,1,0:T(8,128)(2,1)S(1)} custom-call(bf16[512,256]{1,0:T(8,128)(2,1)} %bitcast.10, bf16[512,256]{1,0:T(8,128)(2,1)} %bitcast.12, bf16[512,256]{1,0:T(8,128)(2,1)} %bitcast.14, bf16[512,256]{1,0:T(8,128)(2,1)} %bitcast.16, bf16[64,512]{1,0:T(8,128)(2,1)} %features.3, bf16[64,256]{1,0:T(8,128)(2,1)} %weight.3, f32[1,256]{1,0:T(1,128)} %bitcast.18), custom_call_target="tpu_custom_call" | custom-call | tf_op jit(solution)/shard_map/spread/pallas_call | solution.py:177
  2.4 0.0 copy-start.4
  2.4 0.0 copy-start.7
  2.4 0.0 copy-start.8
  2.4 0.0 copy-start.9
  2.4 20.7 %all_to_all.25.got = bf16[32,80,128]{2,1,0:T(8,128)(2,1)S(1)} all-to-all(bf16[32,80,128]{2,1,0:T(8,128)(2,1)S(1)} %spread.1), channel_id=1, replica_groups={{265,1,2,3,4,5,6,7,8,9,10,11,12,13,14,15,256,257,258,259,260,261,262,26..., dimensions={0} | all-to-all | bytes 1310720 | tf_op jit(solution)/shard_map/all_to_all | solution.py:503
  23.1 0.0 copy-done.4
  23.1 0.0 copy-done.7
  23.1 0.0 copy-done.8
  23.1 0.0 copy-done.9
  23.1 3.7 %spectral.1 = bf16[32,96,128]{2,1,0:T(8,128)(2,1)S(1)} custom-call(bf16[32,80,128]{2,1,0:T(8,128)(2,1)S(1)} %all_to_all.25.got, bf16[512,256]{1,0:T(8,128)(2,1)S(1)} %copy-done.4, f32[2,33,256]{2,1,0:T(8,128)S(1)} %copy-done.7, f32[2,33,256]{2,1,0:T(8,128)S(1)} %copy-done.8, f32[1,256]{1,0:T(1,128)S(1)} %bitcast.19), custom_call_target="tpu_custom_call" | custom-call | tf_op jit(solution)/shard_map/spectral/pallas_call | solution.py:352
  26.9 0.0 copy-start.5
  26.9 0.0 copy-start.6
  26.9 17.6 %all_to_all.26.back = bf16[32,96,128]{2,1,0:T(8,128)(2,1)S(1)} all-to-all(bf16[32,96,128]{2,1,0:T(8,128)(2,1)S(1)} %spectral.1), channel_id=1, replica_groups={{265,1,2,3,4,5,6,7,8,9,10,11,12,13,14,15,256,257,258,259,260,261,262,26..., dimensions={0} | all-to-all | bytes 1572864 | tf_op jit(solution)/shard_map/all_to_all | solution.py:503
  44.5 0.0 copy-done.5
  44.5 0.0 copy-done.6
  44.5 0.0 copy-start.2
  44.5 0.0 copy-start.3
  44.6 0.2 parts.1
  44.8 7.6 %all_to_all.27 = bf16[4,64,128]{2,1,0:T(8,128)(2,1)S(1)} all-to-all(bf16[4,64,128]{2,1,0:T(8,128)(2,1)S(1)} %parts.1), channel_id=1, replica_groups={{32,16,0,48},{96,80,64,112},{144,128,160,176},{208,192,224,240},{33,17,..., dimensions={0} | all-to-all | bytes 131072 | tf_op jit(solution)/shard_map/all_to_all | solution.py:482
  52.4 0.0 copy-start.1
  52.4 0.0 copy-start
  52.4 16.9 %all_to_all.28 = bf16[4,64,128]{2,1,0:T(8,128)(2,1)S(1)} all-to-all(bf16[4,64,128]{2,1,0:T(8,128)(2,1)S(1)} %broadcast_in_dim.31), channel_id=1, replica_groups={{144,208,96,32},{128,192,80,16},{160,224,64,0},{176,240,112,48},{145,20..., dimensions={0} | all-to-all | bytes 131072 | tf_op jit(solution)/shard_map/all_to_all | solution.py:482
  69.4 7.6 %all_to_all.29.own = bf16[4,64,128]{2,1,0:T(8,128)(2,1)S(1)} all-to-all(bf16[4,64,128]{2,1,0:T(8,128)(2,1)S(1)} %broadcast_in_dim.32), channel_id=1, replica_groups={{32,16,0,48},{96,80,64,112},{144,128,160,176},{208,192,224,240},{33,17,..., dimensions={0} | all-to-all | bytes 131072 | tf_op jit(solution)/shard_map/all_to_all | solution.py:482
  76.9 0.0 copy-start.10
  77.0 2.0 %collective-permute-start = (bf16[4,64,128]{2,1,0:T(8,128)(2,1)S(1)}, bf16[4,64,128]{2,1,0:T(8,128)(2,1)S(1)}, u32[]{:S(2)}, u32[]{:S(2)}) collective-permute-start(bf16[4,64,128]{2,1,0:T(8,128)(2,1)S(1)} %all_to_all.29.own), channel_id=1, source_target_pairs={{0,256},{256,0},{1,257},{257,1},{2,258},{258,2},{3,259},{259,3},{4... | collective-permute-start | bytes 196616 | tf_op jit(solution)/shard_map/ppermute | solution.py:519
  79.0 0.0 copy-done.2
  79.0 0.0 copy-done.3
  79.0 0.0 copy-done.1
  79.0 0.0 copy-done
  79.0 0.0 copy-done.10
  79.0 1.5 %final.1 = (bf16[512,256]{1,0:T(8,128)(2,1)}, bf16[512,256]{1,0:T(8,128)(2,1)}, bf16[512,256]{1,0:T(8,128)(2,1)}, bf16[512,256]{1,0:T(8,128)(2,1)}) custom-call(bf16[32,96,128]{2,1,0:T(8,128)(2,1)S(1)} %all_to_all.26.back, bf16[512,256]{1,0:T(8,128)(2,1)S(1)} %bitcast.11, bf16[512,256]{1,0:T(8,128)(2,1)S(1)} %bitcast.13, bf16[512,256]{1,0:T(8,128)(2,1)S(1)} %bitcast.15, ...), custom_call_target="tpu_custom_call" | custom-call | tf_op jit(solution)/shard_map/final/pallas_call | solution.py:456
  80.5 4.2 %collective-permute-done.other = bf16[4,64,128]{2,1,0:T(8,128)(2,1)S(1)} collective-permute-done((bf16[4,64,128]{2,1,0:T(8,128)(2,1)S(1)}, bf16[4,64,128]{2,1,0:T(8,128)(2,1)S(1)}, u32[]{:S(2)}, u32[]{:S(2)}) %collective-permute-start) | collective-permute-done | bytes 65568 | tf_op jit(solution)/shard_map/ppermute | solution.py:519
  84.7 0.7 assemble.1
  (4 shorter events, 0.0 us)
Async XLA Ops:
  2.4 20.7 %copy-start.4 = (bf16[512,256]{1,0:T(8,128)(2,1)S(1)}, bf16[512,256]{1,0:T(8,128)(2,1)}, u32[]{:S(2)}) copy-start(bf16[512,256]{1,0:T(8,128)(2,1)} %constant.10.clone.basis) | copy-start | bytes 786436
  2.4 20.7 %copy-start.7 = (f32[2,33,256]{2,1,0:T(8,128)S(1)}, f32[2,33,256]{2,1,0:T(8,128)}, u32[]{:S(2)}) copy-start(f32[2,33,256]{2,1,0:T(8,128)} %constant.11.clone.forward) | copy-start | bytes 202756
  2.4 20.7 %copy-start.8 = (f32[2,33,256]{2,1,0:T(8,128)S(1)}, f32[2,33,256]{2,1,0:T(8,128)}, u32[]{:S(2)}) copy-start(f32[2,33,256]{2,1,0:T(8,128)} %constant.12.clone.inverse) | copy-start | bytes 202756
  2.4 20.7 %copy-start.9 = (f32[256]{0:T(256)S(1)}, f32[256]{0:T(256)}, u32[]{:S(2)}) copy-start(f32[256]{0:T(256)} %param.16) | copy-start | bytes 3076
  26.9 17.7 %copy-start.5 = (bf16[64,512]{1,0:T(8,128)(2,1)S(1)}, bf16[64,512]{1,0:T(8,128)(2,1)}, u32[]{:S(2)}) copy-start(bf16[64,512]{1,0:T(8,128)(2,1)} %features.3) | copy-start | bytes 196612
  26.9 17.7 %copy-start.6 = (bf16[64,256]{1,0:T(8,128)(2,1)S(1)}, bf16[64,256]{1,0:T(8,128)(2,1)}, u32[]{:S(2)}) copy-start(bf16[64,256]{1,0:T(8,128)(2,1)} %weight.3) | copy-start | bytes 98308
  44.5 34.5 %copy-start.2 = (bf16[1,512,256]{2,1,0:T(8,128)(2,1)S(1)}, bf16[1,512,256]{2,1,0:T(8,128)(2,1)}, u32[]{:S(2)}) copy-start(bf16[1,512,256]{2,1,0:T(8,128)(2,1)} %param.13) | copy-start | bytes 786436
  44.5 34.5 %copy-start.3 = (bf16[1,512,256]{2,1,0:T(8,128)(2,1)S(1)}, bf16[1,512,256]{2,1,0:T(8,128)(2,1)}, u32[]{:S(2)}) copy-start(bf16[1,512,256]{2,1,0:T(8,128)(2,1)} %param.18) | copy-start | bytes 786436
  52.4 26.7 %copy-start.1 = (bf16[1,512,256]{2,1,0:T(8,128)(2,1)S(1)}, bf16[1,512,256]{2,1,0:T(8,128)(2,1)}, u32[]{:S(2)}) copy-start(bf16[1,512,256]{2,1,0:T(8,128)(2,1)} %param.12) | copy-start | bytes 786436
  52.4 26.7 %copy-start = (bf16[1,512,256]{2,1,0:T(8,128)(2,1)S(1)}, bf16[1,512,256]{2,1,0:T(8,128)(2,1)}, u32[]{:S(2)}) copy-start(bf16[1,512,256]{2,1,0:T(8,128)(2,1)} %param.11) | copy-start | bytes 786436
  76.9 2.1 %copy-start.10 = (f32[256]{0:T(256)S(1)}, f32[256]{0:T(256)}, u32[]{:S(2)}) copy-start(f32[256]{0:T(256)} %param.17) | copy-start | bytes 3076
  77.0 7.8 %collective-permute-start = (bf16[4,64,128]{2,1,0:T(8,128)(2,1)S(1)}, bf16[4,64,128]{2,1,0:T(8,128)(2,1)S(1)}, u32[]{:S(2)}, u32[]{:S(2)}) collective-permute-start(bf16[4,64,128]{2,1,0:T(8,128)(2,1)S(1)} %all_to_all.29.own), channel_id=1, source_target_pairs={{0,256},{256,0},{1,257},{257,1},{2,258},{258,2},{3,259},{259,3},{4... | collective-permute-start | bytes 196616 | tf_op jit(solution)/shard_map/ppermute | solution.py:519

commit v10 on v9

--- a/solution.py
+++ b/solution.py
@@ -26,14 +26,14 @@
 PAIRS = (HALF + 1) // 2
 ROWS = 2 * HALF + PAIRS
 QUAD = 4
-CHAN_QUADS = ((2, 1, 0, 3), (6, 5, 4, 7), (9, 8, 10, 11), (13, 12, 14, 15))
+CHAN_QUADS = ((3, 1, 0, 2), (6, 5, 4, 7), (9, 8, 10, 11), (13, 12, 14, 15))
 QUAD_ORDER = (2, 3, 1, 0)
 LEADER = 25
 VMEM_LIMIT = 24 * 1024 * 1024
 
 
 def seat(member):
-    return {0: LEADER, LEADER: 0}.get(member, member)
+    return (member - LEADER) % GROUP
 
 
 def tables():
@@ -191,7 +191,7 @@
     f32, bf16 = jnp.float32, jnp.bfloat16
     rates[...] = jnp.broadcast_to(decay[...], (LANE, CH)).T
     member = lax.axis_index("dp") * BLOCKS + lax.axis_index("ctx")
-    place_of = jnp.where(member == 0, LEADER, jnp.where(member == LEADER, 0, member))
+    place_of = (member + (GROUP - LEADER)) % GROUP
     first = place_of * OWN
 
     def transformed(xs, lanes):
@@ -497,7 +497,8 @@
     values, gate_first, gate_second, output_grad = (
         a[0] for a in (values, gate_first, gate_second, output_grad)
     )
-    planes = [[256 * (seat(i) // 16) + 16 * z + seat(i) % 16 for i in range(GROUP)] for z in range(16)]
+    members = [(LEADER + i) % GROUP for i in range(GROUP)]
+    planes = [[256 * (i // 16) + 16 * z + i % 16 for i in members] for z in range(16)]
 
     def trade(array):
         return lax.all_to_all(

time: 85.8 us -> 85.8 us (level)
  no operation moved by 1% of the time
where the time goes in v10:
time: 85.8 us; the launch traced here: 85.4 us
  blocking collectives  70.3 us (82%)
  Pallas kernels  7.89 us (9%)
  waiting for transfers between devices  4.22 us (5%)
  starting transfers between devices  2.04 us (2%)
    all_to_all x2, blocking collectives, trade(): lax.all_to_all(array, ('dp', 'chan', 'ctx'), 0, 0, axis_index_groups=plan...  38.3 us
    all_to_all x3, blocking collectives, exchange(): lax.all_to_all(pieces, ('dp', 'chan', 'ctx'), 0, 0, axis_index_groups=gro...  32.1 us
    ppermute x1, waiting for transfers between devices, local(): other = lax.ppermute(copies, 'dp', [(0, 1), (1, 0)])  4.22 us
    pallas_call x1, Pallas kernels, spectral(): pl.pallas_call(spectral_kernel, out_shape=pltpu.VMEM((GROUP, (CHUNKS + 2)...  3.73 us
    ppermute x1, starting transfers between devices, local(): other = lax.ppermute(copies, 'dp', [(0, 1), (1, 0)])  2.04 us
    pallas_call x1, Pallas kernels, spread(): pl.pallas_call(spread_kernel, out_shape=pltpu.VMEM((GROUP, (CHUNKS + 1) *...  1.75 us
  transfers between devices with their start and end apart: 1, of which 1 were waited for; matrix products, arithmetic and copies ran while one was open for 0% of the time, Pallas kernels for 2%

profile of v10, /device:TPU:6, one launch (start us, length us, event | category | flops | bytes accessed | tf_op | source)
XLA Modules:
  0.0 85.4 jit_solution(14012305676768767970)
XLA Ops:
  0.6 1.8 %spread.1 = bf16[32,80,128]{2,1,0:T(8,128)(2,1)S(1)} custom-call(bf16[512,256]{1,0:T(8,128)(2,1)} %bitcast.10, bf16[512,256]{1,0:T(8,128)(2,1)} %bitcast.12, bf16[512,256]{1,0:T(8,128)(2,1)} %bitcast.14, bf16[512,256]{1,0:T(8,128)(2,1)} %bitcast.16, bf16[64,512]{1,0:T(8,128)(2,1)} %features.3, bf16[64,256]{1,0:T(8,128)(2,1)} %weight.3, f32[1,256]{1,0:T(1,128)} %bitcast.18), custom_call_target="tpu_custom_call" | custom-call | tf_op jit(solution)/shard_map/spread/pallas_call | solution.py:177
  2.4 0.0 copy-start.4
  2.4 0.0 copy-start.7
  2.4 0.0 copy-start.8
  2.4 0.0 copy-start.9
  2.4 20.7 %all_to_all.25.got = bf16[32,80,128]{2,1,0:T(8,128)(2,1)S(1)} all-to-all(bf16[32,80,128]{2,1,0:T(8,128)(2,1)S(1)} %spread.1), channel_id=1, replica_groups={{265,266,267,268,269,270,271,0,1,2,3,4,5,6,7,8,9,10,11,12,13,14,15,256,..., dimensions={0} | all-to-all | bytes 1310720 | tf_op jit(solution)/shard_map/all_to_all | solution.py:504
  23.1 0.0 copy-done.4
  23.2 0.0 copy-done.7
  23.2 0.0 copy-done.8
  23.2 0.0 copy-done.9
  23.2 3.7 %spectral.1 = bf16[32,96,128]{2,1,0:T(8,128)(2,1)S(1)} custom-call(bf16[32,80,128]{2,1,0:T(8,128)(2,1)S(1)} %all_to_all.25.got, bf16[512,256]{1,0:T(8,128)(2,1)S(1)} %copy-done.4, f32[2,33,256]{2,1,0:T(8,128)S(1)} %copy-done.7, f32[2,33,256]{2,1,0:T(8,128)S(1)} %copy-done.8, f32[1,256]{1,0:T(1,128)S(1)} %bitcast.19), custom_call_target="tpu_custom_call" | custom-call | tf_op jit(solution)/shard_map/spectral/pallas_call | solution.py:352
  26.9 0.0 copy-start.5
  26.9 0.0 copy-start.6
  26.9 17.5 %all_to_all.26.back = bf16[32,96,128]{2,1,0:T(8,128)(2,1)S(1)} all-to-all(bf16[32,96,128]{2,1,0:T(8,128)(2,1)S(1)} %spectral.1), channel_id=1, replica_groups={{265,266,267,268,269,270,271,0,1,2,3,4,5,6,7,8,9,10,11,12,13,14,15,256,..., dimensions={0} | all-to-all | bytes 1572864 | tf_op jit(solution)/shard_map/all_to_all | solution.py:504
  44.5 0.0 copy-done.5
  44.5 0.0 copy-done.6
  44.5 0.0 copy-start.2
  44.5 0.0 copy-start.3
  44.5 0.2 parts.1
  44.7 7.6 %all_to_all.27 = bf16[4,64,128]{2,1,0:T(8,128)(2,1)S(1)} all-to-all(bf16[4,64,128]{2,1,0:T(8,128)(2,1)S(1)} %parts.1), channel_id=1, replica_groups={{48,16,0,32},{96,80,64,112},{144,128,160,176},{208,192,224,240},{49,17,..., dimensions={0} | all-to-all | bytes 131072 | tf_op jit(solution)/shard_map/all_to_all | solution.py:482
  52.3 0.0 copy-start.1
  52.3 0.0 copy-start
  52.3 17.0 %all_to_all.28 = bf16[4,64,128]{2,1,0:T(8,128)(2,1)S(1)} all-to-all(bf16[4,64,128]{2,1,0:T(8,128)(2,1)S(1)} %broadcast_in_dim.31), channel_id=1, replica_groups={{144,208,96,48},{128,192,80,16},{160,224,64,0},{176,240,112,32},{145,20..., dimensions={0} | all-to-all | bytes 131072 | tf_op jit(solution)/shard_map/all_to_all | solution.py:482
  69.3 7.6 %all_to_all.29.own = bf16[4,64,128]{2,1,0:T(8,128)(2,1)S(1)} all-to-all(bf16[4,64,128]{2,1,0:T(8,128)(2,1)S(1)} %broadcast_in_dim.32), channel_id=1, replica_groups={{48,16,0,32},{96,80,64,112},{144,128,160,176},{208,192,224,240},{49,17,..., dimensions={0} | all-to-all | bytes 131072 | tf_op jit(solution)/shard_map/all_to_all | solution.py:482
  76.9 0.0 copy-start.10
  76.9 2.0 %collective-permute-start = (bf16[4,64,128]{2,1,0:T(8,128)(2,1)S(1)}, bf16[4,64,128]{2,1,0:T(8,128)(2,1)S(1)}, u32[]{:S(2)}, u32[]{:S(2)}) collective-permute-start(bf16[4,64,128]{2,1,0:T(8,128)(2,1)S(1)} %all_to_all.29.own), channel_id=1, source_target_pairs={{0,256},{256,0},{1,257},{257,1},{2,258},{258,2},{3,259},{259,3},{4... | collective-permute-start | bytes 196616 | tf_op jit(solution)/shard_map/ppermute | solution.py:520
  78.9 0.0 copy-done.2
  79.0 0.0 copy-done.3
  79.0 0.0 copy-done.1
  79.0 0.0 copy-done
  79.0 0.0 copy-done.10
  79.0 1.5 %final.1 = (bf16[512,256]{1,0:T(8,128)(2,1)}, bf16[512,256]{1,0:T(8,128)(2,1)}, bf16[512,256]{1,0:T(8,128)(2,1)}, bf16[512,256]{1,0:T(8,128)(2,1)}) custom-call(bf16[32,96,128]{2,1,0:T(8,128)(2,1)S(1)} %all_to_all.26.back, bf16[512,256]{1,0:T(8,128)(2,1)S(1)} %bitcast.11, bf16[512,256]{1,0:T(8,128)(2,1)S(1)} %bitcast.13, bf16[512,256]{1,0:T(8,128)(2,1)S(1)} %bitcast.15, ...), custom_call_target="tpu_custom_call" | custom-call | tf_op jit(solution)/shard_map/final/pallas_call | solution.py:456
  80.5 4.2 %collective-permute-done.other = bf16[4,64,128]{2,1,0:T(8,128)(2,1)S(1)} collective-permute-done((bf16[4,64,128]{2,1,0:T(8,128)(2,1)S(1)}, bf16[4,64,128]{2,1,0:T(8,128)(2,1)S(1)}, u32[]{:S(2)}, u32[]{:S(2)}) %collective-permute-start) | collective-permute-done | bytes 65568 | tf_op jit(solution)/shard_map/ppermute | solution.py:520
  84.7 0.7 assemble.1
  (4 shorter events, 0.0 us)
Async XLA Ops:
  2.4 20.8 %copy-start.4 = (bf16[512,256]{1,0:T(8,128)(2,1)S(1)}, bf16[512,256]{1,0:T(8,128)(2,1)}, u32[]{:S(2)}) copy-start(bf16[512,256]{1,0:T(8,128)(2,1)} %constant.10.clone.basis) | copy-start | bytes 786436
  2.4 20.8 %copy-start.7 = (f32[2,33,256]{2,1,0:T(8,128)S(1)}, f32[2,33,256]{2,1,0:T(8,128)}, u32[]{:S(2)}) copy-start(f32[2,33,256]{2,1,0:T(8,128)} %constant.11.clone.forward) | copy-start | bytes 202756
  2.4 20.7 %copy-start.8 = (f32[2,33,256]{2,1,0:T(8,128)S(1)}, f32[2,33,256]{2,1,0:T(8,128)}, u32[]{:S(2)}) copy-start(f32[2,33,256]{2,1,0:T(8,128)} %constant.12.clone.inverse) | copy-start | bytes 202756
  2.4 20.7 %copy-start.9 = (f32[256]{0:T(256)S(1)}, f32[256]{0:T(256)}, u32[]{:S(2)}) copy-start(f32[256]{0:T(256)} %param.16) | copy-start | bytes 3076
  26.9 17.6 %copy-start.5 = (bf16[64,512]{1,0:T(8,128)(2,1)S(1)}, bf16[64,512]{1,0:T(8,128)(2,1)}, u32[]{:S(2)}) copy-start(bf16[64,512]{1,0:T(8,128)(2,1)} %features.3) | copy-start | bytes 196612
  26.9 17.6 %copy-start.6 = (bf16[64,256]{1,0:T(8,128)(2,1)S(1)}, bf16[64,256]{1,0:T(8,128)(2,1)}, u32[]{:S(2)}) copy-start(bf16[64,256]{1,0:T(8,128)(2,1)} %weight.3) | copy-start | bytes 98308
  44.5 34.5 %copy-start.2 = (bf16[1,512,256]{2,1,0:T(8,128)(2,1)S(1)}, bf16[1,512,256]{2,1,0:T(8,128)(2,1)}, u32[]{:S(2)}) copy-start(bf16[1,512,256]{2,1,0:T(8,128)(2,1)} %param.13) | copy-start | bytes 786436
  44.5 34.5 %copy-start.3 = (bf16[1,512,256]{2,1,0:T(8,128)(2,1)S(1)}, bf16[1,512,256]{2,1,0:T(8,128)(2,1)}, u32[]{:S(2)}) copy-start(bf16[1,512,256]{2,1,0:T(8,128)(2,1)} %param.18) | copy-start | bytes 786436
  52.3 26.7 %copy-start.1 = (bf16[1,512,256]{2,1,0:T(8,128)(2,1)S(1)}, bf16[1,512,256]{2,1,0:T(8,128)(2,1)}, u32[]{:S(2)}) copy-start(bf16[1,512,256]{2,1,0:T(8,128)(2,1)} %param.12) | copy-start | bytes 786436
  52.3 26.7 %copy-start = (bf16[1,512,256]{2,1,0:T(8,128)(2,1)S(1)}, bf16[1,512,256]{2,1,0:T(8,128)(2,1)}, u32[]{:S(2)}) copy-start(bf16[1,512,256]{2,1,0:T(8,128)(2,1)} %param.11) | copy-start | bytes 786436
  76.9 2.1 %copy-start.10 = (f32[256]{0:T(256)S(1)}, f32[256]{0:T(256)}, u32[]{:S(2)}) copy-start(f32[256]{0:T(256)} %param.17) | copy-start | bytes 3076
  76.9 7.8 %collective-permute-start = (bf16[4,64,128]{2,1,0:T(8,128)(2,1)S(1)}, bf16[4,64,128]{2,1,0:T(8,128)(2,1)S(1)}, u32[]{:S(2)}, u32[]{:S(2)}) collective-permute-start(bf16[4,64,128]{2,1,0:T(8,128)(2,1)S(1)} %all_to_all.29.own), channel_id=1, source_target_pairs={{0,256},{256,0},{1,257},{257,1},{2,258},{258,2},{3,259},{259,3},{4... | collective-permute-start | bytes 196616 | tf_op jit(solution)/shard_map/ppermute | solution.py:520
